TPU v7x, 32 devices: a whole 2x2x4 slice. The times are simulated.
32 devices in a mesh: phase: 16 (over z, x, core), slab: 2 (over y).
Axes of the slice: x: 2, y: 2, z: 4, core: 2. Of those that a mesh axis runs over, the one named last changes fastest.
Arguments:
- features: bfloat16 [16, 4, 320, 512], P('phase', 'slab'), may hold values from -6 to 6
- conv_weight: bfloat16 [27, 64, 64], replicated, may hold values from -0.15625 to 0.15625
- projection: bfloat16 [2, 64], replicated, may hold values from -0.75 to 0.75
- grad_out: float32 [16, 4, 2, 8, 320], P('phase', 'slab'), may hold values from -6 to 6
- sens: float32 [4, 16, 2, 8, 320], P('slab'), may hold values from -1 to 1
- mask: int32 [16, 4, 320], P('phase'), may hold values 0 or 1
Outputs:
- grad_image: float32 [16, 4, 2, 8, 320], P('phase', 'slab')
- grad_features: bfloat16 [16, 4, 320, 512], P('phase', 'slab')
- grad_weight: float32 [27, 64, 64], replicated
All inputs are finite; a program needn't handle non-finite values. No bound on the sum of `mask` on one device may be relied on, other than what follows from the above.
Results may differ from a plain program's by a relative error of at most 0.0051.
Values may be sent and summed in bfloat16 or wider, within the bound.
No kernel may reach another device: no remote copies, remote signals or barrier semaphores. Data moves between devices by JAX's collectives and lax.ppermute only.
A program may use at most 128 MiB of HBM per device.

v0:
```python
import functools
import math

import jax
import jax.numpy as jnp
import ml_dtypes
import numpy as np
from jax import lax
from jax.experimental import pallas as pl
from jax.experimental.pallas import tpu as pltpu
from jax.sharding import PartitionSpec as P

F32, BF16 = jnp.float32, jnp.bfloat16
VMEM = pl.BlockSpec(memory_space=pltpu.VMEM)
SMEM = pl.BlockSpec(memory_space=pltpu.SMEM)
LIMIT = 48 * 1024 * 1024
LANES = 128


def call(body, outs, n_in, n_smem=0, scratch=(), flops=0, nbytes=0):
    return pl.pallas_call(
        body,
        out_shape=outs,
        in_specs=[SMEM] * n_smem + [VMEM] * n_in,
        out_specs=jax.tree.map(lambda _: VMEM, outs),
        scratch_shapes=list(scratch),
        compiler_params=pltpu.CompilerParams(vmem_limit_bytes=LIMIT),
        cost_estimate=pl.CostEstimate(flops=flops, bytes_accessed=nbytes, transcendentals=0),
    )


def dft_packed(length):
    full = length // LANES * LANES
    part = np.concatenate([np.zeros(full), np.ones(full), np.zeros(length - full), np.ones(length - full)])
    index = np.concatenate([np.arange(full)] * 2 + [np.arange(full, length)] * 2)
    angle = (index[:, None] * index[None, :] % length) * (2.0 * math.pi / length)
    cosine, sine = np.cos(angle), np.sin(angle)
    same = part[:, None] == part[None, :]
    matrix = np.where(same, cosine, np.where(part[:, None] == 0, -sine, sine)) / math.sqrt(length)
    high = matrix.astype(ml_dtypes.bfloat16)
    low = (matrix - high.astype(np.float64)).astype(ml_dtypes.bfloat16)
    return high, low


def split(value):
    high = value.astype(BF16)
    return high, (value - high.astype(F32)).astype(BF16)


def dot3(high, low, mat_high, mat_low, dims):
    dot = functools.partial(lax.dot_general, dimension_numbers=(dims, ((), ())), preferred_element_type=F32)
    return dot(high, mat_high) + (dot(high, mat_low) + dot(low, mat_high))


def coil_forward_body(grad_ref, sens_ref, high_ref, low_ref, out_ref, send_ref, x_high, x_low):
    depth_len, coils, _, col_len, row_len = sens_ref.shape
    full = row_len // LANES * LANES
    count = coils * col_len
    for z in range(depth_len):
        sens_r, sens_i = sens_ref[z, :, 0], sens_ref[z, :, 1]
        img_r, img_i = grad_ref[z, 0][None], grad_ref[z, 1][None]
        real = sens_r * img_r - sens_i * img_i
        imag = sens_r * img_i + sens_i * img_r
        rest = jnp.concatenate([real[..., full:], imag[..., full:]], axis=-1)
        for piece, start in ((real[..., :full], 0), (imag[..., :full], full), (rest, 2 * full)):
            width = piece.shape[-1]
            high, low = split(piece.reshape(count, width))
            x_high[z * count : (z + 1) * count, start : start + width] = high
            x_low[z * count : (z + 1) * count, start : start + width] = low
    result = dot3(x_high[...], x_low[...], high_ref[...], low_ref[...], ((1,), (0,)))
    out_ref[...] = result
    send_ref[...] = result.astype(BF16)


def coil_backward_body(slabs, grad_ref, sens_ref, mask_ref, high_ref, low_ref, own_ref, *refs):
    others, out_ref, x_high, x_low = refs[: slabs - 1], refs[-3], refs[-2], refs[-1]
    depth_len, coils, _, col_len, row_len = sens_ref.shape
    total = slabs * depth_len
    full = row_len // LANES * LANES
    rem = row_len - full
    count = coils * col_len
    mask = mask_ref[...].astype(F32)

    def table(turn):
        real = jnp.zeros((1, row_len), F32)
        imag = jnp.zeros((1, row_len), F32)
        has_imag = False
        for kz in range(total):
            angle = 2.0 * math.pi * ((kz * turn) % total) / total
            cosine, sine = round(math.cos(angle), 15) / total, round(math.sin(angle), 15) / total
            real = real + mask[kz : kz + 1] * cosine
            if sine != 0.0:
                imag = imag + mask[kz : kz + 1] * sine
                has_imag = True
        real_rest = jnp.concatenate([real[:, full:], real[:, full:]], axis=-1)
        imag_rest = jnp.concatenate([-imag[:, full:], imag[:, full:]], axis=-1)
        return real[:, :full], imag[:, :full], real_rest, imag_rest, has_imag

    tables = {}
    for z in range(depth_len):
        sums = None
        for step in range(slabs):
            src = own_ref if step == 0 else others[step - 1]
            for zin in range(depth_len):
                turn = (step * depth_len + z - zin) % total
                if turn not in tables:
                    tables[turn] = table(turn)
                real, imag, real_rest, imag_rest, has_imag = tables[turn]
                block = src[zin * count : (zin + 1) * count, :].astype(F32)
                v_r, v_i, v_rest = block[:, :full], block[:, full : 2 * full], block[:, 2 * full :]
                if has_imag:
                    terms = (
                        real * v_r - imag * v_i,
                        real * v_i + imag * v_r,
                        real_rest * v_rest + imag_rest * pltpu.roll(v_rest, rem, 1),
                    )
                else:
                    terms = (real * v_r, real * v_i, real_rest * v_rest)
                sums = terms if sums is None else tuple(a + b for a, b in zip(sums, terms))
        for piece, start in zip(sums, (0, full, 2 * full)):
            high, low = split(piece)
            x_high[z * count : (z + 1) * count, start : start + piece.shape[1]] = high
            x_low[z * count : (z + 1) * count, start : start + piece.shape[1]] = low
    back = dot3(x_high[...], x_low[...], high_ref[...], low_ref[...], ((1,), (1,)))
    for z in range(depth_len):
        sens_r, sens_i = sens_ref[z, :, 0], sens_ref[z, :, 1]
        block = back[z * count : (z + 1) * count].reshape(coils, col_len, 2 * row_len)
        b_r, b_i, b_rest = block[..., :full], block[..., full : 2 * full], block[..., 2 * full :]
        s_r, s_i = sens_r[..., :full], sens_i[..., :full]
        out_ref[z, 0, :, :full] = grad_ref[z, 0, :, :full] - jnp.sum(s_r * b_r + s_i * b_i, axis=0)
        out_ref[z, 1, :, :full] = grad_ref[z, 1, :, :full] - jnp.sum(s_r * b_i - s_i * b_r, axis=0)
        s_rest = jnp.concatenate([sens_r[..., full:], sens_i[..., full:]], axis=-1)
        turned = pltpu.roll(b_rest, rem, 2)
        along = jnp.sum(s_rest * b_rest, axis=0)
        across = jnp.sum(s_rest * turned, axis=0)
        real = along + pltpu.roll(along, rem, 1)
        imag = across - pltpu.roll(across, rem, 1)
        out_ref[z, 0, :, full:] = grad_ref[z, 0, :, full:] - real[:, :rem]
        out_ref[z, 1, :, full:] = grad_ref[z, 1, :, full:] - imag[:, :rem]


def tap_group(scal_ref, phase_kind, flip, step_z):
    core = scal_ref[1]
    time_off = {"own": 1, "on": 2 - 2 * core, "off": 2 * core}[phase_kind]
    depth_off = jnp.where(scal_ref[0] == 1, 2 - step_z, step_z) if flip else step_z
    return 9 * time_off + 3 * depth_off


def shift_rows(value, step):
    rows = value.shape[0]
    turned = pltpu.roll(value, step % rows, 0)
    place = lax.broadcasted_iota(jnp.int32, value.shape, 0)
    return jnp.where(place == (0 if step > 0 else rows - 1), 0.0, turned)


def fill_band(scal_ref, weight_ref, band, entries, outs, flip):
    width = LANES * len(outs)
    for i, (kind, place) in enumerate(entries):
        for j, out_place in enumerate(outs):
            step_z = place - out_place + 1
            for dy in range(3):
                lanes = slice(dy * width + j * LANES, dy * width + (j + 1) * LANES)
                if 0 <= step_z <= 2:
                    block = weight_ref[tap_group(scal_ref, kind, flip, step_z) + dy]
                else:
                    block = jnp.zeros((LANES, LANES), BF16)
                band[i * LANES : (i + 1) * LANES, lanes] = block


def conv_columns(refs, band, lanes):
    stacked = jnp.concatenate([ref[:, lanes] for ref in refs], axis=1)
    taps = jnp.dot(stacked, band[...], preferred_element_type=F32)
    width = taps.shape[1] // 3
    return (
        shift_rows(taps[:, :width], 1)
        + taps[:, width : 2 * width]
        + shift_rows(taps[:, 2 * width :], -1)
    )


def conv_main_body(entries, outs, flip, scal_ref, weight_ref, *refs):
    inputs, out_ref, band = refs[: len(entries)], refs[-2], refs[-1]
    fill_band(scal_ref, weight_ref, band, entries, outs, flip)
    for start in range(0, out_ref.shape[2], LANES):
        lanes = slice(start, start + LANES)
        result = conv_columns(inputs, band, lanes)
        for j in range(len(outs)):
            out_ref[j, :, lanes] = result[:, j * LANES : (j + 1) * LANES]


def corner_sum(groups, scal_ref, weight_ref, refs, bands, flip):
    at = 0
    plans = {}
    for group, ((entries, out_place), band) in enumerate(zip(groups, bands)):
        fill_band(scal_ref, weight_ref, band, entries, (out_place,), flip)
        plans[out_place] = (refs[at : at + len(entries)], band)
        at += len(entries)
    return plans


def grad_act_body(groups, flip, scal_ref, weight_ref, acc_ref, image_ref, spread_ref, *refs):
    n_in = sum(len(entries) for entries, _ in groups)
    inputs, rest = refs[:n_in], refs[n_in:]
    outs = rest[: acc_ref.shape[0]]
    plans = corner_sum(groups, scal_ref, weight_ref, inputs, rest[len(outs) :], flip)
    row_len = image_ref.shape[3]
    for j, out_ref in enumerate(outs):
        place = jnp.where(scal_ref[0] == 1, len(outs) - 1 - j, j) if flip else j
        image = image_ref[place].reshape(-1, row_len)
        first, low = split(image)
        middle, last = split(image - first.astype(F32))
        stacked = jnp.concatenate([first, middle, last], axis=0)
        for start in range(0, acc_ref.shape[2], LANES):
            lanes = slice(start, start + LANES)
            grad_silu = lax.dot_general(
                stacked, spread_ref[:, lanes], (((0,), (0,)), ((), ())), preferred_element_type=F32
            )
            act = acc_ref[j, :, lanes]
            if j in plans:
                act = act + conv_columns(*plans[j], lanes)
            gate = 0.5 * jnp.tanh(0.5 * act) + 0.5
            out_ref[:, lanes] = (grad_silu * (gate * (1.0 + act * (1.0 - gate)))).astype(BF16)


def grad_feature_body(groups, flip, scal_ref, weight_ref, acc_ref, *refs):
    n_in = sum(len(entries) for entries, _ in groups)
    inputs, out_ref, bands = refs[:n_in], refs[n_in], refs[n_in + 1 :]
    plans = corner_sum(groups, scal_ref, weight_ref, inputs, bands, flip)
    depth_len = acc_ref.shape[0]
    for j in range(depth_len):
        place = jnp.where(scal_ref[0] == 1, depth_len - 1 - j, j) if flip else j
        for start in range(0, acc_ref.shape[2], LANES):
            lanes = slice(start, start + LANES)
            total = acc_ref[j, :, lanes]
            if j in plans:
                total = total + conv_columns(*plans[j], lanes)
            out_ref[place, :, lanes] = total.astype(BF16)


def grad_weight_body(entries, outs, flip, scal_ref, *refs):
    n_in, n_out = len(entries), len(outs)
    inputs, grads = refs[:n_in], refs[n_in : n_in + n_out]
    keep_ref, send_ref, left, right, packed = refs[n_in + n_out :]
    rows, packed_len = inputs[0].shape
    half = LANES // 2
    width = LANES * n_out
    for i, start in enumerate(range(0, packed_len, LANES)):
        lanes = slice(start, start + LANES)
        span = slice(i * rows, (i + 1) * rows)
        for k, ref in enumerate(inputs):
            left[span, k * LANES : (k + 1) * LANES] = ref[:, lanes]
        for j, ref in enumerate(grads):
            value = ref[:, lanes].astype(F32)
            right[span, j * LANES : (j + 1) * LANES] = shift_rows(value, -1).astype(BF16)
            right[span, width + j * LANES : width + (j + 1) * LANES] = ref[:, lanes]
            right[span, 2 * width + j * LANES : 2 * width + (j + 1) * LANES] = shift_rows(value, 1).astype(BF16)
    product = lax.dot_general(left[...], right[...], (((0,), (0,)), ((), ())), preferred_element_type=F32)
    lane = lax.broadcasted_iota(jnp.int32, (half // 2, LANES), 1)
    packed[27 * half // 2 :] = jnp.zeros((packed.shape[0] - 27 * half // 2, LANES), F32)
    quarter = half // 2
    for kind in ("own", "on", "off"):
        for step_z in range(3):
            for dy in range(3):
                total = None
                for k, (this, place) in enumerate(entries):
                    for j, out_place in enumerate(outs):
                        if this == kind and place - out_place + 1 == step_z:
                            block = product[
                                k * LANES : (k + 1) * LANES,
                                dy * width + j * LANES : dy * width + (j + 1) * LANES,
                            ]
                            total = block if total is None else total + block
                direct = jnp.where(lane < half, total[:quarter], total[3 * quarter :])
                turned = jnp.where(lane < half, total[quarter : 2 * quarter], total[2 * quarter : 3 * quarter])
                tap = tap_group(scal_ref, kind, flip, step_z) + dy
                packed[pl.ds(pl.multiple_of(tap * quarter, quarter), quarter), :] = direct + pltpu.roll(turned, half, 1)
    share = packed.shape[0] // 2
    core = scal_ref[1]
    keep_ref[...] = packed[pl.ds(pl.multiple_of(core * share, quarter), share), :]
    send_ref[...] = packed[pl.ds(pl.multiple_of((1 - core) * share, quarter), share), :]


def unpack_body(where_ref, *refs):
    pieces, out_ref, packed = refs[:-2], refs[-2], refs[-1]
    share = pieces[0].shape[0]
    for i, ref in enumerate(pieces):
        packed[where_ref[i]] = ref[...].astype(F32)
    flat = packed[...].reshape(-1, LANES)
    taps, height, _ = out_ref.shape
    quarter = height // 2
    for tap in range(taps):
        block = flat[tap * quarter : (tap + 1) * quarter]
        out_ref[tap, :quarter, :] = block[:, : LANES // 2]
        out_ref[tap, quarter:, :] = pltpu.roll(block, LANES // 2, 1)[:, : LANES // 2]


def pair_on(size):
    return [(i, i ^ 1) for i in range(size)]


def pair_off(size):
    return [(i, (i - 1) % size if i % 2 == 0 else (i + 1) % size) for i in range(size)]


def sum_over_mesh(keep, send, phases, slabs):
    phase, slab = lax.axis_index("phase"), lax.axis_index("slab")
    core, column, level = phase % 2, phase // 2 % 2, phase // 4
    both = ("phase", "slab")
    summed = keep + lax.ppermute(send, "phase", pair_on(phases))
    groups = 2 * slabs
    chunks = summed.reshape(groups, summed.shape[0] // groups, LANES)

    def moves(dx, ds):
        return [
            (p * slabs + s, (p ^ (2 * dx)) * slabs + (s + ds) % slabs) for p in range(phases) for s in range(slabs)
        ]

    offsets = [(dx, ds) for dx in range(2) for ds in range(slabs) if (dx, ds) != (0, 0)]
    place = lambda dx, ds: (column ^ dx) * slabs + (slab + ds) % slabs
    part = lax.dynamic_index_in_dim(chunks, place(0, 0), 0, keepdims=False)
    arrived = [
        lax.ppermute(lax.dynamic_index_in_dim(chunks, place(dx, ds), 0, keepdims=False), both, moves(dx, ds))
        for dx, ds in offsets
    ]
    for value in arrived:
        part = part + value
    levels = phases // 4
    arrived = [
        lax.ppermute(part, "phase", [(p, (p + 4 * k) % phases) for p in range(phases)]) for k in range(1, levels)
    ]
    for value in arrived:
        part = part + value
    part = part.astype(BF16)
    pieces, where = [part], [place(0, 0)]
    for dx, ds in offsets:
        pieces.append(lax.ppermute(part, both, moves(dx, ds)))
        where.append(place(dx, -ds))
    other = [lax.ppermute(piece, "phase", pair_on(phases)) for piece in pieces]
    spots = jnp.stack([core * groups + w for w in where] + [(1 - core) * groups + w for w in where])
    return pieces + other, spots.astype(jnp.int32)


def local(phases, slabs, features, conv_weight, projection, grad_out, sens, mask):
    _, depth_len, row_len, packed_len = features.shape
    channels = conv_weight.shape[1]
    col_len = packed_len // channels
    coils = sens.shape[1]
    taps = conv_weight.shape[0]
    slab, core = lax.axis_index("slab"), lax.axis_index("phase") % 2
    flip = slabs == 2
    scal = jnp.stack([slab, core]).astype(jnp.int32)
    on, off = pair_on(phases), pair_off(phases)

    def pass_phase(value, perm):
        return lax.ppermute(value, "phase", perm)

    if flip:
        order = list(range(depth_len))
        edges = [(depth_len - 1, depth_len, [(0, 1), (1, 0)])]
        pick = lambda j: jnp.where(slab == 1, depth_len - 1 - j, j)
    else:
        order = list(range(depth_len))
        up = [(i, i + 1) for i in range(slabs - 1)]
        edges = [(depth_len - 1, -1, up), (0, depth_len, [(j, i) for i, j in up])]
        pick = lambda j: j

    def halo(own):
        off_in = {}
        for j in [edge[0] for edge in edges] + [j for j in order if all(j != edge[0] for edge in edges)]:
            off_in[j] = pass_phase(own[j], off)
        slab_in = [lax.ppermute(own[edge[0]], "slab", edge[2]) for edge in edges]
        on_in = [pass_phase(own[j], on) for j in order]
        corner_off = [lax.ppermute(off_in[edge[0]], "slab", edge[2]) for edge in edges]
        corner_on = [pass_phase(value, on) for value in slab_in]
        main = list(own) + slab_in + on_in + [off_in[j] for j in order]
        corners = []
        for a, b in zip(corner_off, corner_on):
            corners += [a, b]
        return main, corners

    main_entries = (
        [("own", j) for j in order]
        + [("own", edge[1]) for edge in edges]
        + [("on", j) for j in order]
        + [("off", j) for j in order]
    )
    corner_entries = []
    corner_groups = []
    for edge in edges:
        near = min(max(edge[1], 0), depth_len - 1)
        corner_groups.append(([("off", edge[1]), ("on", edge[1])], near))
        corner_entries += [("off", edge[1]), ("on", edge[1])]
    corner_groups.sort(key=lambda g: g[1])

    own_features = [lax.dynamic_index_in_dim(features[0], pick(j), 0, keepdims=False) for j in order]
    main_in, corner_in = halo(own_features)

    high, low = dft_packed(row_len)
    high, low = jnp.asarray(high), jnp.asarray(low)
    lines = depth_len * coils * col_len
    grad_now = grad_out[0]
    line_shape = (lines, 2 * row_len)
    scratch = [pltpu.VMEM(line_shape, BF16)] * 2
    coil_flops = 3 * 2 * lines * (2 * row_len) ** 2
    own_lines, sent_lines = call(
        coil_forward_body,
        (jax.ShapeDtypeStruct(line_shape, F32), jax.ShapeDtypeStruct(line_shape, BF16)),
        4,
        scratch=scratch,
        flops=coil_flops,
        nbytes=4000000,
    )(grad_now, sens, high, low)
    other_lines = [
        lax.ppermute(sent_lines, "slab", [(i, (i + k) % slabs) for i in range(slabs)]) for k in range(1, slabs)
    ]
    grad_image = call(
        functools.partial(coil_backward_body, slabs),
        jax.ShapeDtypeStruct(grad_now.shape, F32),
        6 + len(other_lines),
        scratch=scratch,
        flops=coil_flops,
        nbytes=5000000,
    )(grad_now, sens, mask[0], high, low, own_lines, *other_lines)

    def two_columns(weight):
        zero = jnp.zeros_like(weight)
        return jnp.concatenate(
            [jnp.concatenate([weight, zero], axis=2), jnp.concatenate([zero, weight], axis=2)], axis=1
        )

    weight_forward = two_columns(conv_weight)
    weight_backward = two_columns(jnp.swapaxes(conv_weight[::-1], 1, 2))
    spread = -(projection[:, None, None, :] * jnp.eye(col_len, dtype=BF16)[None, :, :, None])
    spread = spread.reshape(2 * col_len, packed_len)
    spread = jnp.concatenate([spread] * 3, axis=0)

    slice_shape = (row_len, packed_len)
    slab_shape = (depth_len, row_len, packed_len)
    conv_flops = 2 * row_len * len(main_entries) * packed_len * 3 * depth_len * LANES
    bands = [pltpu.VMEM((len(g[0]) * LANES, 3 * LANES), BF16) for g in corner_groups]
    small_flops = 2 * row_len * 2 * packed_len * 3 * LANES

    def conv_main(weight, inputs):
        return call(
            functools.partial(conv_main_body, main_entries, tuple(order), flip),
            jax.ShapeDtypeStruct(slab_shape, F32),
            1 + len(inputs),
            1,
            scratch=[pltpu.VMEM((len(inputs) * LANES, 3 * depth_len * LANES), BF16)],
            flops=conv_flops,
            nbytes=5000000,
        )(scal, weight, *inputs)

    def sorted_corners(values):
        if flip:
            return values
        return values[:2] + values[2:]

    acc = conv_main(weight_forward, main_in)
    grad_act = call(
        functools.partial(grad_act_body, corner_groups, flip),
        [jax.ShapeDtypeStruct(slice_shape, BF16)] * depth_len,
        4 + len(corner_in),
        1,
        scratch=bands,
        flops=small_flops,
        nbytes=4000000,
    )(scal, weight_forward, acc, grad_image, spread, *sorted_corners(corner_in))

    main_grad, corner_grad = halo(grad_act)

    share = (taps + 1) // 2 * channels // 2
    keep, send = call(
        functools.partial(grad_weight_body, main_entries + corner_entries, tuple(order), flip),
        [jax.ShapeDtypeStruct((share, LANES), F32)] * 2,
        len(main_in) + len(corner_in) + depth_len,
        1,
        scratch=[
            pltpu.VMEM((packed_len // LANES * row_len, (len(main_in) + len(corner_in)) * LANES), BF16),
            pltpu.VMEM((packed_len // LANES * row_len, 3 * depth_len * LANES), BF16),
            pltpu.VMEM((2 * share, LANES), F32),
        ],
        flops=conv_flops,
        nbytes=5000000,
    )(scal, *main_in, *corner_in, *grad_act)
    pieces, spots = sum_over_mesh(keep, send, phases, slabs)

    acc_back = conv_main(weight_backward, main_grad)
    grad_features = call(
        functools.partial(grad_feature_body, corner_groups, flip),
        jax.ShapeDtypeStruct(slab_shape, BF16),
        2 + len(corner_grad),
        1,
        scratch=bands,
        flops=small_flops,
        nbytes=4000000,
    )(scal, weight_backward, acc_back, *sorted_corners(corner_grad))

    grad_weight = call(
        unpack_body,
        jax.ShapeDtypeStruct(conv_weight.shape, F32),
        len(pieces),
        1,
        scratch=[pltpu.VMEM((len(pieces),) + pieces[0].shape, F32)],
        nbytes=1000000,
    )(spots, *pieces)
    return (grad_image[None], grad_features[None], grad_weight)


def solution(mesh):
    in_specs = (
        P("phase", "slab", None, None),
        P(),
        P(),
        P("phase", "slab", None, None, None),
        P("slab", None, None, None, None),
        P("phase", None, None),
    )
    out_specs = (P("phase", "slab", None, None, None), P("phase", "slab", None, None), P())
    body = functools.partial(local, mesh.shape["phase"], mesh.shape["slab"])
    return jax.shard_map(body, mesh=mesh, in_specs=in_specs, out_specs=out_specs, check_vma=False)
```

profile of v0, /device:TPU:0, one launch (start us, length us, event | category | flops | bytes accessed | tf_op | source)
XLA Modules:
  0.0 79.2 jit_solution(8401340644071768061)
XLA Ops:
  0.7 2.0 %dynamic-slice_bitcast_fusion = (bf16[320,512]{1,0:T(8,128)(2,1)}, bf16[320,512]{1,0:T(8,128)(2,1)}) fusion(bf16[1,2,320,512]{3,2,1,0:T(8,128)(2,1)} %param.8, s32[]{:T(128)S(6)} %select_n.64, s32[]{:T(128)S(6)} %select_n.63), kind=kLoop, calls=%fused_computation.9 | loop fusion | bytes 1310728 | tf_op jit(solution)/shard_map/jit(dynamic_index_in_dim)/squeeze | solution.py:395
  2.7 3.0 %collective-permute-start.1 = (bf16[320,512]{1,0:T(8,128)(2,1)}, bf16[320,512]{1,0:T(8,128)(2,1)}, u32[]{:S(2)}, u32[]{:S(2)}) collective-permute-start(bf16[320,512]{1,0:T(8,128)(2,1)} %get-tuple-element.15.refs_1_), channel_id=1, source_target_pairs={{0,1},{1,0},{2,3},{3,2},{4,5},{5,4},{6,7},{7,6},{8,9},{9,8},{10,11... | collective-permute-start | bytes 983048 | tf_op jit(solution)/shard_map/ppermute | solution.py:371
  5.6 3.7 %collective-permute-start.5 = (bf16[320,512]{1,0:T(8,128)(2,1)}, bf16[320,512]{1,0:T(8,128)(2,1)}, u32[]{:S(2)}, u32[]{:S(2)}) collective-permute-start(bf16[320,512]{1,0:T(8,128)(2,1)} %get-tuple-element.15.refs_1_), channel_id=1, source_target_pairs={{0,30},{2,4},{4,2},{6,8},{8,6},{10,12},{12,10},{14,16},{16,14},{18... | collective-permute-start | bytes 983048 | tf_op jit(solution)/shard_map/ppermute | solution.py:355
  9.3 0.5 collective-permute-start.2
  9.8 1.1 %copy-done.1 = bf16[640,640]{1,0:T(8,128)(2,1)S(1)} copy-done((bf16[640,640]{1,0:T(8,128)(2,1)S(1)}, bf16[640,640]{1,0:T(8,128)(2,1)}, u32[]{:S(2)}) %copy-start.1) | copy-done | bytes 819224
  11.0 1.1 %copy-done.3 = f32[2,16,2,8,320]{4,3,2,1,0:T(8,128)S(1)} copy-done((f32[2,16,2,8,320]{4,3,2,1,0:T(8,128)S(1)}, f32[2,16,2,8,320]{4,3,2,1,0:T(8,128)}, u32[]{:S(2)}) %copy-start.3) | copy-done | bytes 655384
  12.1 1.8 %shard_map.103 = (f32[256,640]{1,0:T(8,128)S(1)}, bf16[256,640]{1,0:T(8,128)(2,1)}) custom-call(f32[2,2,8,320]{3,2,1,0:T(8,128)S(1)} %bitcast.35, f32[2,16,2,8,320]{4,3,2,1,0:T(8,128)S(1)} %copy-done.3, bf16[640,640]{1,0:T(8,128)(2,1)S(1)} %copy-done, bf16[640,640]{1,0:T(8,128)(2,1)S(1)} %copy-done.1), custom_call_target="tpu_custom_call" | custom-call | flops 629145600 | bytes 4000000 | tf_op jit(solution)/shard_map/pallas_call | solution.py:405
  13.9 0.5 collective-permute-start
  14.5 0.1 neg.8
  14.7 2.3 %collective-permute-start.4 = (bf16[320,512]{1,0:T(8,128)(2,1)}, bf16[320,512]{1,0:T(8,128)(2,1)}, u32[]{:S(2)}, u32[]{:S(2)}) collective-permute-start(bf16[320,512]{1,0:T(8,128)(2,1)} %get-tuple-element.16.refs_0_), channel_id=1, source_target_pairs={{0,30},{2,4},{4,2},{6,8},{8,6},{10,12},{12,10},{14,16},{16,14},{18... | collective-permute-start | bytes 983048 | tf_op jit(solution)/shard_map/ppermute | solution.py:355
  17.0 1.5 %fusion.5.weight_ref = bf16[27,128,128]{2,1,0:T(8,128)(2,1)S(1)} fusion(bf16[27,64,64]{2,1,0:T(8,128)(2,1)} %param.9), kind=kLoop, calls=%fused_computation.7 | loop fusion | flops 3538944 | bytes 1105920 | tf_op jit(solution)/shard_map/concatenate | solution.py:427
  18.5 1.6 %collective-permute-start.6 = (bf16[320,512]{1,0:T(8,128)(2,1)}, bf16[320,512]{1,0:T(8,128)(2,1)S(1)}, u32[]{:S(2)}, u32[]{:S(2)}) collective-permute-start(bf16[320,512]{1,0:T(8,128)(2,1)} %collective-permute-done.5.refs_6_), channel_id=1, source_target_pairs={{0,1},{1,0},{2,3},{3,2},{4,5},{5,4},{6,7},{7,6},{8,9},{9,8},{10,11... | collective-permute-start | bytes 983048 | tf_op jit(solution)/shard_map/ppermute | solution.py:373
  20.1 4.7 %collective-permute-done.refs_0_ = bf16[256,640]{1,0:T(8,128)(2,1)S(1)} collective-permute-done((bf16[256,640]{1,0:T(8,128)(2,1)}, bf16[256,640]{1,0:T(8,128)(2,1)S(1)}, u32[]{:S(2)}, u32[]{:S(2)}) %collective-permute-start) | collective-permute-done | bytes 327712 | tf_op jit(solution)/shard_map/ppermute | solution.py:414
  24.8 2.1 %shard_map.104.image_ref = f32[2,2,8,320]{3,2,1,0:T(8,128)} custom-call(f32[2,2,8,320]{3,2,1,0:T(8,128)S(1)} %bitcast.36, f32[2,16,2,8,320]{4,3,2,1,0:T(8,128)S(1)} %copy-done.4, s32[4,320]{1,0:T(4,128)S(1)} %bitcast.38, bf16[640,640]{1,0:T(8,128)(2,1)S(1)} %copy-done, bf16[640,640]{1,0:T(8,128)(2,1)S(1)} %copy-done.2, ...), custom_call_target="tpu_custom_call" | custom-call | flops 629145600 | bytes 5000000 | tf_op jit(solution)/shard_map/pallas_call | solution.py:416
  26.9 3.9 %shard_map.105.acc_ref = f32[2,320,512]{2,1,0:T(8,128)S(1)} custom-call(s32[2]{0:T(128)S(1)} %pad_add_fusion.scal_ref, bf16[27,128,128]{2,1,0:T(8,128)(2,1)S(1)} %fusion.5.weight_ref, bf16[320,512]{1,0:T(8,128)(2,1)} %get-tuple-element.16.refs_0_, bf16[320,512]{1,0:T(8,128)(2,1)} %get-tuple-element.15.refs_1_, ...), custom_call_target="tpu_custom_call" | custom-call | flops 1761607680 | bytes 5000000 | tf_op jit(solution)/shard_map/pallas_call | solution.py:444
  30.9 1.4 %shard_map.106 = (bf16[320,512]{1,0:T(8,128)(2,1)S(1)}, bf16[320,512]{1,0:T(8,128)(2,1)S(1)}) custom-call(s32[2]{0:T(128)S(1)} %pad_add_fusion.scal_ref, bf16[27,128,128]{2,1,0:T(8,128)(2,1)S(1)} %fusion.5.weight_ref, f32[2,320,512]{2,1,0:T(8,128)S(1)} %shard_map.105.acc_ref, f32[2,2,8,320]{3,2,1,0:T(8,128)S(1)} %copy-done.6, ...), custom_call_target="tpu_custom_call" | custom-call | flops 251658240 | bytes 4000000 | tf_op jit(solution)/shard_map/pallas_call | solution.py:460
  32.3 4.7 %shard_map.109 = (f32[448,128]{1,0:T(8,128)S(1)}, f32[448,128]{1,0:T(8,128)S(1)}) custom-call(s32[2]{0:T(128)S(1)} %pad_add_fusion.scal_ref, bf16[320,512]{1,0:T(8,128)(2,1)} %get-tuple-element.16.refs_0_, bf16[320,512]{1,0:T(8,128)(2,1)} %get-tuple-element.15.refs_1_, bf16[320,512]{1,0:T(8,128)(2,1)} %collective-permute-done.1.refs_2_, ...), custom_call_target="tpu_custom_call" | custom-call | flops 1761607680 | bytes 5000000 | tf_op jit(solution)/shard_map/pallas_call | solution.py:473
  36.9 0.6 collective-permute-start.15
  37.5 1.8 %collective-permute-start.12 = (bf16[320,512]{1,0:T(8,128)(2,1)S(1)}, bf16[320,512]{1,0:T(8,128)(2,1)S(1)}, u32[]{:S(2)}, u32[]{:S(2)}) collective-permute-start(bf16[320,512]{1,0:T(8,128)(2,1)S(1)} %get-tuple-element.12.refs_1_.refs_10_), channel_id=1, source_target_pairs={{0,30},{2,4},{4,2},{6,8},{8,6},{10,12},{12,10},{14,16},{16,14},{18... | collective-permute-start | bytes 983048 | tf_op jit(solution)/shard_map/ppermute | solution.py:355
  39.3 2.4 %collective-permute-start.16 = (f32[112,128]{1,0:T(8,128)S(1)}, f32[112,128]{1,0:T(8,128)S(1)}, u32[]{:S(2)}, u32[]{:S(2)}) collective-permute-start(f32[112,128]{1,0:T(8,128)S(1)} %get-tuple-element.17), channel_id=1, source_target_pairs={{0,1},{1,0},{2,3},{3,2},{4,5},{5,4},{6,7},{7,6},{8,9},{9,8},{10,11... | collective-permute-start | bytes 172040 | tf_op jit(solution)/shard_map/ppermute | solution.py:322
  41.7 1.5 %collective-permute-start.18 = (f32[112,128]{1,0:T(8,128)S(1)}, f32[112,128]{1,0:T(8,128)S(1)}, u32[]{:S(2)}, u32[]{:S(2)}) collective-permute-start(f32[112,128]{1,0:T(8,128)S(1)} %get-tuple-element.18), channel_id=1, source_target_pairs={{0,5},{1,4},{2,7},{3,6},{4,1},{5,0},{6,3},{7,2},{8,13},{9,12},{10,... | collective-permute-start | bytes 172040 | tf_op jit(solution)/shard_map/ppermute | solution.py:322
  43.2 1.9 %collective-permute-start.8 = (bf16[320,512]{1,0:T(8,128)(2,1)S(1)}, bf16[320,512]{1,0:T(8,128)(2,1)S(1)}, u32[]{:S(2)}, u32[]{:S(2)}) collective-permute-start(bf16[320,512]{1,0:T(8,128)(2,1)S(1)} %get-tuple-element.12.refs_1_.refs_10_), channel_id=1, source_target_pairs={{0,1},{1,0},{2,3},{3,2},{4,5},{5,4},{6,7},{7,6},{8,9},{9,8},{10,11... | collective-permute-start | bytes 983048 | tf_op jit(solution)/shard_map/ppermute | solution.py:371
  45.2 4.5 %collective-permute-done.17 = f32[112,128]{1,0:T(8,128)S(1)} collective-permute-done((f32[112,128]{1,0:T(8,128)S(1)}, f32[112,128]{1,0:T(8,128)S(1)}, u32[]{:S(2)}, u32[]{:S(2)}) %collective-permute-start.17) | collective-permute-done | bytes 57376 | tf_op jit(solution)/shard_map/ppermute | solution.py:322
  49.7 0.7 collective-permute-done.18
  50.4 2.9 %collective-permute-start.20 = (f32[112,128]{1,0:T(8,128)S(1)}, f32[112,128]{1,0:T(8,128)S(1)}, u32[]{:S(2)}, u32[]{:S(2)}) collective-permute-start(f32[112,128]{1,0:T(8,128)S(1)} %fusion.7), channel_id=1, source_target_pairs={{0,16},{2,18},{4,20},{6,22},{8,24},{10,26},{12,28},{14,30},{16,0},... | collective-permute-start | bytes 172040 | tf_op jit(solution)/shard_map/ppermute | solution.py:329
  53.4 0.9 %collective-permute-start.21 = (f32[112,128]{1,0:T(8,128)S(1)}, f32[112,128]{1,0:T(8,128)S(1)}, u32[]{:S(2)}, u32[]{:S(2)}) collective-permute-start(f32[112,128]{1,0:T(8,128)S(1)} %fusion.7), channel_id=1, source_target_pairs={{0,24},{2,26},{4,28},{6,30},{8,0},{10,2},{12,4},{14,6},{16,8},{18,... | collective-permute-start | bytes 172040 | tf_op jit(solution)/shard_map/ppermute | solution.py:329
  54.3 0.2 copy.11
  54.5 0.8 collective-permute-start.11
  55.3 1.2 %collective-permute-done.19 = f32[112,128]{1,0:T(8,128)S(1)} collective-permute-done((f32[112,128]{1,0:T(8,128)S(1)}, f32[112,128]{1,0:T(8,128)S(1)}, u32[]{:S(2)}, u32[]{:S(2)}) %collective-permute-start.19) | collective-permute-done | bytes 57376 | tf_op jit(solution)/shard_map/ppermute | solution.py:329
  56.5 0.7 collective-permute-done.20
  57.2 0.7 collective-permute-start.13
  57.9 0.2 collective-permute-start.14
  58.2 1.2 %collective-permute-start.22 = (bf16[112,128]{1,0:T(8,128)(2,1)S(1)}, bf16[112,128]{1,0:T(8,128)(2,1)S(1)}, u32[]{:S(2)}, u32[]{:S(2)}) collective-permute-start(bf16[112,128]{1,0:T(8,128)(2,1)S(1)} %add_convert_fusion.refs_0_), channel_id=1, source_target_pairs={{0,1},{1,0},{2,3},{3,2},{4,5},{5,4},{6,7},{7,6},{8,9},{9,8},{10,11... | collective-permute-start | bytes 86024 | tf_op jit(solution)/shard_map/ppermute | solution.py:336
  59.4 4.4 %collective-permute-done.11.refs_5_ = bf16[320,512]{1,0:T(8,128)(2,1)S(1)} collective-permute-done((bf16[320,512]{1,0:T(8,128)(2,1)S(1)}, bf16[320,512]{1,0:T(8,128)(2,1)S(1)}, u32[]{:S(2)}, u32[]{:S(2)}) %collective-permute-start.11) | collective-permute-done | bytes 327712 | tf_op jit(solution)/shard_map/ppermute | solution.py:355
  63.8 0.7 copy-done.8
  64.5 0.3 collective-permute-start.23
  64.8 0.7 copy-done.10
  65.5 2.7 %collective-permute-start.24 = (bf16[112,128]{1,0:T(8,128)(2,1)S(1)}, bf16[112,128]{1,0:T(8,128)(2,1)S(1)}, u32[]{:S(2)}, u32[]{:S(2)}) collective-permute-start(bf16[112,128]{1,0:T(8,128)(2,1)S(1)} %add_convert_fusion.refs_0_), channel_id=1, source_target_pairs={{0,5},{1,4},{2,7},{3,6},{4,1},{5,0},{6,3},{7,2},{8,13},{9,12},{10,... | collective-permute-start | bytes 86024 | tf_op jit(solution)/shard_map/ppermute | solution.py:336
  68.2 0.3 fusion.4.weight_ref
  68.5 0.1 stack.47.where_ref
  68.6 0.6 collective-permute-start.26
  69.2 1.1 %collective-permute-done.24.refs_3_ = bf16[112,128]{1,0:T(8,128)(2,1)S(1)} collective-permute-done((bf16[112,128]{1,0:T(8,128)(2,1)S(1)}, bf16[112,128]{1,0:T(8,128)(2,1)S(1)}, u32[]{:S(2)}, u32[]{:S(2)}) %collective-permute-start.24) | collective-permute-done | bytes 28704 | tf_op jit(solution)/shard_map/ppermute | solution.py:336
  70.3 0.5 collective-permute-start.28
  70.8 1.0 %copy-done.9 = bf16[320,512]{1,0:T(8,128)(2,1)S(1)} copy-done((bf16[320,512]{1,0:T(8,128)(2,1)S(1)}, bf16[320,512]{1,0:T(8,128)(2,1)}, u32[]{:S(2)}) %copy-start.9) | copy-done | bytes 327704
  71.8 1.0 %copy-done.11 = bf16[320,512]{1,0:T(8,128)(2,1)S(1)} copy-done((bf16[320,512]{1,0:T(8,128)(2,1)S(1)}, bf16[320,512]{1,0:T(8,128)(2,1)}, u32[]{:S(2)}) %copy-start.11) | copy-done | bytes 327704
  72.8 2.8 %shard_map.107.acc_ref = f32[2,320,512]{2,1,0:T(8,128)S(1)} custom-call(s32[2]{0:T(128)S(1)} %pad_add_fusion.scal_ref, bf16[27,128,128]{2,1,0:T(8,128)(2,1)S(1)} %fusion.4.weight_ref, bf16[320,512]{1,0:T(8,128)(2,1)S(1)} %get-tuple-element.11.refs_0_.refs_9_, bf16[320,512]{1,0:T(8,128)(2,1)S(1)} %get-tuple-element.12.refs_1_.refs_10_, ...), custom_call_target="tpu_custom_call" | custom-call | flops 1761607680 | bytes 5000000 | tf_op jit(solution)/shard_map/pallas_call | solution.py:444
  75.6 1.7 %shard_map.110 = f32[27,64,64]{2,1,0:T(8,128)} custom-call(s32[8]{0:T(128)S(1)} %stack.47.where_ref, bf16[112,128]{1,0:T(8,128)(2,1)S(1)} %add_convert_fusion.refs_0_, bf16[112,128]{1,0:T(8,128)(2,1)S(1)} %collective-permute-done.22.refs_1_, bf16[112,128]{1,0:T(8,128)(2,1)S(1)} %collective-permute-done.23.refs_2_, ...), custom_call_target="tpu_custom_call" | custom-call | bytes 1000000 | tf_op jit(solution)/shard_map/pallas_call | solution.py:499
  77.3 1.9 %shard_map.108 = bf16[2,320,512]{2,1,0:T(8,128)(2,1)} custom-call(s32[2]{0:T(128)S(1)} %pad_add_fusion.scal_ref, bf16[27,128,128]{2,1,0:T(8,128)(2,1)S(1)} %fusion.4.weight_ref, f32[2,320,512]{2,1,0:T(8,128)S(1)} %shard_map.107.acc_ref, bf16[320,512]{1,0:T(8,128)(2,1)S(1)} %collective-permute-done.13.refs_0_, ...), custom_call_target="tpu_custom_call" | custom-call | flops 251658240 | bytes 4000000 | tf_op jit(solution)/shard_map/pallas_call | solution.py:489
  (61 shorter events, 0.5 us)
Async XLA Ops:
  0.6 9.2 %copy-start = (bf16[640,640]{1,0:T(8,128)(2,1)S(1)}, bf16[640,640]{1,0:T(8,128)(2,1)}, u32[]{:S(2)}) copy-start(bf16[640,640]{1,0:T(8,128)(2,1)} %constant.91.clone.high_ref) | copy-start | bytes 2457604
  0.6 9.2 %copy-start.5 = (f32[1,2,2,8,320]{4,3,2,1,0:T(8,128)S(1)}, f32[1,2,2,8,320]{4,3,2,1,0:T(8,128)}, u32[]{:S(2)}) copy-start(f32[1,2,2,8,320]{4,3,2,1,0:T(8,128)} %param.11) | copy-start | bytes 122884
  2.7 11.8 %copy-start.13 = (bf16[2,64]{1,0:T(2,128)(2,1)S(1)}, bf16[2,64]{1,0:T(2,128)(2,1)}, u32[]{:S(2)}) copy-start(bf16[2,64]{1,0:T(2,128)(2,1)} %param.10) | copy-start | bytes 772
  2.7 12.0 %collective-permute-start.1 = (bf16[320,512]{1,0:T(8,128)(2,1)}, bf16[320,512]{1,0:T(8,128)(2,1)}, u32[]{:S(2)}, u32[]{:S(2)}) collective-permute-start(bf16[320,512]{1,0:T(8,128)(2,1)} %get-tuple-element.15.refs_1_), channel_id=1, source_target_pairs={{0,1},{1,0},{2,3},{3,2},{4,5},{5,4},{6,7},{7,6},{8,9},{9,8},{10,11... | collective-permute-start | bytes 983048 | tf_op jit(solution)/shard_map/ppermute | solution.py:371
  5.6 12.8 %collective-permute-start.5 = (bf16[320,512]{1,0:T(8,128)(2,1)}, bf16[320,512]{1,0:T(8,128)(2,1)}, u32[]{:S(2)}, u32[]{:S(2)}) collective-permute-start(bf16[320,512]{1,0:T(8,128)(2,1)} %get-tuple-element.15.refs_1_), channel_id=1, source_target_pairs={{0,30},{2,4},{4,2},{6,8},{8,6},{10,12},{12,10},{14,16},{16,14},{18... | collective-permute-start | bytes 983048 | tf_op jit(solution)/shard_map/ppermute | solution.py:355
  9.3 17.6 %collective-permute-start.3 = (bf16[320,512]{1,0:T(8,128)(2,1)}, bf16[320,512]{1,0:T(8,128)(2,1)}, u32[]{:S(2)}, u32[]{:S(2)}) collective-permute-start(bf16[320,512]{1,0:T(8,128)(2,1)} %get-tuple-element.15.refs_1_), channel_id=1, source_target_pairs={{0,2},{2,0},{4,6},{6,4},{8,10},{10,8},{12,14},{14,12},{16,18},{18,... | collective-permute-start | bytes 983048 | tf_op jit(solution)/shard_map/ppermute | solution.py:355
  9.3 17.6 %collective-permute-start.2 = (bf16[320,512]{1,0:T(8,128)(2,1)}, bf16[320,512]{1,0:T(8,128)(2,1)}, u32[]{:S(2)}, u32[]{:S(2)}) collective-permute-start(bf16[320,512]{1,0:T(8,128)(2,1)} %get-tuple-element.16.refs_0_), channel_id=1, source_target_pairs={{0,2},{2,0},{4,6},{6,4},{8,10},{10,8},{12,14},{14,12},{16,18},{18,... | collective-permute-start | bytes 983048 | tf_op jit(solution)/shard_map/ppermute | solution.py:355
  9.8 1.1 %copy-start.1 = (bf16[640,640]{1,0:T(8,128)(2,1)S(1)}, bf16[640,640]{1,0:T(8,128)(2,1)}, u32[]{:S(2)}) copy-start(bf16[640,640]{1,0:T(8,128)(2,1)} %constant.92.clone.low_ref) | copy-start | bytes 2457604
  11.0 1.1 %copy-start.3 = (f32[2,16,2,8,320]{4,3,2,1,0:T(8,128)S(1)}, f32[2,16,2,8,320]{4,3,2,1,0:T(8,128)}, u32[]{:S(2)}) copy-start(f32[2,16,2,8,320]{4,3,2,1,0:T(8,128)} %sens_ref.3) | copy-start | bytes 1966084
  12.1 12.7 %copy-start.4 = (f32[2,16,2,8,320]{4,3,2,1,0:T(8,128)S(1)}, f32[2,16,2,8,320]{4,3,2,1,0:T(8,128)}, u32[]{:S(2)}) copy-start(f32[2,16,2,8,320]{4,3,2,1,0:T(8,128)} %sens_ref.3) | copy-start | bytes 1966084
  13.9 10.9 %copy-start.2 = (bf16[640,640]{1,0:T(8,128)(2,1)S(1)}, bf16[640,640]{1,0:T(8,128)(2,1)}, u32[]{:S(2)}) copy-start(bf16[640,640]{1,0:T(8,128)(2,1)} %constant.92.clone.low_ref) | copy-start | bytes 2457604
  13.9 10.9 %copy-start.7 = (s32[1,4,320]{2,1,0:T(4,128)S(1)}, s32[1,4,320]{2,1,0:T(4,128)}, u32[]{:S(2)}) copy-start(s32[1,4,320]{2,1,0:T(4,128)} %param.13) | copy-start | bytes 15364
  13.9 10.8 %collective-permute-start = (bf16[256,640]{1,0:T(8,128)(2,1)}, bf16[256,640]{1,0:T(8,128)(2,1)S(1)}, u32[]{:S(2)}, u32[]{:S(2)}) collective-permute-start(bf16[256,640]{1,0:T(8,128)(2,1)} %get-tuple-element.10), channel_id=1, source_target_pairs={{0,1},{1,0},{2,3},{3,2},{4,5},{5,4},{6,7},{7,6},{8,9},{9,8},{10,11... | collective-permute-start | bytes 983048 | tf_op jit(solution)/shard_map/ppermute | solution.py:414
  14.7 12.3 %collective-permute-start.4 = (bf16[320,512]{1,0:T(8,128)(2,1)}, bf16[320,512]{1,0:T(8,128)(2,1)}, u32[]{:S(2)}, u32[]{:S(2)}) collective-permute-start(bf16[320,512]{1,0:T(8,128)(2,1)} %get-tuple-element.16.refs_0_), channel_id=1, source_target_pairs={{0,30},{2,4},{4,2},{6,8},{8,6},{10,12},{12,10},{14,16},{16,14},{18... | collective-permute-start | bytes 983048 | tf_op jit(solution)/shard_map/ppermute | solution.py:355
  18.5 12.4 %collective-permute-start.6 = (bf16[320,512]{1,0:T(8,128)(2,1)}, bf16[320,512]{1,0:T(8,128)(2,1)S(1)}, u32[]{:S(2)}, u32[]{:S(2)}) collective-permute-start(bf16[320,512]{1,0:T(8,128)(2,1)} %collective-permute-done.5.refs_6_), channel_id=1, source_target_pairs={{0,1},{1,0},{2,3},{3,2},{4,5},{5,4},{6,7},{7,6},{8,9},{9,8},{10,11... | collective-permute-start | bytes 983048 | tf_op jit(solution)/shard_map/ppermute | solution.py:373
  24.7 6.1 %collective-permute-start.7 = (bf16[320,512]{1,0:T(8,128)(2,1)}, bf16[320,512]{1,0:T(8,128)(2,1)S(1)}, u32[]{:S(2)}, u32[]{:S(2)}) collective-permute-start(bf16[320,512]{1,0:T(8,128)(2,1)} %collective-permute-done.1.refs_2_), channel_id=1, source_target_pairs={{0,2},{2,0},{4,6},{6,4},{8,10},{10,8},{12,14},{14,12},{16,18},{18,... | collective-permute-start | bytes 983048 | tf_op jit(solution)/shard_map/ppermute | solution.py:355
  26.9 3.9 %copy-start.6 = (f32[2,2,8,320]{3,2,1,0:T(8,128)S(1)}, f32[2,2,8,320]{3,2,1,0:T(8,128)}, u32[]{:S(2)}) copy-start(f32[2,2,8,320]{3,2,1,0:T(8,128)} %shard_map.104.image_ref) | copy-start | bytes 122884
  36.9 17.3 %copy-start.12 = (bf16[27,64,64]{2,1,0:T(8,128)(2,1)S(1)}, bf16[27,64,64]{2,1,0:T(8,128)(2,1)}, u32[]{:S(2)}) copy-start(bf16[27,64,64]{2,1,0:T(8,128)(2,1)} %param.9) | copy-start | bytes 663556
  36.9 2.3 %collective-permute-start.15 = (f32[448,128]{1,0:T(8,128)S(1)}, f32[448,128]{1,0:T(8,128)S(1)}, u32[]{:S(2)}, u32[]{:S(2)}) collective-permute-start(f32[448,128]{1,0:T(8,128)S(1)} %get-tuple-element.14), channel_id=1, source_target_pairs={{0,2},{2,0},{4,6},{6,4},{8,10},{10,8},{12,14},{14,12},{16,18},{18,... | collective-permute-start | bytes 688136 | tf_op jit(solution)/shard_map/ppermute | solution.py:309
  37.5 15.9 %collective-permute-start.12 = (bf16[320,512]{1,0:T(8,128)(2,1)S(1)}, bf16[320,512]{1,0:T(8,128)(2,1)S(1)}, u32[]{:S(2)}, u32[]{:S(2)}) collective-permute-start(bf16[320,512]{1,0:T(8,128)(2,1)S(1)} %get-tuple-element.12.refs_1_.refs_10_), channel_id=1, source_target_pairs={{0,30},{2,4},{4,2},{6,8},{8,6},{10,12},{12,10},{14,16},{16,14},{18... | collective-permute-start | bytes 983048 | tf_op jit(solution)/shard_map/ppermute | solution.py:355
  39.3 5.9 %collective-permute-start.16 = (f32[112,128]{1,0:T(8,128)S(1)}, f32[112,128]{1,0:T(8,128)S(1)}, u32[]{:S(2)}, u32[]{:S(2)}) collective-permute-start(f32[112,128]{1,0:T(8,128)S(1)} %get-tuple-element.17), channel_id=1, source_target_pairs={{0,1},{1,0},{2,3},{3,2},{4,5},{5,4},{6,7},{7,6},{8,9},{9,8},{10,11... | collective-permute-start | bytes 172040 | tf_op jit(solution)/shard_map/ppermute | solution.py:322
  41.7 8.0 %collective-permute-start.17 = (f32[112,128]{1,0:T(8,128)S(1)}, f32[112,128]{1,0:T(8,128)S(1)}, u32[]{:S(2)}, u32[]{:S(2)}) collective-permute-start(f32[112,128]{1,0:T(8,128)S(1)} %get-tuple-element.19), channel_id=1, source_target_pairs={{0,4},{1,5},{2,6},{3,7},{4,0},{5,1},{6,2},{7,3},{8,12},{9,13},{10,... | collective-permute-start | bytes 172040 | tf_op jit(solution)/shard_map/ppermute | solution.py:322
  41.7 8.6 %collective-permute-start.18 = (f32[112,128]{1,0:T(8,128)S(1)}, f32[112,128]{1,0:T(8,128)S(1)}, u32[]{:S(2)}, u32[]{:S(2)}) collective-permute-start(f32[112,128]{1,0:T(8,128)S(1)} %get-tuple-element.18), channel_id=1, source_target_pairs={{0,5},{1,4},{2,7},{3,6},{4,1},{5,0},{6,3},{7,2},{8,13},{9,12},{10,... | collective-permute-start | bytes 172040 | tf_op jit(solution)/shard_map/ppermute | solution.py:322
  43.2 11.3 %collective-permute-start.8 = (bf16[320,512]{1,0:T(8,128)(2,1)S(1)}, bf16[320,512]{1,0:T(8,128)(2,1)S(1)}, u32[]{:S(2)}, u32[]{:S(2)}) collective-permute-start(bf16[320,512]{1,0:T(8,128)(2,1)S(1)} %get-tuple-element.12.refs_1_.refs_10_), channel_id=1, source_target_pairs={{0,1},{1,0},{2,3},{3,2},{4,5},{5,4},{6,7},{7,6},{8,9},{9,8},{10,11... | collective-permute-start | bytes 983048 | tf_op jit(solution)/shard_map/ppermute | solution.py:371
  45.2 13.0 %collective-permute-start.10 = (bf16[320,512]{1,0:T(8,128)(2,1)S(1)}, bf16[320,512]{1,0:T(8,128)(2,1)S(1)}, u32[]{:S(2)}, u32[]{:S(2)}) collective-permute-start(bf16[320,512]{1,0:T(8,128)(2,1)S(1)} %get-tuple-element.12.refs_1_.refs_10_), channel_id=1, source_target_pairs={{0,2},{2,0},{4,6},{6,4},{8,10},{10,8},{12,14},{14,12},{16,18},{18,... | collective-permute-start | bytes 983048 | tf_op jit(solution)/shard_map/ppermute | solution.py:355
  50.4 6.1 %collective-permute-start.19 = (f32[112,128]{1,0:T(8,128)S(1)}, f32[112,128]{1,0:T(8,128)S(1)}, u32[]{:S(2)}, u32[]{:S(2)}) collective-permute-start(f32[112,128]{1,0:T(8,128)S(1)} %fusion.7), channel_id=1, source_target_pairs={{0,8},{2,10},{4,12},{6,14},{8,16},{10,18},{12,20},{14,22},{16,24},... | collective-permute-start | bytes 172040 | tf_op jit(solution)/shard_map/ppermute | solution.py:329
  50.4 6.8 %collective-permute-start.20 = (f32[112,128]{1,0:T(8,128)S(1)}, f32[112,128]{1,0:T(8,128)S(1)}, u32[]{:S(2)}, u32[]{:S(2)}) collective-permute-start(f32[112,128]{1,0:T(8,128)S(1)} %fusion.7), channel_id=1, source_target_pairs={{0,16},{2,18},{4,20},{6,22},{8,24},{10,26},{12,28},{14,30},{16,0},... | collective-permute-start | bytes 172040 | tf_op jit(solution)/shard_map/ppermute | solution.py:329
  53.4 4.5 %collective-permute-start.21 = (f32[112,128]{1,0:T(8,128)S(1)}, f32[112,128]{1,0:T(8,128)S(1)}, u32[]{:S(2)}, u32[]{:S(2)}) collective-permute-start(f32[112,128]{1,0:T(8,128)S(1)} %fusion.7), channel_id=1, source_target_pairs={{0,24},{2,26},{4,28},{6,30},{8,0},{10,2},{12,4},{14,6},{16,8},{18,... | collective-permute-start | bytes 172040 | tf_op jit(solution)/shard_map/ppermute | solution.py:329
  54.5 9.3 %collective-permute-start.11 = (bf16[320,512]{1,0:T(8,128)(2,1)S(1)}, bf16[320,512]{1,0:T(8,128)(2,1)S(1)}, u32[]{:S(2)}, u32[]{:S(2)}) collective-permute-start(bf16[320,512]{1,0:T(8,128)(2,1)S(1)} %get-tuple-element.11.refs_0_.refs_9_), channel_id=1, source_target_pairs={{0,30},{2,4},{4,2},{6,8},{8,6},{10,12},{12,10},{14,16},{16,14},{18... | collective-permute-start | bytes 983048 | tf_op jit(solution)/shard_map/ppermute | solution.py:355
  56.5 8.3 %collective-permute-start.9 = (bf16[320,512]{1,0:T(8,128)(2,1)S(1)}, bf16[320,512]{1,0:T(8,128)(2,1)S(1)}, u32[]{:S(2)}, u32[]{:S(2)}) collective-permute-start(bf16[320,512]{1,0:T(8,128)(2,1)S(1)} %get-tuple-element.11.refs_0_.refs_9_), channel_id=1, source_target_pairs={{0,2},{2,0},{4,6},{6,4},{8,10},{10,8},{12,14},{14,12},{16,18},{18,... | collective-permute-start | bytes 983048 | tf_op jit(solution)/shard_map/ppermute | solution.py:355
  57.2 20.0 %collective-permute-start.13 = (bf16[320,512]{1,0:T(8,128)(2,1)S(1)}, bf16[320,512]{1,0:T(8,128)(2,1)S(1)}, u32[]{:S(2)}, u32[]{:S(2)}) collective-permute-start(bf16[320,512]{1,0:T(8,128)(2,1)S(1)} %collective-permute-done.12.refs_6_), channel_id=1, source_target_pairs={{0,1},{1,0},{2,3},{3,2},{4,5},{5,4},{6,7},{7,6},{8,9},{9,8},{10,11... | collective-permute-start | bytes 983048 | tf_op jit(solution)/shard_map/ppermute | solution.py:373
  57.9 19.4 %collective-permute-start.14 = (bf16[320,512]{1,0:T(8,128)(2,1)S(1)}, bf16[320,512]{1,0:T(8,128)(2,1)S(1)}, u32[]{:S(2)}, u32[]{:S(2)}) collective-permute-start(bf16[320,512]{1,0:T(8,128)(2,1)S(1)} %collective-permute-done.8.refs_2_), channel_id=1, source_target_pairs={{0,2},{2,0},{4,6},{6,4},{8,10},{10,8},{12,14},{14,12},{16,18},{18,... | collective-permute-start | bytes 983048 | tf_op jit(solution)/shard_map/ppermute | solution.py:355
  58.2 10.0 %collective-permute-start.22 = (bf16[112,128]{1,0:T(8,128)(2,1)S(1)}, bf16[112,128]{1,0:T(8,128)(2,1)S(1)}, u32[]{:S(2)}, u32[]{:S(2)}) collective-permute-start(bf16[112,128]{1,0:T(8,128)(2,1)S(1)} %add_convert_fusion.refs_0_), channel_id=1, source_target_pairs={{0,1},{1,0},{2,3},{3,2},{4,5},{5,4},{6,7},{7,6},{8,9},{9,8},{10,11... | collective-permute-start | bytes 86024 | tf_op jit(solution)/shard_map/ppermute | solution.py:336
  63.8 0.7 copy-start.8
  64.5 4.1 %collective-permute-start.23 = (bf16[112,128]{1,0:T(8,128)(2,1)S(1)}, bf16[112,128]{1,0:T(8,128)(2,1)S(1)}, u32[]{:S(2)}, u32[]{:S(2)}) collective-permute-start(bf16[112,128]{1,0:T(8,128)(2,1)S(1)} %add_convert_fusion.refs_0_), channel_id=1, source_target_pairs={{0,4},{1,5},{2,6},{3,7},{4,0},{5,1},{6,2},{7,3},{8,12},{9,13},{10,... | collective-permute-start | bytes 86024 | tf_op jit(solution)/shard_map/ppermute | solution.py:336
  64.8 0.7 copy-start.10
  65.5 4.8 %collective-permute-start.24 = (bf16[112,128]{1,0:T(8,128)(2,1)S(1)}, bf16[112,128]{1,0:T(8,128)(2,1)S(1)}, u32[]{:S(2)}, u32[]{:S(2)}) collective-permute-start(bf16[112,128]{1,0:T(8,128)(2,1)S(1)} %add_convert_fusion.refs_0_), channel_id=1, source_target_pairs={{0,5},{1,4},{2,7},{3,6},{4,1},{5,0},{6,3},{7,2},{8,13},{9,12},{10,... | collective-permute-start | bytes 86024 | tf_op jit(solution)/shard_map/ppermute | solution.py:336
  68.2 2.1 %collective-permute-start.25 = (bf16[112,128]{1,0:T(8,128)(2,1)S(1)}, bf16[112,128]{1,0:T(8,128)(2,1)S(1)}, u32[]{:S(2)}, u32[]{:S(2)}) collective-permute-start(bf16[112,128]{1,0:T(8,128)(2,1)S(1)} %add_convert_fusion.refs_0_), channel_id=1, source_target_pairs={{0,2},{2,0},{4,6},{6,4},{8,10},{10,8},{12,14},{14,12},{16,18},{18,... | collective-permute-start | bytes 86024 | tf_op jit(solution)/shard_map/ppermute | solution.py:338
  68.6 7.0 %collective-permute-start.26 = (bf16[112,128]{1,0:T(8,128)(2,1)S(1)}, bf16[112,128]{1,0:T(8,128)(2,1)S(1)}, u32[]{:S(2)}, u32[]{:S(2)}) collective-permute-start(bf16[112,128]{1,0:T(8,128)(2,1)S(1)} %collective-permute-done.22.refs_1_), channel_id=1, source_target_pairs={{0,2},{2,0},{4,6},{6,4},{8,10},{10,8},{12,14},{14,12},{16,18},{18,... | collective-permute-start | bytes 86024 | tf_op jit(solution)/shard_map/ppermute | solution.py:338
  70.3 5.3 %collective-permute-start.27 = (bf16[112,128]{1,0:T(8,128)(2,1)S(1)}, bf16[112,128]{1,0:T(8,128)(2,1)S(1)}, u32[]{:S(2)}, u32[]{:S(2)}) collective-permute-start(bf16[112,128]{1,0:T(8,128)(2,1)S(1)} %collective-permute-done.23.refs_2_), channel_id=1, source_target_pairs={{0,2},{2,0},{4,6},{6,4},{8,10},{10,8},{12,14},{14,12},{16,18},{18,... | collective-permute-start | bytes 86024 | tf_op jit(solution)/shard_map/ppermute | solution.py:338
  70.3 5.3 %collective-permute-start.28 = (bf16[112,128]{1,0:T(8,128)(2,1)S(1)}, bf16[112,128]{1,0:T(8,128)(2,1)S(1)}, u32[]{:S(2)}, u32[]{:S(2)}) collective-permute-start(bf16[112,128]{1,0:T(8,128)(2,1)S(1)} %collective-permute-done.24.refs_3_), channel_id=1, source_target_pairs={{0,2},{2,0},{4,6},{6,4},{8,10},{10,8},{12,14},{14,12},{16,18},{18,... | collective-permute-start | bytes 86024 | tf_op jit(solution)/shard_map/ppermute | solution.py:338
  70.8 1.0 %copy-start.9 = (bf16[320,512]{1,0:T(8,128)(2,1)S(1)}, bf16[320,512]{1,0:T(8,128)(2,1)}, u32[]{:S(2)}) copy-start(bf16[320,512]{1,0:T(8,128)(2,1)} %copy-done.8) | copy-start | bytes 983044
  71.8 1.0 %copy-start.11 = (bf16[320,512]{1,0:T(8,128)(2,1)S(1)}, bf16[320,512]{1,0:T(8,128)(2,1)}, u32[]{:S(2)}) copy-start(bf16[320,512]{1,0:T(8,128)(2,1)} %copy-done.10) | copy-start | bytes 983044
where the time goes:
time: 79.6 us; the launch traced here: 79.2 us
  starting transfers between devices  30.6 us (38%)
  Pallas kernels  20.3 us (26%)
  waiting for transfers between devices  17.3 us (22%)
  local copies, waits for them, and re-layouts  8.2 us (10%)
  other arithmetic  1.94 us (2%)
  between operations  0.92 us (1%)
    ppermute x10, starting transfers between devices, pass_phase(): return lax.ppermute(value, 'phase', perm)  9.29 us
    pallas_call x2, Pallas kernels, conv_main(): call(functools.partial(conv_main_body, main_entries, tuple(order), flip),...  6.7 us
    unnamed x29, local copies, waits for them, and re-layouts  5.95 us
    ppermute x3, waiting for transfers between devices, sum_over_mesh(): lax.ppermute(lax.dynamic_index_in_dim(chunks, place(dx, ds), 0, keepdims=...  5.15 us
    ppermute x2, starting transfers between devices, halo(): slab_in = [lax.ppermute(own[edge[0]], 'slab', edge[2]) for edge in edges]  4.91 us
    ppermute x1, waiting for transfers between devices, local(): lax.ppermute(sent_lines, 'slab', [(i, (i + k) % slabs) for i in range(sla...  4.67 us
    pallas_call x1, Pallas kernels, local(): call(functools.partial(grad_weight_body, main_entries + corner_entries, t...  4.67 us
    ppermute x10, waiting for transfers between devices, pass_phase(): return lax.ppermute(value, 'phase', perm)  4.39 us
  transfers between devices with their start and end apart: 29, of which 7 were waited for; matrix products, arithmetic and copies ran while one was open for 3% of the time, Pallas kernels for 16%

commit v1 on v0

--- a/solution.py
+++ b/solution.py
@@ -17,16 +17,27 @@
 LANES = 128
 
 
-def call(body, outs, n_in, n_smem=0, scratch=(), flops=0, nbytes=0):
+ANY = pl.BlockSpec(memory_space=pl.ANY)
+SPECS = {"S": SMEM, "V": VMEM, "M": VMEM}
+
+
+def call(name, body, outs, ins, kinds, scratch=(), flops=0, nbytes=0, after=()):
+    count, waits = len(ins), len(after)
+
+    def run(*refs):
+        body(*refs[:count], *refs[count + waits :])
+
+    ins = [pltpu.with_memory_space_constraint(x, pltpu.VMEM) if kind == "M" else x for x, kind in zip(ins, kinds)]
     return pl.pallas_call(
-        body,
+        run,
         out_shape=outs,
-        in_specs=[SMEM] * n_smem + [VMEM] * n_in,
-        out_specs=jax.tree.map(lambda _: VMEM, outs),
+        in_specs=[SPECS[kind] for kind in kinds] + [ANY] * waits,
+        out_specs=[VMEM] * len(outs) if isinstance(outs, (list, tuple)) else VMEM,
         scratch_shapes=list(scratch),
         compiler_params=pltpu.CompilerParams(vmem_limit_bytes=LIMIT),
         cost_estimate=pl.CostEstimate(flops=flops, bytes_accessed=nbytes, transcendentals=0),
-    )
+        name=name,
+    )(*ins, *after)
 
 
 def dft_packed(length):
@@ -153,7 +164,14 @@
     return jnp.where(place == (0 if step > 0 else rows - 1), 0.0, turned)
 
 
-def fill_band(scal_ref, weight_ref, band, entries, outs, flip):
+def two_columns(weight):
+    zero = jnp.zeros_like(weight)
+    return jnp.concatenate(
+        [jnp.concatenate([weight, zero], axis=1), jnp.concatenate([zero, weight], axis=1)], axis=0
+    ).astype(BF16)
+
+
+def fill_band(scal_ref, weight_ref, band, entries, outs, flip, back):
     width = LANES * len(outs)
     for i, (kind, place) in enumerate(entries):
         for j, out_place in enumerate(outs):
@@ -161,10 +179,16 @@
             for dy in range(3):
                 lanes = slice(dy * width + j * LANES, dy * width + (j + 1) * LANES)
                 if 0 <= step_z <= 2:
-                    block = weight_ref[tap_group(scal_ref, kind, flip, step_z) + dy]
+                    tap = tap_group(scal_ref, kind, flip, step_z) + dy
+                    weight = weight_ref[weight_ref.shape[0] - 1 - tap if back else tap].astype(F32)
+                    block = two_columns(weight.T if back else weight)
                 else:
                     block = jnp.zeros((LANES, LANES), BF16)
                 band[i * LANES : (i + 1) * LANES, lanes] = block
+
+
+def place_of(scal_ref, j, depth_len, flip):
+    return jnp.where(scal_ref[0] == 1, depth_len - 1 - j, j) if flip else j
 
 
 def conv_columns(refs, band, lanes):
@@ -178,34 +202,34 @@
     )
 
 
-def conv_main_body(entries, outs, flip, scal_ref, weight_ref, *refs):
-    inputs, out_ref, band = refs[: len(entries)], refs[-2], refs[-1]
-    fill_band(scal_ref, weight_ref, band, entries, outs, flip)
+def conv_main_body(entries, flip, back, scal_ref, weight_ref, *refs):
+    inputs, out_ref, band = refs[:-2], refs[-2], refs[-1]
+    depth_len = out_ref.shape[0]
+    fill_band(scal_ref, weight_ref, band, entries, tuple(range(depth_len)), flip, back)
     for start in range(0, out_ref.shape[2], LANES):
         lanes = slice(start, start + LANES)
         result = conv_columns(inputs, band, lanes)
-        for j in range(len(outs)):
+        for j in range(depth_len):
             out_ref[j, :, lanes] = result[:, j * LANES : (j + 1) * LANES]
 
 
-def corner_sum(groups, scal_ref, weight_ref, refs, bands, flip):
-    at = 0
+def corner_plans(groups, flip, back, scal_ref, weight_ref, inputs, bands):
     plans = {}
-    for group, ((entries, out_place), band) in enumerate(zip(groups, bands)):
-        fill_band(scal_ref, weight_ref, band, entries, (out_place,), flip)
-        plans[out_place] = (refs[at : at + len(entries)], band)
-        at += len(entries)
+    for (entries, out_place), band in zip(groups, bands):
+        fill_band(scal_ref, weight_ref, band, entries, (out_place,), flip, back)
+        plans[out_place] = (inputs[: len(entries)], band)
+        inputs = inputs[len(entries) :]
     return plans
 
 
-def grad_act_body(groups, flip, scal_ref, weight_ref, acc_ref, image_ref, spread_ref, *refs):
-    n_in = sum(len(entries) for entries, _ in groups)
-    inputs, rest = refs[:n_in], refs[n_in:]
-    outs = rest[: acc_ref.shape[0]]
-    plans = corner_sum(groups, scal_ref, weight_ref, inputs, rest[len(outs) :], flip)
+def grad_act_body(groups, flip, scal_ref, acc_ref, image_ref, spread_ref, weight_ref, *refs):
+    depth_len = acc_ref.shape[0]
+    inputs, refs = refs[: 2 * len(groups)], refs[2 * len(groups) :]
+    outs, bands = refs[:depth_len], refs[depth_len:]
+    plans = corner_plans(groups, flip, False, scal_ref, weight_ref, inputs, bands)
     row_len = image_ref.shape[3]
-    for j, out_ref in enumerate(outs):
-        place = jnp.where(scal_ref[0] == 1, len(outs) - 1 - j, j) if flip else j
+    for j in range(depth_len):
+        place = place_of(scal_ref, j, depth_len, flip)
         image = image_ref[place].reshape(-1, row_len)
         first, low = split(image)
         middle, last = split(image - first.astype(F32))
@@ -219,13 +243,12 @@
             if j in plans:
                 act = act + conv_columns(*plans[j], lanes)
             gate = 0.5 * jnp.tanh(0.5 * act) + 0.5
-            out_ref[:, lanes] = (grad_silu * (gate * (1.0 + act * (1.0 - gate)))).astype(BF16)
-
-
-def grad_feature_body(groups, flip, scal_ref, weight_ref, acc_ref, *refs):
-    n_in = sum(len(entries) for entries, _ in groups)
-    inputs, out_ref, bands = refs[:n_in], refs[n_in], refs[n_in + 1 :]
-    plans = corner_sum(groups, scal_ref, weight_ref, inputs, bands, flip)
+            outs[j][:, lanes] = (grad_silu * (gate * (1.0 + act * (1.0 - gate)))).astype(BF16)
+
+
+def grad_feature_body(groups, flip, scal_ref, acc_ref, weight_ref, *refs):
+    inputs, out_ref, bands = refs[: 2 * len(groups)], refs[2 * len(groups)], refs[2 * len(groups) + 1 :]
+    plans = corner_plans(groups, flip, True, scal_ref, weight_ref, inputs, bands)
     depth_len = acc_ref.shape[0]
     for j in range(depth_len):
         place = jnp.where(scal_ref[0] == 1, depth_len - 1 - j, j) if flip else j
@@ -237,27 +260,50 @@
             out_ref[place, :, lanes] = total.astype(BF16)
 
 
-def grad_weight_body(entries, outs, flip, scal_ref, *refs):
-    n_in, n_out = len(entries), len(outs)
-    inputs, grads = refs[:n_in], refs[n_in : n_in + n_out]
-    keep_ref, send_ref, left, right, packed = refs[n_in + n_out :]
+def stack_body(*refs):
+    inputs, out_ref = refs[:-1], refs[-1]
     rows, packed_len = inputs[0].shape
+    for i, start in enumerate(range(0, packed_len, 2 * LANES)):
+        for k, ref in enumerate(inputs):
+            pair = jnp.concatenate([ref[:, start : start + LANES], ref[:, start + LANES : start + 2 * LANES]], axis=0)
+            value = pair.astype(F32).T
+            out_ref[k * LANES : (k + 1) * LANES, 2 * rows * i : 2 * rows * (i + 1)] = value.astype(BF16)
+
+
+def reach(place, outs):
+    return [j for j, out_place in enumerate(outs) if 0 <= place - out_place + 1 <= 2]
+
+
+def grad_weight_body(groups, outs, flip, scal_ref, *refs):
+    n_out = len(outs)
+    keep_ref, send_ref, right, packed = refs[-4:]
+    stacks, grads = refs[: -4 - n_out], refs[-4 - n_out : -4]
+    rows, packed_len = grads[0].shape
     half = LANES // 2
-    width = LANES * n_out
+    width = 3 * LANES
     for i, start in enumerate(range(0, packed_len, LANES)):
         lanes = slice(start, start + LANES)
         span = slice(i * rows, (i + 1) * rows)
-        for k, ref in enumerate(inputs):
-            left[span, k * LANES : (k + 1) * LANES] = ref[:, lanes]
         for j, ref in enumerate(grads):
             value = ref[:, lanes].astype(F32)
-            right[span, j * LANES : (j + 1) * LANES] = shift_rows(value, -1).astype(BF16)
-            right[span, width + j * LANES : width + (j + 1) * LANES] = ref[:, lanes]
-            right[span, 2 * width + j * LANES : 2 * width + (j + 1) * LANES] = shift_rows(value, 1).astype(BF16)
-    product = lax.dot_general(left[...], right[...], (((0,), (0,)), ((), ())), preferred_element_type=F32)
-    lane = lax.broadcasted_iota(jnp.int32, (half // 2, LANES), 1)
-    packed[27 * half // 2 :] = jnp.zeros((packed.shape[0] - 27 * half // 2, LANES), F32)
+            at = j * width
+            right[span, at : at + LANES] = shift_rows(value, -1).astype(BF16)
+            right[span, at + LANES : at + 2 * LANES] = ref[:, lanes]
+            right[span, at + 2 * LANES : at + 3 * LANES] = shift_rows(value, 1).astype(BF16)
+    entries, rows_of = [], []
+    for stack, group in zip(stacks, groups):
+        near = reach(group[0][1], outs)
+        part = jnp.dot(
+            stack[...], right[:, near[0] * width : (near[-1] + 1) * width], preferred_element_type=F32
+        )
+        for k, entry in enumerate(group):
+            entries.append(entry)
+            rows_of.append({
+                j: part[k * LANES : (k + 1) * LANES, (j - near[0]) * width : (j - near[0] + 1) * width] for j in near
+            })
     quarter = half // 2
+    lane = lax.broadcasted_iota(jnp.int32, (quarter, LANES), 1)
+    packed[27 * quarter :] = jnp.zeros((packed.shape[0] - 27 * quarter, LANES), F32)
     for kind in ("own", "on", "off"):
         for step_z in range(3):
             for dy in range(3):
@@ -265,10 +311,7 @@
                 for k, (this, place) in enumerate(entries):
                     for j, out_place in enumerate(outs):
                         if this == kind and place - out_place + 1 == step_z:
-                            block = product[
-                                k * LANES : (k + 1) * LANES,
-                                dy * width + j * LANES : dy * width + (j + 1) * LANES,
-                            ]
+                            block = rows_of[k][j][:, dy * LANES : (dy + 1) * LANES]
                             total = block if total is None else total + block
                 direct = jnp.where(lane < half, total[:quarter], total[3 * quarter :])
                 turned = jnp.where(lane < half, total[quarter : 2 * quarter], total[2 * quarter : 3 * quarter])
@@ -302,42 +345,53 @@
     return [(i, (i - 1) % size if i % 2 == 0 else (i + 1) % size) for i in range(size)]
 
 
-def sum_over_mesh(keep, send, phases, slabs):
-    phase, slab = lax.axis_index("phase"), lax.axis_index("slab")
-    core, column, level = phase % 2, phase // 2 % 2, phase // 4
-    both = ("phase", "slab")
-    summed = keep + lax.ppermute(send, "phase", pair_on(phases))
-    groups = 2 * slabs
-    chunks = summed.reshape(groups, summed.shape[0] // groups, LANES)
-
-    def moves(dx, ds):
-        return [
-            (p * slabs + s, (p ^ (2 * dx)) * slabs + (s + ds) % slabs) for p in range(phases) for s in range(slabs)
-        ]
-
-    offsets = [(dx, ds) for dx in range(2) for ds in range(slabs) if (dx, ds) != (0, 0)]
-    place = lambda dx, ds: (column ^ dx) * slabs + (slab + ds) % slabs
-    part = lax.dynamic_index_in_dim(chunks, place(0, 0), 0, keepdims=False)
-    arrived = [
-        lax.ppermute(lax.dynamic_index_in_dim(chunks, place(dx, ds), 0, keepdims=False), both, moves(dx, ds))
-        for dx, ds in offsets
-    ]
-    for value in arrived:
-        part = part + value
-    levels = phases // 4
-    arrived = [
-        lax.ppermute(part, "phase", [(p, (p + 4 * k) % phases) for p in range(phases)]) for k in range(1, levels)
-    ]
-    for value in arrived:
-        part = part + value
-    part = part.astype(BF16)
-    pieces, where = [part], [place(0, 0)]
-    for dx, ds in offsets:
-        pieces.append(lax.ppermute(part, both, moves(dx, ds)))
-        where.append(place(dx, -ds))
-    other = [lax.ppermute(piece, "phase", pair_on(phases)) for piece in pieces]
-    spots = jnp.stack([core * groups + w for w in where] + [(1 - core) * groups + w for w in where])
-    return pieces + other, spots.astype(jnp.int32)
+def fold_body(pick_ref, keep_ref, got_ref, own_ref, send_ref):
+    rows = own_ref.shape[0]
+    for spot, out_ref in ((pick_ref[0], own_ref), (1 - pick_ref[0], send_ref)):
+        span = pl.ds(pl.multiple_of(spot * rows, rows), rows)
+        out_ref[...] = keep_ref[span, :] + got_ref[span, :]
+
+
+def round_body(value_ref, got_ref, out_ref):
+    out_ref[...] = (value_ref[...] + got_ref[...]).astype(out_ref.dtype)
+
+
+def exchanges(axis, stride, size, total):
+    return [(axis, [(i, i ^ (stride * bit)) for i in range(total)]) for bit in (1 << k for k in range(size.bit_length() - 1))]
+
+
+def sum_over_mesh(keep, send, phases, slabs, after_finish):
+    phase = lax.axis_index("phase")
+    core, column = phase % 2, phase // 2 % 2
+    part_shape = (keep.shape[0] // 2, LANES)
+    across = [(p, p ^ 2) for p in range(phases)]
+    part, other = call(
+        "fold",
+        fold_body,
+        [jax.ShapeDtypeStruct(part_shape, F32)] * 2,
+        (column.reshape(1), keep, lax.ppermute(send, "phase", pair_on(phases))),
+        "SVV",
+        nbytes=100000,
+    )
+    part = part + lax.ppermute(other, "phase", across)
+    steps = exchanges("slab", 1, slabs, slabs) + exchanges("phase", 4, phases // 4, phases)
+    for axis, perm in steps[:-1]:
+        part = part + lax.ppermute(part, axis, perm)
+    axis, perm = steps[-1]
+    part = call(
+        "finish",
+        round_body,
+        jax.ShapeDtypeStruct(part_shape, BF16),
+        (part, lax.ppermute(part, axis, perm)),
+        "VV",
+        nbytes=30000,
+        after=after_finish,
+    )
+    pieces = [part, lax.ppermute(part, "phase", across)]
+    pieces += [lax.ppermute(piece, "phase", pair_on(phases)) for piece in pieces]
+    spots = [2 * core + column, 2 * core + 1 - column]
+    spots += [2 * (1 - core) + column, 2 * (1 - core) + 1 - column]
+    return pieces, jnp.stack(spots).astype(jnp.int32)
 
 
 def local(phases, slabs, features, conv_weight, projection, grad_out, sens, mask):
@@ -364,25 +418,25 @@
         edges = [(depth_len - 1, -1, up), (0, depth_len, [(j, i) for i, j in up])]
         pick = lambda j: j
 
+    first_sent = [edge[0] for edge in edges]
+
     def halo(own):
         off_in = {}
-        for j in [edge[0] for edge in edges] + [j for j in order if all(j != edge[0] for edge in edges)]:
+        for j in first_sent + [j for j in order if j not in first_sent]:
             off_in[j] = pass_phase(own[j], off)
         slab_in = [lax.ppermute(own[edge[0]], "slab", edge[2]) for edge in edges]
         on_in = [pass_phase(own[j], on) for j in order]
         corner_off = [lax.ppermute(off_in[edge[0]], "slab", edge[2]) for edge in edges]
         corner_on = [pass_phase(value, on) for value in slab_in]
-        main = list(own) + slab_in + on_in + [off_in[j] for j in order]
         corners = []
         for a, b in zip(corner_off, corner_on):
             corners += [a, b]
-        return main, corners
+        full = list(own) + on_in + [off_in[j] for j in order]
+        ends = [list(values) for values in zip(slab_in, corner_off, corner_on)]
+        return full, full + slab_in, corners, ends
 
     main_entries = (
-        [("own", j) for j in order]
-        + [("own", edge[1]) for edge in edges]
-        + [("on", j) for j in order]
-        + [("off", j) for j in order]
+        [(kind, j) for kind in ("own", "on", "off") for j in order] + [("own", edge[1]) for edge in edges]
     )
     corner_entries = []
     corner_groups = []
@@ -392,118 +446,131 @@
         corner_entries += [("off", edge[1]), ("on", edge[1])]
     corner_groups.sort(key=lambda g: g[1])
 
-    own_features = [lax.dynamic_index_in_dim(features[0], pick(j), 0, keepdims=False) for j in order]
-    main_in, corner_in = halo(own_features)
-
     high, low = dft_packed(row_len)
     high, low = jnp.asarray(high), jnp.asarray(low)
     lines = depth_len * coils * col_len
     grad_now = grad_out[0]
     line_shape = (lines, 2 * row_len)
+    slice_shape = (row_len, packed_len)
+    slab_shape = (depth_len, row_len, packed_len)
     scratch = [pltpu.VMEM(line_shape, BF16)] * 2
     coil_flops = 3 * 2 * lines * (2 * row_len) ** 2
     own_lines, sent_lines = call(
+        "coil_forward",
         coil_forward_body,
-        (jax.ShapeDtypeStruct(line_shape, F32), jax.ShapeDtypeStruct(line_shape, BF16)),
-        4,
+        [jax.ShapeDtypeStruct(line_shape, F32), jax.ShapeDtypeStruct(line_shape, BF16)],
+        (grad_now, sens, high, low),
+        "VVVV",
         scratch=scratch,
         flops=coil_flops,
         nbytes=4000000,
-    )(grad_now, sens, high, low)
+    )
+    own_slices = [lax.dynamic_index_in_dim(features[0], pick(j), 0, keepdims=False) for j in order]
+    full_in, main_in, corner_in, ends_in = halo(own_slices)
     other_lines = [
         lax.ppermute(sent_lines, "slab", [(i, (i + k) % slabs) for i in range(slabs)]) for k in range(1, slabs)
     ]
+    spread = -(projection[:, None, None, :] * jnp.eye(col_len, dtype=BF16)[None, :, :, None])
+    spread = spread.reshape(2 * col_len, packed_len)
+    spread = jnp.concatenate([spread] * 3, axis=0)
+
+    bands = [pltpu.VMEM((len(g[0]) * LANES, 3 * LANES), BF16) for g in corner_groups]
+
+    conv_flops = 2 * row_len * len(main_entries) * packed_len * 3 * depth_len * LANES
+    small_flops = 2 * row_len * 2 * packed_len * 3 * LANES
+
+    def conv_main(name, back, inputs, after=()):
+        return call(
+            name,
+            functools.partial(conv_main_body, main_entries, flip, back),
+            jax.ShapeDtypeStruct(slab_shape, F32),
+            (scal, conv_weight, *inputs),
+            "SV" + "V" * len(inputs),
+            scratch=[pltpu.VMEM((len(main_entries) * LANES, 3 * depth_len * LANES), BF16)],
+            flops=conv_flops,
+            nbytes=5000000,
+            after=after,
+        )
+
+    def stack(name, inputs):
+        return call(
+            name,
+            stack_body,
+            pltpu.VMEM((len(inputs) * LANES, packed_len // LANES * row_len), BF16),
+            tuple(inputs),
+            "V" * len(inputs),
+            nbytes=5000000,
+        )
+
+    acc = conv_main("conv_act", False, main_in)
     grad_image = call(
+        "coil_back",
         functools.partial(coil_backward_body, slabs),
         jax.ShapeDtypeStruct(grad_now.shape, F32),
-        6 + len(other_lines),
+        (grad_now, sens, mask[0], high, low, own_lines, *other_lines),
+        "VVVVVV" + "V" * len(other_lines),
+        after=[acc],
         scratch=scratch,
         flops=coil_flops,
         nbytes=5000000,
-    )(grad_now, sens, mask[0], high, low, own_lines, *other_lines)
-
-    def two_columns(weight):
-        zero = jnp.zeros_like(weight)
-        return jnp.concatenate(
-            [jnp.concatenate([weight, zero], axis=2), jnp.concatenate([zero, weight], axis=2)], axis=1
-        )
-
-    weight_forward = two_columns(conv_weight)
-    weight_backward = two_columns(jnp.swapaxes(conv_weight[::-1], 1, 2))
-    spread = -(projection[:, None, None, :] * jnp.eye(col_len, dtype=BF16)[None, :, :, None])
-    spread = spread.reshape(2 * col_len, packed_len)
-    spread = jnp.concatenate([spread] * 3, axis=0)
-
-    slice_shape = (row_len, packed_len)
-    slab_shape = (depth_len, row_len, packed_len)
-    conv_flops = 2 * row_len * len(main_entries) * packed_len * 3 * depth_len * LANES
-    bands = [pltpu.VMEM((len(g[0]) * LANES, 3 * LANES), BF16) for g in corner_groups]
-    small_flops = 2 * row_len * 2 * packed_len * 3 * LANES
-
-    def conv_main(weight, inputs):
-        return call(
-            functools.partial(conv_main_body, main_entries, tuple(order), flip),
-            jax.ShapeDtypeStruct(slab_shape, F32),
-            1 + len(inputs),
-            1,
-            scratch=[pltpu.VMEM((len(inputs) * LANES, 3 * depth_len * LANES), BF16)],
-            flops=conv_flops,
-            nbytes=5000000,
-        )(scal, weight, *inputs)
-
-    def sorted_corners(values):
-        if flip:
-            return values
-        return values[:2] + values[2:]
-
-    acc = conv_main(weight_forward, main_in)
+    )
+
+    stack_full = stack("stack_full", full_in)
     grad_act = call(
+        "grad_act",
         functools.partial(grad_act_body, corner_groups, flip),
-        [jax.ShapeDtypeStruct(slice_shape, BF16)] * depth_len,
-        4 + len(corner_in),
-        1,
-        scratch=bands,
+        [pltpu.VMEM(slice_shape, BF16)] * depth_len,
+        (scal, acc, grad_image, spread, conv_weight, *corner_in),
+        "SVVVV" + "V" * len(corner_in),
         flops=small_flops,
         nbytes=4000000,
-    )(scal, weight_forward, acc, grad_image, spread, *sorted_corners(corner_in))
-
-    main_grad, corner_grad = halo(grad_act)
+        scratch=bands,
+        after=[stack_full],
+    )
+
+    _, main_grad, corner_grad, _ = halo(grad_act)
 
     share = (taps + 1) // 2 * channels // 2
+    stacks = [stack_full] + [stack("stack_end", values) for values in ends_in]
+    weight_groups = [[(kind, j) for kind in ("own", "on", "off") for j in order]]
+    weight_groups += [[(kind, edge[1]) for kind in ("own", "off", "on")] for edge in edges]
     keep, send = call(
-        functools.partial(grad_weight_body, main_entries + corner_entries, tuple(order), flip),
+        "grad_weight",
+        functools.partial(grad_weight_body, weight_groups, tuple(order), flip),
         [jax.ShapeDtypeStruct((share, LANES), F32)] * 2,
-        len(main_in) + len(corner_in) + depth_len,
-        1,
+        (scal, *stacks, *grad_act),
+        "S" + "M" * (len(stacks) + depth_len),
+        after=[],
         scratch=[
-            pltpu.VMEM((packed_len // LANES * row_len, (len(main_in) + len(corner_in)) * LANES), BF16),
             pltpu.VMEM((packed_len // LANES * row_len, 3 * depth_len * LANES), BF16),
             pltpu.VMEM((2 * share, LANES), F32),
         ],
         flops=conv_flops,
         nbytes=5000000,
-    )(scal, *main_in, *corner_in, *grad_act)
-    pieces, spots = sum_over_mesh(keep, send, phases, slabs)
-
-    acc_back = conv_main(weight_backward, main_grad)
+    )
+
+    acc_back = conv_main("conv_back", True, main_grad)
+    pieces, spots = sum_over_mesh(keep, send, phases, slabs, [acc_back])
+    grad_weight = call(
+        "unpack",
+        unpack_body,
+        jax.ShapeDtypeStruct(conv_weight.shape, F32),
+        (spots, *pieces),
+        "S" + "V" * len(pieces),
+        scratch=[pltpu.VMEM((len(pieces),) + pieces[0].shape, F32)],
+        nbytes=1000000,
+    )
     grad_features = call(
+        "grad_features",
         functools.partial(grad_feature_body, corner_groups, flip),
         jax.ShapeDtypeStruct(slab_shape, BF16),
-        2 + len(corner_grad),
-        1,
+        (scal, acc_back, conv_weight, *corner_grad),
+        "SVV" + "V" * len(corner_grad),
         scratch=bands,
         flops=small_flops,
         nbytes=4000000,
-    )(scal, weight_backward, acc_back, *sorted_corners(corner_grad))
-
-    grad_weight = call(
-        unpack_body,
-        jax.ShapeDtypeStruct(conv_weight.shape, F32),
-        len(pieces),
-        1,
-        scratch=[pltpu.VMEM((len(pieces),) + pieces[0].shape, F32)],
-        nbytes=1000000,
-    )(spots, *pieces)
+    )
+
     return (grad_image[None], grad_features[None], grad_weight)
 
 

time: 79.6 us -> 75.4 us (0.947)
  local copies, waits for them, and re-layouts: 8.2 us -> 5.3 us
  Pallas kernels: 20.3 us -> 22.8 us
  other arithmetic: 1.94 us -> 0.28 us
  waiting for transfers between devices: 17.3 us -> 15.9 us
  starting transfers between devices: 30.6 us -> 29.8 us
    ppermute x10, starting transfers between devices: 9.29 us -> 14.8 us  [pass_phase(): return lax.ppermute(value, 'phase', perm)]
    ppermute x1, waiting for transfers between devices: 4.67 us -> 0.01 us  [local(): lax.ppermute(sent_lines, 'slab', [(i, (i + k) % slabs) for i in range(sla...]
    ppermute x14 -> x8, starting transfers between devices: 13.6 us -> 9.47 us  [the longest x1 3.14 us: sum_over_mesh(): lax.ppermute(part, axis, perm)]
    ppermute x10, waiting for transfers between devices: 4.39 us -> 0.44 us  [pass_phase(): return lax.ppermute(value, 'phase', perm)]
    ppermute x2, waiting for transfers between devices: 0.01 us -> 3.87 us  [halo(): slab_in = [lax.ppermute(own[edge[0]], 'slab', edge[2]) for edge in edges]]
    ppermute x2, waiting for transfers between devices: 0.01 us -> 3.13 us  [halo(): lax.ppermute(off_in[edge[0]], 'slab', edge[2])]
    pallas_call x8 -> x12, Pallas kernels: 20.3 us -> 22.8 us  [call(): pl.pallas_call(run, out_shape=outs, in_specs=[SPECS[kind] for kind in kin...]
    unnamed x29 -> x26, local copies, waits for them, and re-layouts: 5.95 us -> 4.02 us
  transfers between devices with their start and end apart: 29 -> 23, of which waited for: 7 -> 10; matrix products, arithmetic and copies ran while one was open for 3% -> 1% of each run, Pallas kernels for 16% -> 21%
where the time goes in v1:
time: 75.4 us; the launch traced here: 75 us
  starting transfers between devices  29.8 us (40%)
  Pallas kernels  22.8 us (30%)
  waiting for transfers between devices  15.9 us (21%)
  local copies, waits for them, and re-layouts  5.3 us (7%)
  between operations  0.88 us (1%)
    pallas_call x12, Pallas kernels, call(): pl.pallas_call(run, out_shape=outs, in_specs=[SPECS[kind] for kind in kin...  22.8 us
    ppermute x10, starting transfers between devices, pass_phase(): return lax.ppermute(value, 'phase', perm)  14.8 us
    unnamed x26, local copies, waits for them, and re-layouts  4.02 us
    ppermute x2, waiting for transfers between devices, halo(): slab_in = [lax.ppermute(own[edge[0]], 'slab', edge[2]) for edge in edges]  3.87 us
    ppermute x1, starting transfers between devices, sum_over_mesh(): lax.ppermute(part, axis, perm)  3.14 us
    ppermute x2, waiting for transfers between devices, halo(): lax.ppermute(off_in[edge[0]], 'slab', edge[2])  3.13 us
    ppermute x2, starting transfers between devices, halo(): slab_in = [lax.ppermute(own[edge[0]], 'slab', edge[2]) for edge in edges]  3.04 us
    ppermute x1, starting transfers between devices, sum_over_mesh(): pieces = [part, lax.ppermute(part, 'phase', across)]  2.64 us
  transfers between devices with their start and end apart: 23, of which 10 were waited for; matrix products, arithmetic and copies ran while one was open for 1% of the time, Pallas kernels for 21%

profile of v1, /device:TPU:0, one launch (start us, length us, event | category | flops | bytes accessed | tf_op | source)
XLA Modules:
  0.0 75.0 jit_solution(13295147957365772981)
XLA Ops:
  0.6 0.0 copy-start
  0.7 1.2 %dynamic-slice_bitcast_fusion = (bf16[320,512]{1,0:T(8,128)(2,1)S(1)}, bf16[320,512]{1,0:T(8,128)(2,1)S(1)}) fusion(bf16[1,2,320,512]{3,2,1,0:T(8,128)(2,1)} %param.8, s32[]{:T(128)S(6)} %select_n.29, s32[]{:T(128)S(6)} %select_n.28), kind=kLoop, calls=%fused_computation | loop fusion | bytes 1310728 | tf_op jit(solution)/shard_map/jit(dynamic_index_in_dim)/squeeze | solution.py:468
  1.9 5.5 %collective-permute-start.4 = (bf16[320,512]{1,0:T(8,128)(2,1)S(1)}, bf16[320,512]{1,0:T(8,128)(2,1)}, u32[]{:S(2)}, u32[]{:S(2)}) collective-permute-start(bf16[320,512]{1,0:T(8,128)(2,1)S(1)} %get-tuple-element.19.refs_3_.refs_1_), channel_id=1, source_target_pairs={{0,30},{2,4},{4,2},{6,8},{8,6},{10,12},{12,10},{14,16},{16,14},{18... | collective-permute-start | bytes 983048 | tf_op jit(solution)/shard_map/ppermute | solution.py:409
  7.3 1.5 %collective-permute-start.5 = (bf16[320,512]{1,0:T(8,128)(2,1)S(1)}, bf16[320,512]{1,0:T(8,128)(2,1)}, u32[]{:S(2)}, u32[]{:S(2)}) collective-permute-start(bf16[320,512]{1,0:T(8,128)(2,1)S(1)} %get-tuple-element.19.refs_3_.refs_1_), channel_id=1, source_target_pairs={{0,1},{1,0},{2,3},{3,2},{4,5},{5,4},{6,7},{7,6},{8,9},{9,8},{10,11... | collective-permute-start | bytes 983048 | tf_op jit(solution)/shard_map/ppermute | solution.py:427
  8.9 0.5 collective-permute-start.1
  9.4 0.2 collective-permute-start.3
  9.6 0.1 multiply_negate_fusion
  9.7 0.1 neg.8
  9.8 1.1 %copy-done.1 = bf16[640,640]{1,0:T(8,128)(2,1)S(1)} copy-done((bf16[640,640]{1,0:T(8,128)(2,1)S(1)}, bf16[640,640]{1,0:T(8,128)(2,1)}, u32[]{:S(2)}) %copy-start.1) | copy-done | bytes 819224
  11.0 1.1 %copy-done.3 = f32[2,16,2,8,320]{4,3,2,1,0:T(8,128)S(1)} copy-done((f32[2,16,2,8,320]{4,3,2,1,0:T(8,128)S(1)}, f32[2,16,2,8,320]{4,3,2,1,0:T(8,128)}, u32[]{:S(2)}) %copy-start.3) | copy-done | bytes 655384
  12.1 1.8 %coil_forward.1 = (f32[256,640]{1,0:T(8,128)S(1)}, bf16[256,640]{1,0:T(8,128)(2,1)}) custom-call(f32[2,2,8,320]{3,2,1,0:T(8,128)S(1)} %bitcast.18, f32[2,16,2,8,320]{4,3,2,1,0:T(8,128)S(1)} %copy-done.3, bf16[640,640]{1,0:T(8,128)(2,1)S(1)} %copy-done, bf16[640,640]{1,0:T(8,128)(2,1)S(1)} %copy-done.1), custom_call_target="tpu_custom_call" | custom-call | flops 629145600 | bytes 4000000 | tf_op jit(solution)/shard_map/coil_forward/pallas_call | solution.py:31
  13.9 0.5 collective-permute-start
  14.4 0.3 collective-permute-done.5.refs_8_.refs_0_
  14.7 1.5 %collective-permute-start.6 = (bf16[320,512]{1,0:T(8,128)(2,1)}, bf16[320,512]{1,0:T(8,128)(2,1)S(1)}, u32[]{:S(2)}, u32[]{:S(2)}) collective-permute-start(bf16[320,512]{1,0:T(8,128)(2,1)} %collective-permute-done.4.refs_7_.refs_5_), channel_id=1, source_target_pairs={{0,1},{1,0},{2,3},{3,2},{4,5},{5,4},{6,7},{7,6},{8,9},{9,8},{10,11... | collective-permute-start | bytes 983048 | tf_op jit(solution)/shard_map/ppermute | solution.py:429
  16.2 0.7 copy-done.6
  17.0 1.3 %collective-permute-start.7 = (bf16[320,512]{1,0:T(8,128)(2,1)}, bf16[320,512]{1,0:T(8,128)(2,1)S(1)}, u32[]{:S(2)}, u32[]{:S(2)}) collective-permute-start(bf16[320,512]{1,0:T(8,128)(2,1)} %collective-permute-done.5.refs_8_.refs_0_), channel_id=1, source_target_pairs={{0,2},{2,0},{4,6},{6,4},{8,10},{10,8},{12,14},{14,12},{16,18},{18,... | collective-permute-start | bytes 983048 | tf_op jit(solution)/shard_map/ppermute | solution.py:409
  18.3 0.1 pad_add_fusion.refs_0_
  18.4 0.4 collective-permute-done.3.refs_6_.refs_4_
  18.8 1.0 %copy-done.7 = bf16[320,512]{1,0:T(8,128)(2,1)S(1)} copy-done((bf16[320,512]{1,0:T(8,128)(2,1)S(1)}, bf16[320,512]{1,0:T(8,128)(2,1)}, u32[]{:S(2)}) %copy-start.7) | copy-done | bytes 327704
  19.8 1.8 %stack_full.1.refs_7_.refs_1_ = bf16[768,1280]{1,0:T(8,128)(2,1)S(1)} custom-call(bf16[320,512]{1,0:T(8,128)(2,1)S(1)} %get-tuple-element.20.refs_2_.refs_0_, bf16[320,512]{1,0:T(8,128)(2,1)S(1)} %get-tuple-element.19.refs_3_.refs_1_, bf16[320,512]{1,0:T(8,128)(2,1)} %collective-permute-done.1.refs_4_.refs_2_, bf16[320,512]{1,0:T(8,128)(2,1)S(1)} %copy-done.7, ...), custom_call_target="tpu_custom_call" | custom-call | bytes 5000000 | tf_op jit(solution)/shard_map/stack_full/pallas_call | solution.py:31
  21.6 3.7 %conv_act.1.refs_7_.refs_1_ = f32[2,320,512]{2,1,0:T(8,128)S(1)} custom-call(s32[2]{0:T(128)S(1)} %pad_add_fusion.refs_0_, bf16[27,64,64]{2,1,0:T(8,128)(2,1)S(1)} %copy-done.5, bf16[320,512]{1,0:T(8,128)(2,1)S(1)} %get-tuple-element.20.refs_2_.refs_0_, bf16[320,512]{1,0:T(8,128)(2,1)S(1)} %get-tuple-element.19.refs_3_.refs_1_, ...), custom_call_target="tpu_custom_call" | custom-call | flops 1761607680 | bytes 5000000 | tf_op jit(solution)/shard_map/conv_act/pallas_call | solution.py:31
  25.4 2.1 %coil_back.1.refs_2_ = f32[2,2,8,320]{3,2,1,0:T(8,128)} custom-call(f32[2,2,8,320]{3,2,1,0:T(8,128)S(1)} %bitcast.19, f32[2,16,2,8,320]{4,3,2,1,0:T(8,128)S(1)} %copy-done.4, s32[4,320]{1,0:T(4,128)S(1)} %bitcast.20, bf16[640,640]{1,0:T(8,128)(2,1)S(1)} %copy-done, bf16[640,640]{1,0:T(8,128)(2,1)S(1)} %copy-done.2, ...), custom_call_target="tpu_custom_call" | custom-call | flops 629145600 | bytes 5000000 | tf_op jit(solution)/shard_map/coil_back/pallas_call | solution.py:31
  27.5 3.1 %collective-permute-done.6.refs_5_.refs_1_ = bf16[320,512]{1,0:T(8,128)(2,1)S(1)} collective-permute-done((bf16[320,512]{1,0:T(8,128)(2,1)}, bf16[320,512]{1,0:T(8,128)(2,1)S(1)}, u32[]{:S(2)}, u32[]{:S(2)}) %collective-permute-start.6) | collective-permute-done | bytes 327712 | tf_op jit(solution)/shard_map/ppermute | solution.py:429
  30.6 1.3 %stack_end.1.refs_2_ = bf16[384,1280]{1,0:T(8,128)(2,1)S(1)} custom-call(bf16[320,512]{1,0:T(8,128)(2,1)} %collective-permute-done.5.refs_8_.refs_0_, bf16[320,512]{1,0:T(8,128)(2,1)S(1)} %collective-permute-done.6.refs_5_.refs_1_, bf16[320,512]{1,0:T(8,128)(2,1)S(1)} %collective-permute-done.7.refs_6_.refs_2_), custom_call_target="tpu_custom_call" | custom-call | bytes 5000000 | tf_op jit(solution)/shard_map/stack_end/pallas_call | solution.py:31
  31.9 1.4 %grad_act.1 = (bf16[320,512]{1,0:T(8,128)(2,1)S(1)}, bf16[320,512]{1,0:T(8,128)(2,1)S(1)}) custom-call(s32[2]{0:T(128)S(1)} %pad_add_fusion.refs_0_, f32[2,320,512]{2,1,0:T(8,128)S(1)} %conv_act.1.refs_7_.refs_1_, f32[2,2,8,320]{3,2,1,0:T(8,128)S(1)} %copy-done.9, bf16[48,512]{1,0:T(8,128)(2,1)S(1)} %pad_maximum_fusion.refs_3_, ...), custom_call_target="tpu_custom_call" | custom-call | flops 251658240 | bytes 4000000 | tf_op jit(solution)/shard_map/grad_act/pallas_call | solution.py:31
  33.3 3.1 %grad_weight.1 = (f32[448,128]{1,0:T(8,128)S(1)}, f32[448,128]{1,0:T(8,128)S(1)}) custom-call(s32[2]{0:T(128)S(1)} %pad_add_fusion.refs_0_, bf16[768,1280]{1,0:T(8,128)(2,1)S(1)} %stack_full.1.refs_7_.refs_1_, bf16[384,1280]{1,0:T(8,128)(2,1)S(1)} %stack_end.1.refs_2_, bf16[320,512]{1,0:T(8,128)(2,1)S(1)} %get-tuple-element.13.refs_2_.refs_3_, ...), custom_call_target="tpu_custom_call" | custom-call | flops 1761607680 | bytes 5000000 | tf_op jit(solution)/shard_map/grad_weight/pallas_call | solution.py:31
  36.4 1.0 %collective-permute-start.15 = (f32[448,128]{1,0:T(8,128)S(1)}, f32[448,128]{1,0:T(8,128)S(1)}, u32[]{:S(2)}, u32[]{:S(2)}) collective-permute-start(f32[448,128]{1,0:T(8,128)S(1)} %get-tuple-element.16), channel_id=1, source_target_pairs={{0,2},{2,0},{4,6},{6,4},{8,10},{10,8},{12,14},{14,12},{16,18},{18,... | collective-permute-start | bytes 688136 | tf_op jit(solution)/shard_map/ppermute | solution.py:372
  37.4 1.1 %collective-permute-done.15.refs_2_ = f32[448,128]{1,0:T(8,128)S(1)} collective-permute-done((f32[448,128]{1,0:T(8,128)S(1)}, f32[448,128]{1,0:T(8,128)S(1)}, u32[]{:S(2)}, u32[]{:S(2)}) %collective-permute-start.15) | collective-permute-done | bytes 229408 | tf_op jit(solution)/shard_map/ppermute | solution.py:372
  38.6 0.1 collective-permute-start.16
  38.6 4.0 %collective-permute-start.11 = (bf16[320,512]{1,0:T(8,128)(2,1)S(1)}, bf16[320,512]{1,0:T(8,128)(2,1)}, u32[]{:S(2)}, u32[]{:S(2)}) collective-permute-start(bf16[320,512]{1,0:T(8,128)(2,1)S(1)} %get-tuple-element.14.refs_3_.refs_4_), channel_id=1, source_target_pairs={{0,30},{2,4},{4,2},{6,8},{8,6},{10,12},{12,10},{14,16},{16,14},{18... | collective-permute-start | bytes 983048 | tf_op jit(solution)/shard_map/ppermute | solution.py:409
  42.6 1.4 %collective-permute-done.16 = f32[224,128]{1,0:T(8,128)S(1)} collective-permute-done((f32[224,128]{1,0:T(8,128)S(1)}, f32[224,128]{1,0:T(8,128)S(1)}, u32[]{:S(2)}, u32[]{:S(2)}) %collective-permute-start.16) | collective-permute-done | bytes 114720 | tf_op jit(solution)/shard_map/ppermute | solution.py:376
  44.1 0.6 collective-permute-start.17
  44.6 1.5 %collective-permute-start.12 = (bf16[320,512]{1,0:T(8,128)(2,1)S(1)}, bf16[320,512]{1,0:T(8,128)(2,1)}, u32[]{:S(2)}, u32[]{:S(2)}) collective-permute-start(bf16[320,512]{1,0:T(8,128)(2,1)S(1)} %get-tuple-element.14.refs_3_.refs_4_), channel_id=1, source_target_pairs={{0,1},{1,0},{2,3},{3,2},{4,5},{5,4},{6,7},{7,6},{8,9},{9,8},{10,11... | collective-permute-start | bytes 983048 | tf_op jit(solution)/shard_map/ppermute | solution.py:427
  46.2 2.3 %collective-permute-start.10 = (bf16[320,512]{1,0:T(8,128)(2,1)S(1)}, bf16[320,512]{1,0:T(8,128)(2,1)S(1)}, u32[]{:S(2)}, u32[]{:S(2)}) collective-permute-start(bf16[320,512]{1,0:T(8,128)(2,1)S(1)} %get-tuple-element.13.refs_2_.refs_3_), channel_id=1, source_target_pairs={{0,30},{2,4},{4,2},{6,8},{8,6},{10,12},{12,10},{14,16},{16,14},{18... | collective-permute-start | bytes 983048 | tf_op jit(solution)/shard_map/ppermute | solution.py:409
  48.5 0.9 %collective-permute-start.8 = (bf16[320,512]{1,0:T(8,128)(2,1)S(1)}, bf16[320,512]{1,0:T(8,128)(2,1)S(1)}, u32[]{:S(2)}, u32[]{:S(2)}) collective-permute-start(bf16[320,512]{1,0:T(8,128)(2,1)S(1)} %get-tuple-element.13.refs_2_.refs_3_), channel_id=1, source_target_pairs={{0,2},{2,0},{4,6},{6,4},{8,10},{10,8},{12,14},{14,12},{16,18},{18,... | collective-permute-start | bytes 983048 | tf_op jit(solution)/shard_map/ppermute | solution.py:409
  49.4 0.8 %collective-permute-done.17 = f32[224,128]{1,0:T(8,128)S(1)} collective-permute-done((f32[224,128]{1,0:T(8,128)S(1)}, f32[224,128]{1,0:T(8,128)S(1)}, u32[]{:S(2)}, u32[]{:S(2)}) %collective-permute-start.17) | collective-permute-done | bytes 114720 | tf_op jit(solution)/shard_map/ppermute | solution.py:379
  50.2 2.0 %collective-permute-start.18 = (f32[224,128]{1,0:T(8,128)S(1)}, f32[224,128]{1,0:T(8,128)S(1)}, u32[]{:S(2)}, u32[]{:S(2)}) collective-permute-start(f32[224,128]{1,0:T(8,128)S(1)} %add.40), channel_id=1, source_target_pairs={{0,8},{2,10},{4,12},{6,14},{8,0},{10,2},{12,4},{14,6},{16,24},{18,... | collective-permute-start | bytes 344072 | tf_op jit(solution)/shard_map/ppermute | solution.py:379
  52.3 3.6 %collective-permute-done.12.refs_8_ = bf16[320,512]{1,0:T(8,128)(2,1)} collective-permute-done((bf16[320,512]{1,0:T(8,128)(2,1)S(1)}, bf16[320,512]{1,0:T(8,128)(2,1)}, u32[]{:S(2)}, u32[]{:S(2)}) %collective-permute-start.12) | collective-permute-done | bytes 327712 | tf_op jit(solution)/shard_map/ppermute | solution.py:427
  55.9 0.5 collective-permute-start.13
  56.4 0.6 collective-permute-done.18
  57.0 3.1 %collective-permute-start.19 = (f32[224,128]{1,0:T(8,128)S(1)}, f32[224,128]{1,0:T(8,128)S(1)}, u32[]{:S(2)}, u32[]{:S(2)}) collective-permute-start(f32[224,128]{1,0:T(8,128)S(1)} %add.41.refs_0_), channel_id=1, source_target_pairs={{0,16},{2,18},{4,20},{6,22},{8,24},{10,26},{12,28},{14,30},{16,0},... | collective-permute-start | bytes 344072 | tf_op jit(solution)/shard_map/ppermute | solution.py:385
  60.1 3.9 %conv_back.1.refs_1_.refs_2_ = f32[2,320,512]{2,1,0:T(8,128)S(1)} custom-call(s32[2]{0:T(128)S(1)} %pad_add_fusion.refs_0_, bf16[27,64,64]{2,1,0:T(8,128)(2,1)S(1)} %copy-done.5, bf16[320,512]{1,0:T(8,128)(2,1)S(1)} %get-tuple-element.13.refs_2_.refs_3_, bf16[320,512]{1,0:T(8,128)(2,1)S(1)} %get-tuple-element.14.refs_3_.refs_4_, ...), custom_call_target="tpu_custom_call" | custom-call | flops 1761607680 | bytes 5000000 | tf_op jit(solution)/shard_map/conv_back/pallas_call | solution.py:31
  64.0 2.3 %collective-permute-done.19.refs_1_ = f32[224,128]{1,0:T(8,128)S(1)} collective-permute-done((f32[224,128]{1,0:T(8,128)S(1)}, f32[224,128]{1,0:T(8,128)S(1)}, u32[]{:S(2)}, u32[]{:S(2)}) %collective-permute-start.19) | collective-permute-done | bytes 114720 | tf_op jit(solution)/shard_map/ppermute | solution.py:385
  66.3 2.6 %collective-permute-start.20 = (bf16[224,128]{1,0:T(8,128)(2,1)S(1)}, bf16[224,128]{1,0:T(8,128)(2,1)S(1)}, u32[]{:S(2)}, u32[]{:S(2)}) collective-permute-start(bf16[224,128]{1,0:T(8,128)(2,1)S(1)} %finish.1.refs_1_), channel_id=1, source_target_pairs={{0,4},{2,6},{4,0},{6,2},{8,12},{10,14},{12,8},{14,10},{16,20},{18,... | collective-permute-start | bytes 172040 | tf_op jit(solution)/shard_map/ppermute | solution.py:390
  69.0 2.2 %collective-permute-done.20.refs_2_ = bf16[224,128]{1,0:T(8,128)(2,1)S(1)} collective-permute-done((bf16[224,128]{1,0:T(8,128)(2,1)S(1)}, bf16[224,128]{1,0:T(8,128)(2,1)S(1)}, u32[]{:S(2)}, u32[]{:S(2)}) %collective-permute-start.20) | collective-permute-done | bytes 57376 | tf_op jit(solution)/shard_map/ppermute | solution.py:390
  71.1 0.1 pad_add_fusion.1.refs_0_
  71.2 2.1 %grad_features.1 = bf16[2,320,512]{2,1,0:T(8,128)(2,1)} custom-call(s32[2]{0:T(128)S(1)} %pad_add_fusion.refs_0_, f32[2,320,512]{2,1,0:T(8,128)S(1)} %conv_back.1.refs_1_.refs_2_, bf16[27,64,64]{2,1,0:T(8,128)(2,1)S(1)} %copy-done.5, bf16[320,512]{1,0:T(8,128)(2,1)S(1)} %collective-permute-done.13.refs_3_, bf16[320,512]{1,0:T(8,128)(2,1)S(1)} %collective-permute-done.14.refs_4_), custom_call_target="tpu_custom_call" | custom-call | flops 251658240 | bytes 4000000 | tf_op jit(solution)/shard_map/grad_features/pallas_call | solution.py:31
  73.3 1.7 %unpack.1 = f32[27,64,64]{2,1,0:T(8,128)} custom-call(s32[4]{0:T(128)S(1)} %pad_add_fusion.1.refs_0_, bf16[224,128]{1,0:T(8,128)(2,1)S(1)} %finish.1.refs_1_, bf16[224,128]{1,0:T(8,128)(2,1)S(1)} %collective-permute-done.20.refs_2_, bf16[224,128]{1,0:T(8,128)(2,1)S(1)} %collective-permute-done.21.refs_3_, bf16[224,128]{1,0:T(8,128)(2,1)S(1)} %collective-permute-done.22.refs_4_), custom_call_target="tpu_custom_call" | custom-call | bytes 1000000 | tf_op jit(solution)/shard_map/unpack/pallas_call | solution.py:31
  (46 shorter events, 0.2 us)
Async XLA Ops:
  0.6 9.2 %copy-start = (bf16[640,640]{1,0:T(8,128)(2,1)S(1)}, bf16[640,640]{1,0:T(8,128)(2,1)}, u32[]{:S(2)}) copy-start(bf16[640,640]{1,0:T(8,128)(2,1)} %constant.54.clone.refs_2_.refs_3_) | copy-start | bytes 2457604
  0.6 9.0 %copy-start.12 = (bf16[2,64]{1,0:T(2,128)(2,1)S(1)}, bf16[2,64]{1,0:T(2,128)(2,1)}, u32[]{:S(2)}) copy-start(bf16[2,64]{1,0:T(2,128)(2,1)} %param.10) | copy-start | bytes 772
  0.7 9.2 %copy-start.10 = (f32[1,2,2,8,320]{4,3,2,1,0:T(8,128)S(1)}, f32[1,2,2,8,320]{4,3,2,1,0:T(8,128)}, u32[]{:S(2)}) copy-start(f32[1,2,2,8,320]{4,3,2,1,0:T(8,128)} %param.11) | copy-start | bytes 122884
  1.9 12.1 %collective-permute-start.4 = (bf16[320,512]{1,0:T(8,128)(2,1)S(1)}, bf16[320,512]{1,0:T(8,128)(2,1)}, u32[]{:S(2)}, u32[]{:S(2)}) collective-permute-start(bf16[320,512]{1,0:T(8,128)(2,1)S(1)} %get-tuple-element.19.refs_3_.refs_1_), channel_id=1, source_target_pairs={{0,30},{2,4},{4,2},{6,8},{8,6},{10,12},{12,10},{14,16},{16,14},{18... | collective-permute-start | bytes 983048 | tf_op jit(solution)/shard_map/ppermute | solution.py:409
  7.3 7.4 %collective-permute-start.5 = (bf16[320,512]{1,0:T(8,128)(2,1)S(1)}, bf16[320,512]{1,0:T(8,128)(2,1)}, u32[]{:S(2)}, u32[]{:S(2)}) collective-permute-start(bf16[320,512]{1,0:T(8,128)(2,1)S(1)} %get-tuple-element.19.refs_3_.refs_1_), channel_id=1, source_target_pairs={{0,1},{1,0},{2,3},{3,2},{4,5},{5,4},{6,7},{7,6},{8,9},{9,8},{10,11... | collective-permute-start | bytes 983048 | tf_op jit(solution)/shard_map/ppermute | solution.py:427
  8.9 7.4 %collective-permute-start.2 = (bf16[320,512]{1,0:T(8,128)(2,1)S(1)}, bf16[320,512]{1,0:T(8,128)(2,1)S(1)}, u32[]{:S(2)}, u32[]{:S(2)}) collective-permute-start(bf16[320,512]{1,0:T(8,128)(2,1)S(1)} %get-tuple-element.19.refs_3_.refs_1_), channel_id=1, source_target_pairs={{0,2},{2,0},{4,6},{6,4},{8,10},{10,8},{12,14},{14,12},{16,18},{18,... | collective-permute-start | bytes 983048 | tf_op jit(solution)/shard_map/ppermute | solution.py:409
  8.9 9.5 %collective-permute-start.1 = (bf16[320,512]{1,0:T(8,128)(2,1)S(1)}, bf16[320,512]{1,0:T(8,128)(2,1)}, u32[]{:S(2)}, u32[]{:S(2)}) collective-permute-start(bf16[320,512]{1,0:T(8,128)(2,1)S(1)} %get-tuple-element.20.refs_2_.refs_0_), channel_id=1, source_target_pairs={{0,2},{2,0},{4,6},{6,4},{8,10},{10,8},{12,14},{14,12},{16,18},{18,... | collective-permute-start | bytes 983048 | tf_op jit(solution)/shard_map/ppermute | solution.py:409
  9.4 9.4 %collective-permute-start.3 = (bf16[320,512]{1,0:T(8,128)(2,1)S(1)}, bf16[320,512]{1,0:T(8,128)(2,1)}, u32[]{:S(2)}, u32[]{:S(2)}) collective-permute-start(bf16[320,512]{1,0:T(8,128)(2,1)S(1)} %get-tuple-element.20.refs_2_.refs_0_), channel_id=1, source_target_pairs={{0,30},{2,4},{4,2},{6,8},{8,6},{10,12},{12,10},{14,16},{16,14},{18... | collective-permute-start | bytes 983048 | tf_op jit(solution)/shard_map/ppermute | solution.py:409
  9.8 1.1 %copy-start.1 = (bf16[640,640]{1,0:T(8,128)(2,1)S(1)}, bf16[640,640]{1,0:T(8,128)(2,1)}, u32[]{:S(2)}) copy-start(bf16[640,640]{1,0:T(8,128)(2,1)} %constant.55.clone.refs_3_.refs_4_) | copy-start | bytes 2457604
  11.0 1.1 %copy-start.3 = (f32[2,16,2,8,320]{4,3,2,1,0:T(8,128)S(1)}, f32[2,16,2,8,320]{4,3,2,1,0:T(8,128)}, u32[]{:S(2)}) copy-start(f32[2,16,2,8,320]{4,3,2,1,0:T(8,128)} %refs_1_.6) | copy-start | bytes 1966084
  13.9 11.4 %collective-permute-start = (bf16[256,640]{1,0:T(8,128)(2,1)}, bf16[256,640]{1,0:T(8,128)(2,1)S(1)}, u32[]{:S(2)}, u32[]{:S(2)}) collective-permute-start(bf16[256,640]{1,0:T(8,128)(2,1)} %get-tuple-element.12), channel_id=1, source_target_pairs={{0,1},{1,0},{2,3},{3,2},{4,5},{5,4},{6,7},{7,6},{8,9},{9,8},{10,11... | collective-permute-start | bytes 983048 | tf_op jit(solution)/shard_map/ppermute | solution.py:471
  14.7 15.9 %collective-permute-start.6 = (bf16[320,512]{1,0:T(8,128)(2,1)}, bf16[320,512]{1,0:T(8,128)(2,1)S(1)}, u32[]{:S(2)}, u32[]{:S(2)}) collective-permute-start(bf16[320,512]{1,0:T(8,128)(2,1)} %collective-permute-done.4.refs_7_.refs_5_), channel_id=1, source_target_pairs={{0,1},{1,0},{2,3},{3,2},{4,5},{5,4},{6,7},{7,6},{8,9},{9,8},{10,11... | collective-permute-start | bytes 983048 | tf_op jit(solution)/shard_map/ppermute | solution.py:429
  16.2 0.7 copy-start.6
  17.0 13.7 %collective-permute-start.7 = (bf16[320,512]{1,0:T(8,128)(2,1)}, bf16[320,512]{1,0:T(8,128)(2,1)S(1)}, u32[]{:S(2)}, u32[]{:S(2)}) collective-permute-start(bf16[320,512]{1,0:T(8,128)(2,1)} %collective-permute-done.5.refs_8_.refs_0_), channel_id=1, source_target_pairs={{0,2},{2,0},{4,6},{6,4},{8,10},{10,8},{12,14},{14,12},{16,18},{18,... | collective-permute-start | bytes 983048 | tf_op jit(solution)/shard_map/ppermute | solution.py:409
  18.4 3.2 %copy-start.5 = (bf16[27,64,64]{2,1,0:T(8,128)(2,1)S(1)}, bf16[27,64,64]{2,1,0:T(8,128)(2,1)}, u32[]{:S(2)}) copy-start(bf16[27,64,64]{2,1,0:T(8,128)(2,1)} %refs_2_.2) | copy-start | bytes 663556
  18.8 1.0 %copy-start.7 = (bf16[320,512]{1,0:T(8,128)(2,1)S(1)}, bf16[320,512]{1,0:T(8,128)(2,1)}, u32[]{:S(2)}) copy-start(bf16[320,512]{1,0:T(8,128)(2,1)} %copy-done.6) | copy-start | bytes 983044
  19.8 1.8 %copy-start.8 = (bf16[320,512]{1,0:T(8,128)(2,1)S(1)}, bf16[320,512]{1,0:T(8,128)(2,1)}, u32[]{:S(2)}) copy-start(bf16[320,512]{1,0:T(8,128)(2,1)} %copy-done.6) | copy-start | bytes 983044
  21.6 3.8 %copy-start.2 = (bf16[640,640]{1,0:T(8,128)(2,1)S(1)}, bf16[640,640]{1,0:T(8,128)(2,1)}, u32[]{:S(2)}) copy-start(bf16[640,640]{1,0:T(8,128)(2,1)} %constant.55.clone.refs_3_.refs_4_) | copy-start | bytes 2457604
  21.6 3.8 %copy-start.4 = (f32[2,16,2,8,320]{4,3,2,1,0:T(8,128)S(1)}, f32[2,16,2,8,320]{4,3,2,1,0:T(8,128)}, u32[]{:S(2)}) copy-start(f32[2,16,2,8,320]{4,3,2,1,0:T(8,128)} %refs_1_.6) | copy-start | bytes 1966084
  21.6 3.8 %copy-start.11 = (s32[1,4,320]{2,1,0:T(4,128)S(1)}, s32[1,4,320]{2,1,0:T(4,128)}, u32[]{:S(2)}) copy-start(s32[1,4,320]{2,1,0:T(4,128)} %param.13) | copy-start | bytes 15364
  27.5 4.4 %copy-start.9 = (f32[2,2,8,320]{3,2,1,0:T(8,128)S(1)}, f32[2,2,8,320]{3,2,1,0:T(8,128)}, u32[]{:S(2)}) copy-start(f32[2,2,8,320]{3,2,1,0:T(8,128)} %coil_back.1.refs_2_) | copy-start | bytes 122884
  36.4 2.1 %collective-permute-start.15 = (f32[448,128]{1,0:T(8,128)S(1)}, f32[448,128]{1,0:T(8,128)S(1)}, u32[]{:S(2)}, u32[]{:S(2)}) collective-permute-start(f32[448,128]{1,0:T(8,128)S(1)} %get-tuple-element.16), channel_id=1, source_target_pairs={{0,2},{2,0},{4,6},{6,4},{8,10},{10,8},{12,14},{14,12},{16,18},{18,... | collective-permute-start | bytes 688136 | tf_op jit(solution)/shard_map/ppermute | solution.py:372
  38.6 5.5 %collective-permute-start.16 = (f32[224,128]{1,0:T(8,128)S(1)}, f32[224,128]{1,0:T(8,128)S(1)}, u32[]{:S(2)}, u32[]{:S(2)}) collective-permute-start(f32[224,128]{1,0:T(8,128)S(1)} %get-tuple-element.18), channel_id=1, source_target_pairs={{0,4},{2,6},{4,0},{6,2},{8,12},{10,14},{12,8},{14,10},{16,20},{18,... | collective-permute-start | bytes 344072 | tf_op jit(solution)/shard_map/ppermute | solution.py:376
  38.6 11.6 %collective-permute-start.11 = (bf16[320,512]{1,0:T(8,128)(2,1)S(1)}, bf16[320,512]{1,0:T(8,128)(2,1)}, u32[]{:S(2)}, u32[]{:S(2)}) collective-permute-start(bf16[320,512]{1,0:T(8,128)(2,1)S(1)} %get-tuple-element.14.refs_3_.refs_4_), channel_id=1, source_target_pairs={{0,30},{2,4},{4,2},{6,8},{8,6},{10,12},{12,10},{14,16},{16,14},{18... | collective-permute-start | bytes 983048 | tf_op jit(solution)/shard_map/ppermute | solution.py:409
  44.1 6.1 %collective-permute-start.17 = (f32[224,128]{1,0:T(8,128)S(1)}, f32[224,128]{1,0:T(8,128)S(1)}, u32[]{:S(2)}, u32[]{:S(2)}) collective-permute-start(f32[224,128]{1,0:T(8,128)S(1)} %add.39), channel_id=1, source_target_pairs={{0,1},{1,0},{2,3},{3,2},{4,5},{5,4},{6,7},{7,6},{8,9},{9,8},{10,11... | collective-permute-start | bytes 344072 | tf_op jit(solution)/shard_map/ppermute | solution.py:379
  44.6 11.2 %collective-permute-start.12 = (bf16[320,512]{1,0:T(8,128)(2,1)S(1)}, bf16[320,512]{1,0:T(8,128)(2,1)}, u32[]{:S(2)}, u32[]{:S(2)}) collective-permute-start(bf16[320,512]{1,0:T(8,128)(2,1)S(1)} %get-tuple-element.14.refs_3_.refs_4_), channel_id=1, source_target_pairs={{0,1},{1,0},{2,3},{3,2},{4,5},{5,4},{6,7},{7,6},{8,9},{9,8},{10,11... | collective-permute-start | bytes 983048 | tf_op jit(solution)/shard_map/ppermute | solution.py:427
  46.2 10.8 %collective-permute-start.10 = (bf16[320,512]{1,0:T(8,128)(2,1)S(1)}, bf16[320,512]{1,0:T(8,128)(2,1)S(1)}, u32[]{:S(2)}, u32[]{:S(2)}) collective-permute-start(bf16[320,512]{1,0:T(8,128)(2,1)S(1)} %get-tuple-element.13.refs_2_.refs_3_), channel_id=1, source_target_pairs={{0,30},{2,4},{4,2},{6,8},{8,6},{10,12},{12,10},{14,16},{16,14},{18... | collective-permute-start | bytes 983048 | tf_op jit(solution)/shard_map/ppermute | solution.py:409
  48.5 11.7 %collective-permute-start.8 = (bf16[320,512]{1,0:T(8,128)(2,1)S(1)}, bf16[320,512]{1,0:T(8,128)(2,1)S(1)}, u32[]{:S(2)}, u32[]{:S(2)}) collective-permute-start(bf16[320,512]{1,0:T(8,128)(2,1)S(1)} %get-tuple-element.13.refs_2_.refs_3_), channel_id=1, source_target_pairs={{0,2},{2,0},{4,6},{6,4},{8,10},{10,8},{12,14},{14,12},{16,18},{18,... | collective-permute-start | bytes 983048 | tf_op jit(solution)/shard_map/ppermute | solution.py:409
  50.2 9.9 %collective-permute-start.9 = (bf16[320,512]{1,0:T(8,128)(2,1)S(1)}, bf16[320,512]{1,0:T(8,128)(2,1)S(1)}, u32[]{:S(2)}, u32[]{:S(2)}) collective-permute-start(bf16[320,512]{1,0:T(8,128)(2,1)S(1)} %get-tuple-element.14.refs_3_.refs_4_), channel_id=1, source_target_pairs={{0,2},{2,0},{4,6},{6,4},{8,10},{10,8},{12,14},{14,12},{16,18},{18,... | collective-permute-start | bytes 983048 | tf_op jit(solution)/shard_map/ppermute | solution.py:409
  50.2 6.7 %collective-permute-start.18 = (f32[224,128]{1,0:T(8,128)S(1)}, f32[224,128]{1,0:T(8,128)S(1)}, u32[]{:S(2)}, u32[]{:S(2)}) collective-permute-start(f32[224,128]{1,0:T(8,128)S(1)} %add.40), channel_id=1, source_target_pairs={{0,8},{2,10},{4,12},{6,14},{8,0},{10,2},{12,4},{14,6},{16,24},{18,... | collective-permute-start | bytes 344072 | tf_op jit(solution)/shard_map/ppermute | solution.py:379
  55.9 15.3 %collective-permute-start.13 = (bf16[320,512]{1,0:T(8,128)(2,1)}, bf16[320,512]{1,0:T(8,128)(2,1)S(1)}, u32[]{:S(2)}, u32[]{:S(2)}) collective-permute-start(bf16[320,512]{1,0:T(8,128)(2,1)} %collective-permute-done.11.refs_7_), channel_id=1, source_target_pairs={{0,1},{1,0},{2,3},{3,2},{4,5},{5,4},{6,7},{7,6},{8,9},{9,8},{10,11... | collective-permute-start | bytes 983048 | tf_op jit(solution)/shard_map/ppermute | solution.py:429
  57.0 14.3 %collective-permute-start.14 = (bf16[320,512]{1,0:T(8,128)(2,1)}, bf16[320,512]{1,0:T(8,128)(2,1)S(1)}, u32[]{:S(2)}, u32[]{:S(2)}) collective-permute-start(bf16[320,512]{1,0:T(8,128)(2,1)} %collective-permute-done.12.refs_8_), channel_id=1, source_target_pairs={{0,2},{2,0},{4,6},{6,4},{8,10},{10,8},{12,14},{14,12},{16,18},{18,... | collective-permute-start | bytes 983048 | tf_op jit(solution)/shard_map/ppermute | solution.py:409
  57.0 9.3 %collective-permute-start.19 = (f32[224,128]{1,0:T(8,128)S(1)}, f32[224,128]{1,0:T(8,128)S(1)}, u32[]{:S(2)}, u32[]{:S(2)}) collective-permute-start(f32[224,128]{1,0:T(8,128)S(1)} %add.41.refs_0_), channel_id=1, source_target_pairs={{0,16},{2,18},{4,20},{6,22},{8,24},{10,26},{12,28},{14,30},{16,0},... | collective-permute-start | bytes 344072 | tf_op jit(solution)/shard_map/ppermute | solution.py:385
  66.3 4.8 %collective-permute-start.20 = (bf16[224,128]{1,0:T(8,128)(2,1)S(1)}, bf16[224,128]{1,0:T(8,128)(2,1)S(1)}, u32[]{:S(2)}, u32[]{:S(2)}) collective-permute-start(bf16[224,128]{1,0:T(8,128)(2,1)S(1)} %finish.1.refs_1_), channel_id=1, source_target_pairs={{0,4},{2,6},{4,0},{6,2},{8,12},{10,14},{12,8},{14,10},{16,20},{18,... | collective-permute-start | bytes 172040 | tf_op jit(solution)/shard_map/ppermute | solution.py:390
  69.0 4.3 %collective-permute-start.21 = (bf16[224,128]{1,0:T(8,128)(2,1)S(1)}, bf16[224,128]{1,0:T(8,128)(2,1)S(1)}, u32[]{:S(2)}, u32[]{:S(2)}) collective-permute-start(bf16[224,128]{1,0:T(8,128)(2,1)S(1)} %finish.1.refs_1_), channel_id=1, source_target_pairs={{0,2},{2,0},{4,6},{6,4},{8,10},{10,8},{12,14},{14,12},{16,18},{18,... | collective-permute-start | bytes 172040 | tf_op jit(solution)/shard_map/ppermute | solution.py:391
  71.1 2.2 %collective-permute-start.22 = (bf16[224,128]{1,0:T(8,128)(2,1)S(1)}, bf16[224,128]{1,0:T(8,128)(2,1)S(1)}, u32[]{:S(2)}, u32[]{:S(2)}) collective-permute-start(bf16[224,128]{1,0:T(8,128)(2,1)S(1)} %collective-permute-done.20.refs_2_), channel_id=1, source_target_pairs={{0,2},{2,0},{4,6},{6,4},{8,10},{10,8},{12,14},{14,12},{16,18},{18,... | collective-permute-start | bytes 172040 | tf_op jit(solution)/shard_map/ppermute | solution.py:391

commit v2 on v1

--- a/solution.py
+++ b/solution.py
@@ -18,7 +18,7 @@
 
 
 ANY = pl.BlockSpec(memory_space=pl.ANY)
-SPECS = {"S": SMEM, "V": VMEM, "M": VMEM}
+SPECS = {"S": SMEM, "V": VMEM, "M": VMEM, "H": VMEM}
 
 
 def call(name, body, outs, ins, kinds, scratch=(), flops=0, nbytes=0, after=()):
@@ -27,7 +27,10 @@
     def run(*refs):
         body(*refs[:count], *refs[count + waits :])
 
-    ins = [pltpu.with_memory_space_constraint(x, pltpu.VMEM) if kind == "M" else x for x, kind in zip(ins, kinds)]
+    spaces = {"M": pltpu.VMEM, "H": pltpu.HBM}
+    ins = [
+        pltpu.with_memory_space_constraint(x, spaces[kind]) if kind in spaces else x for x, kind in zip(ins, kinds)
+    ]
     return pl.pallas_call(
         run,
         out_shape=outs,
@@ -173,15 +176,18 @@
 
 def fill_band(scal_ref, weight_ref, band, entries, outs, flip, back):
     width = LANES * len(outs)
+    made = {}
     for i, (kind, place) in enumerate(entries):
         for j, out_place in enumerate(outs):
             step_z = place - out_place + 1
             for dy in range(3):
                 lanes = slice(dy * width + j * LANES, dy * width + (j + 1) * LANES)
                 if 0 <= step_z <= 2:
-                    tap = tap_group(scal_ref, kind, flip, step_z) + dy
-                    weight = weight_ref[weight_ref.shape[0] - 1 - tap if back else tap].astype(F32)
-                    block = two_columns(weight.T if back else weight)
+                    if (kind, step_z, dy) not in made:
+                        tap = tap_group(scal_ref, kind, flip, step_z) + dy
+                        weight = weight_ref[weight_ref.shape[0] - 1 - tap if back else tap].astype(F32)
+                        made[kind, step_z, dy] = two_columns(weight.T if back else weight)
+                    block = made[kind, step_z, dy]
                 else:
                     block = jnp.zeros((LANES, LANES), BF16)
                 band[i * LANES : (i + 1) * LANES, lanes] = block
@@ -222,10 +228,22 @@
     return plans
 
 
+def stack_body(*refs):
+    inputs, out_ref = refs[:-1], refs[-1]
+    rows, packed_len = inputs[0].shape
+    for i, start in enumerate(range(0, packed_len, 2 * LANES)):
+        for k, ref in enumerate(inputs):
+            pair = jnp.concatenate([ref[:, start : start + LANES], ref[:, start + LANES : start + 2 * LANES]], axis=0)
+            value = pair.astype(F32).T
+            out_ref[k * LANES : (k + 1) * LANES, 2 * rows * i : 2 * rows * (i + 1)] = value.astype(BF16)
+
+
 def grad_act_body(groups, flip, scal_ref, acc_ref, image_ref, spread_ref, weight_ref, *refs):
-    depth_len = acc_ref.shape[0]
-    inputs, refs = refs[: 2 * len(groups)], refs[2 * len(groups) :]
-    outs, bands = refs[:depth_len], refs[depth_len:]
+    depth_len, count = acc_ref.shape[0], len(groups)
+    slab_in, inputs, refs = refs[:count], refs[count : 3 * count], refs[3 * count :]
+    outs, ends, bands = refs[:depth_len], refs[depth_len : depth_len + count], refs[depth_len + count :]
+    for k, end in enumerate(ends):
+        stack_body(slab_in[k], *inputs[2 * k : 2 * k + 2], end)
     plans = corner_plans(groups, flip, False, scal_ref, weight_ref, inputs, bands)
     row_len = image_ref.shape[3]
     for j in range(depth_len):
@@ -258,16 +276,6 @@
             if j in plans:
                 total = total + conv_columns(*plans[j], lanes)
             out_ref[place, :, lanes] = total.astype(BF16)
-
-
-def stack_body(*refs):
-    inputs, out_ref = refs[:-1], refs[-1]
-    rows, packed_len = inputs[0].shape
-    for i, start in enumerate(range(0, packed_len, 2 * LANES)):
-        for k, ref in enumerate(inputs):
-            pair = jnp.concatenate([ref[:, start : start + LANES], ref[:, start + LANES : start + 2 * LANES]], axis=0)
-            value = pair.astype(F32).T
-            out_ref[k * LANES : (k + 1) * LANES, 2 * rows * i : 2 * rows * (i + 1)] = value.astype(BF16)
 
 
 def reach(place, outs):
@@ -337,6 +345,14 @@
         out_ref[tap, quarter:, :] = pltpu.roll(block, LANES // 2, 1)[:, : LANES // 2]
 
 
+def final_body(groups, flip, scal_ref, acc_ref, weight_ref, *refs):
+    corners, count = refs[: 2 * len(groups)], 2 * len(groups)
+    where_ref, pieces = refs[count], refs[count + 1 : count + 5]
+    features_ref, taps_ref, packed, bands = refs[count + 5], refs[count + 6], refs[-1], refs[count + 7 : -1]
+    unpack_body(where_ref, *pieces, taps_ref, packed)
+    grad_feature_body(groups, flip, scal_ref, acc_ref, weight_ref, *corners, features_ref, *bands)
+
+
 def pair_on(size):
     return [(i, i ^ 1) for i in range(size)]
 
@@ -460,7 +476,7 @@
         coil_forward_body,
         [jax.ShapeDtypeStruct(line_shape, F32), jax.ShapeDtypeStruct(line_shape, BF16)],
         (grad_now, sens, high, low),
-        "VVVV",
+        "VHHH",
         scratch=scratch,
         flops=coil_flops,
         nbytes=4000000,
@@ -496,7 +512,7 @@
         return call(
             name,
             stack_body,
-            pltpu.VMEM((len(inputs) * LANES, packed_len // LANES * row_len), BF16),
+            jax.ShapeDtypeStruct((len(inputs) * LANES, packed_len // LANES * row_len), BF16),
             tuple(inputs),
             "V" * len(inputs),
             nbytes=5000000,
@@ -516,22 +532,24 @@
     )
 
     stack_full = stack("stack_full", full_in)
-    grad_act = call(
+    grad_outs = call(
         "grad_act",
         functools.partial(grad_act_body, corner_groups, flip),
-        [pltpu.VMEM(slice_shape, BF16)] * depth_len,
-        (scal, acc, grad_image, spread, conv_weight, *corner_in),
-        "SVVVV" + "V" * len(corner_in),
+        [pltpu.VMEM(slice_shape, BF16)] * depth_len
+        + [pltpu.VMEM((3 * LANES, packed_len // LANES * row_len), BF16)] * len(edges),
+        (scal, acc, grad_image, spread, conv_weight, *[values[0] for values in ends_in], *corner_in),
+        "SVHVV" + "V" * (len(edges) + len(corner_in)),
         flops=small_flops,
         nbytes=4000000,
         scratch=bands,
         after=[stack_full],
     )
 
+    grad_act, stack_ends = grad_outs[:depth_len], grad_outs[depth_len:]
     _, main_grad, corner_grad, _ = halo(grad_act)
 
     share = (taps + 1) // 2 * channels // 2
-    stacks = [stack_full] + [stack("stack_end", values) for values in ends_in]
+    stacks = [stack_full, *stack_ends]
     weight_groups = [[(kind, j) for kind in ("own", "on", "off") for j in order]]
     weight_groups += [[(kind, edge[1]) for kind in ("own", "off", "on")] for edge in edges]
     keep, send = call(
@@ -539,7 +557,7 @@
         functools.partial(grad_weight_body, weight_groups, tuple(order), flip),
         [jax.ShapeDtypeStruct((share, LANES), F32)] * 2,
         (scal, *stacks, *grad_act),
-        "S" + "M" * (len(stacks) + depth_len),
+        "SV" + "M" * (len(stacks) - 1 + depth_len),
         after=[],
         scratch=[
             pltpu.VMEM((packed_len // LANES * row_len, 3 * depth_len * LANES), BF16),
@@ -551,26 +569,16 @@
 
     acc_back = conv_main("conv_back", True, main_grad)
     pieces, spots = sum_over_mesh(keep, send, phases, slabs, [acc_back])
-    grad_weight = call(
-        "unpack",
-        unpack_body,
-        jax.ShapeDtypeStruct(conv_weight.shape, F32),
-        (spots, *pieces),
-        "S" + "V" * len(pieces),
-        scratch=[pltpu.VMEM((len(pieces),) + pieces[0].shape, F32)],
-        nbytes=1000000,
-    )
-    grad_features = call(
-        "grad_features",
-        functools.partial(grad_feature_body, corner_groups, flip),
-        jax.ShapeDtypeStruct(slab_shape, BF16),
-        (scal, acc_back, conv_weight, *corner_grad),
-        "SVV" + "V" * len(corner_grad),
-        scratch=bands,
+    grad_features, grad_weight = call(
+        "finish_both",
+        functools.partial(final_body, corner_groups, flip),
+        [jax.ShapeDtypeStruct(slab_shape, BF16), jax.ShapeDtypeStruct(conv_weight.shape, F32)],
+        (scal, acc_back, conv_weight, *corner_grad, spots, *pieces),
+        "SVV" + "V" * len(corner_grad) + "S" + "V" * len(pieces),
+        scratch=bands + [pltpu.VMEM((len(pieces),) + pieces[0].shape, F32)],
         flops=small_flops,
         nbytes=4000000,
     )
-
     return (grad_image[None], grad_features[None], grad_weight)
 
 

time: 75.4 us -> 73.4 us (0.973)
  local copies, waits for them, and re-layouts: 5.3 us -> 2.55 us
  Pallas kernels: 22.8 us -> 21.4 us
  starting transfers between devices: 29.8 us -> 31 us
  waiting for transfers between devices: 15.9 us -> 17 us
    unnamed x26 -> x18, local copies, waits for them, and re-layouts: 4.02 us -> 1.33 us
    ppermute x2, starting transfers between devices: 2.59 us -> 4.14 us  [sum_over_mesh(): part = part + lax.ppermute(part, axis, perm)]
    ppermute x2, starting transfers between devices: 3.04 us -> 1.6 us  [halo(): slab_in = [lax.ppermute(own[edge[0]], 'slab', edge[2]) for edge in edges]]
    pallas_call x12 -> x10, Pallas kernels: 22.8 us -> 21.4 us  [call(): pl.pallas_call(run, out_shape=outs, in_specs=[SPECS[kind] for kind in kin...]
    ppermute x2, waiting for transfers between devices: 3.13 us -> 1.96 us  [halo(): lax.ppermute(off_in[edge[0]], 'slab', edge[2])]
    ppermute x2, waiting for transfers between devices: 0.01 us -> 1.15 us  [sum_over_mesh(): lax.ppermute(piece, 'phase', pair_on(phases))]
  transfers between devices with their start and end apart: 23 -> 23, of which waited for: 10 -> 11; matrix products, arithmetic and copies ran while one was open for 1% -> 1% of each run, Pallas kernels for 21% -> 19%
where the time goes in v2:
time: 73.4 us; the launch traced here: 73.1 us
  starting transfers between devices  31 us (42%)
  Pallas kernels  21.4 us (29%)
  waiting for transfers between devices  17 us (23%)
  local copies, waits for them, and re-layouts  2.55 us (3%)
  between operations  0.84 us (1%)
    pallas_call x10, Pallas kernels, call(): pl.pallas_call(run, out_shape=outs, in_specs=[SPECS[kind] for kind in kin...  21.4 us
    ppermute x10, starting transfers between devices, pass_phase(): return lax.ppermute(value, 'phase', perm)  14.3 us
    ppermute x2, starting transfers between devices, sum_over_mesh(): part = part + lax.ppermute(part, axis, perm)  4.14 us
    ppermute x2, waiting for transfers between devices, halo(): slab_in = [lax.ppermute(own[edge[0]], 'slab', edge[2]) for edge in edges]  3.96 us
    ppermute x1, starting transfers between devices, sum_over_mesh(): lax.ppermute(part, axis, perm)  3.1 us
    ppermute x1, waiting for transfers between devices, sum_over_mesh(): lax.ppermute(part, axis, perm)  2.64 us
    ppermute x1, starting transfers between devices, sum_over_mesh(): pieces = [part, lax.ppermute(part, 'phase', across)]  2.52 us
    ppermute x2, starting transfers between devices, halo(): lax.ppermute(off_in[edge[0]], 'slab', edge[2])  2.45 us
  transfers between devices with their start and end apart: 23, of which 11 were waited for; matrix products, arithmetic and copies ran while one was open for 1% of the time, Pallas kernels for 19%

profile of v2, /device:TPU:0, one launch (start us, length us, event | category | flops | bytes accessed | tf_op | source)
XLA Modules:
  0.0 73.1 jit_solution(11832692973332902101)
XLA Ops:
  0.7 1.1 %dynamic-slice_bitcast_fusion = (bf16[320,512]{1,0:T(8,128)(2,1)S(1)}, bf16[320,512]{1,0:T(8,128)(2,1)S(1)}) fusion(bf16[1,2,320,512]{3,2,1,0:T(8,128)(2,1)} %param.8, s32[]{:T(128)S(6)} %select_n.29, s32[]{:T(128)S(6)} %select_n.28), kind=kLoop, calls=%fused_computation | loop fusion | bytes 1310728 | tf_op jit(solution)/shard_map/jit(dynamic_index_in_dim)/squeeze | solution.py:484
  1.8 5.5 %collective-permute-start.4 = (bf16[320,512]{1,0:T(8,128)(2,1)S(1)}, bf16[320,512]{1,0:T(8,128)(2,1)S(1)}, u32[]{:S(2)}, u32[]{:S(2)}) collective-permute-start(bf16[320,512]{1,0:T(8,128)(2,1)S(1)} %get-tuple-element.25.refs_3_.refs_1_), channel_id=1, source_target_pairs={{0,30},{2,4},{4,2},{6,8},{8,6},{10,12},{12,10},{14,16},{16,14},{18... | collective-permute-start | bytes 983048 | tf_op jit(solution)/shard_map/ppermute | solution.py:425
  7.3 1.5 %collective-permute-start.5 = (bf16[320,512]{1,0:T(8,128)(2,1)S(1)}, bf16[320,512]{1,0:T(8,128)(2,1)S(1)}, u32[]{:S(2)}, u32[]{:S(2)}) collective-permute-start(bf16[320,512]{1,0:T(8,128)(2,1)S(1)} %get-tuple-element.25.refs_3_.refs_1_), channel_id=1, source_target_pairs={{0,1},{1,0},{2,3},{3,2},{4,5},{5,4},{6,7},{7,6},{8,9},{9,8},{10,11... | collective-permute-start | bytes 983048 | tf_op jit(solution)/shard_map/ppermute | solution.py:443
  8.8 0.0 collective-permute-start.2
  8.8 0.5 collective-permute-start.1
  9.3 0.2 collective-permute-start.3
  9.6 0.1 multiply_negate_fusion
  9.6 0.1 neg.8
  9.7 3.4 %coil_forward.1 = (f32[256,640]{1,0:T(8,128)S(1)}, bf16[256,640]{1,0:T(8,128)(2,1)}) custom-call(f32[2,2,8,320]{3,2,1,0:T(8,128)S(1)} %bitcast.17, f32[2,16,2,8,320]{4,3,2,1,0:T(8,128)} %refs_1_.6, bf16[640,640]{1,0:T(8,128)(2,1)} %constant.54.clone.refs_2_.refs_3_, bf16[640,640]{1,0:T(8,128)(2,1)} %constant.55.clone.refs_3_.refs_4_), custom_call_target="tpu_custom_call" | custom-call | flops 629145600 | bytes 4000000 | tf_op jit(solution)/shard_map/coil_forward/pallas_call | solution.py:34
  13.2 0.0 collective-permute-done.4.refs_7_.refs_5_
  13.2 0.9 %collective-permute-start = (bf16[256,640]{1,0:T(8,128)(2,1)}, bf16[256,640]{1,0:T(8,128)(2,1)S(1)}, u32[]{:S(2)}, u32[]{:S(2)}) collective-permute-start(bf16[256,640]{1,0:T(8,128)(2,1)} %get-tuple-element.15), channel_id=1, source_target_pairs={{0,1},{1,0},{2,3},{3,2},{4,5},{5,4},{6,7},{7,6},{8,9},{9,8},{10,11... | collective-permute-start | bytes 983048 | tf_op jit(solution)/shard_map/ppermute | solution.py:487
  14.1 0.4 collective-permute-done.5.refs_8_.refs_5_
  14.5 1.5 %collective-permute-start.6 = (bf16[320,512]{1,0:T(8,128)(2,1)S(1)}, bf16[320,512]{1,0:T(8,128)(2,1)S(1)}, u32[]{:S(2)}, u32[]{:S(2)}) collective-permute-start(bf16[320,512]{1,0:T(8,128)(2,1)S(1)} %collective-permute-done.4.refs_7_.refs_5_), channel_id=1, source_target_pairs={{0,1},{1,0},{2,3},{3,2},{4,5},{5,4},{6,7},{7,6},{8,9},{9,8},{10,11... | collective-permute-start | bytes 983048 | tf_op jit(solution)/shard_map/ppermute | solution.py:445
  16.0 0.0 collective-permute-done.2.refs_5_.refs_3_
  16.0 1.4 %collective-permute-start.7 = (bf16[320,512]{1,0:T(8,128)(2,1)S(1)}, bf16[320,512]{1,0:T(8,128)(2,1)S(1)}, u32[]{:S(2)}, u32[]{:S(2)}) collective-permute-start(bf16[320,512]{1,0:T(8,128)(2,1)S(1)} %collective-permute-done.5.refs_8_.refs_5_), channel_id=1, source_target_pairs={{0,2},{2,0},{4,6},{6,4},{8,10},{10,8},{12,14},{14,12},{16,18},{18,... | collective-permute-start | bytes 983048 | tf_op jit(solution)/shard_map/ppermute | solution.py:425
  17.5 0.1 pad_add_fusion.refs_0_
  17.6 1.1 %collective-permute-done.3.refs_6_.refs_4_ = bf16[320,512]{1,0:T(8,128)(2,1)} collective-permute-done((bf16[320,512]{1,0:T(8,128)(2,1)S(1)}, bf16[320,512]{1,0:T(8,128)(2,1)}, u32[]{:S(2)}, u32[]{:S(2)}) %collective-permute-start.3) | collective-permute-done | bytes 327712 | tf_op jit(solution)/shard_map/ppermute | solution.py:425
  18.7 1.5 %stack_full.1.refs_8_.refs_1_ = bf16[768,1280]{1,0:T(8,128)(2,1)S(1)} custom-call(bf16[320,512]{1,0:T(8,128)(2,1)S(1)} %get-tuple-element.26.refs_2_.refs_0_, bf16[320,512]{1,0:T(8,128)(2,1)S(1)} %get-tuple-element.25.refs_3_.refs_1_, bf16[320,512]{1,0:T(8,128)(2,1)S(1)} %collective-permute-done.1.refs_4_.refs_2_, ...), custom_call_target="tpu_custom_call" | custom-call | bytes 5000000 | tf_op jit(solution)/shard_map/stack_full/pallas_call | solution.py:34
  20.3 1.3 %copy-done = bf16[768,1280]{1,0:T(8,128)(2,1)} copy-done((bf16[768,1280]{1,0:T(8,128)(2,1)}, bf16[768,1280]{1,0:T(8,128)(2,1)S(1)}, u32[]{:S(2)}) %copy-start) | copy-done | bytes 1966104
  21.6 0.0 copy-start.7
  21.6 3.4 %conv_act.1.refs_7_.refs_1_ = f32[2,320,512]{2,1,0:T(8,128)S(1)} custom-call(s32[2]{0:T(128)S(1)} %pad_add_fusion.refs_0_, bf16[27,64,64]{2,1,0:T(8,128)(2,1)S(1)} %copy-done.5, bf16[320,512]{1,0:T(8,128)(2,1)S(1)} %get-tuple-element.26.refs_2_.refs_0_, bf16[320,512]{1,0:T(8,128)(2,1)S(1)} %get-tuple-element.25.refs_3_.refs_1_, ...), custom_call_target="tpu_custom_call" | custom-call | flops 1761607680 | bytes 5000000 | tf_op jit(solution)/shard_map/conv_act/pallas_call | solution.py:34
  25.0 0.0 collective-permute-done.refs_6_
  25.1 2.1 %coil_back.1.refs_2_ = f32[2,2,8,320]{3,2,1,0:T(8,128)} custom-call(f32[2,2,8,320]{3,2,1,0:T(8,128)S(1)} %bitcast.18, f32[2,16,2,8,320]{4,3,2,1,0:T(8,128)S(1)} %copy-done.4, s32[4,320]{1,0:T(4,128)S(1)} %bitcast.19, bf16[640,640]{1,0:T(8,128)(2,1)S(1)} %copy-done.2, bf16[640,640]{1,0:T(8,128)(2,1)S(1)} %copy-done.3, ...), custom_call_target="tpu_custom_call" | custom-call | flops 629145600 | bytes 5000000 | tf_op jit(solution)/shard_map/coil_back/pallas_call | solution.py:34
  27.2 2.0 %collective-permute-done.6.refs_6_ = bf16[320,512]{1,0:T(8,128)(2,1)S(1)} collective-permute-done((bf16[320,512]{1,0:T(8,128)(2,1)S(1)}, bf16[320,512]{1,0:T(8,128)(2,1)S(1)}, u32[]{:S(2)}, u32[]{:S(2)}) %collective-permute-start.6) | collective-permute-done | bytes 327712 | tf_op jit(solution)/shard_map/ppermute | solution.py:445
  29.2 1.9 %grad_act.1 = (bf16[320,512]{1,0:T(8,128)(2,1)S(1)}, bf16[320,512]{1,0:T(8,128)(2,1)S(1)}, bf16[384,1280]{1,0:T(8,128)(2,1)S(1)}) custom-call(s32[2]{0:T(128)S(1)} %pad_add_fusion.refs_0_, f32[2,320,512]{2,1,0:T(8,128)S(1)} %conv_act.1.refs_7_.refs_1_, f32[2,2,8,320]{3,2,1,0:T(8,128)} %coil_back.1.refs_2_, bf16[48,512]{1,0:T(8,128)(2,1)S(1)} %pad_maximum_fusion.refs_3_, ...), custom_call_target="tpu_custom_call" | custom-call | flops 251658240 | bytes 4000000 | tf_op jit(solution)/shard_map/grad_act/pallas_call | solution.py:34
  31.1 3.1 %grad_weight.1 = (f32[448,128]{1,0:T(8,128)S(1)}, f32[448,128]{1,0:T(8,128)S(1)}) custom-call(s32[2]{0:T(128)S(1)} %pad_add_fusion.refs_0_, bf16[768,1280]{1,0:T(8,128)(2,1)S(1)} %copy-done.1, bf16[384,1280]{1,0:T(8,128)(2,1)S(1)} %get-tuple-element.18.refs_2_, bf16[320,512]{1,0:T(8,128)(2,1)S(1)} %get-tuple-element.16.refs_2_.refs_3_, ...), custom_call_target="tpu_custom_call" | custom-call | flops 1761607680 | bytes 5000000 | tf_op jit(solution)/shard_map/grad_weight/pallas_call | solution.py:34
  34.1 1.7 %collective-permute-start.15 = (f32[448,128]{1,0:T(8,128)S(1)}, f32[448,128]{1,0:T(8,128)S(1)}, u32[]{:S(2)}, u32[]{:S(2)}) collective-permute-start(f32[448,128]{1,0:T(8,128)S(1)} %get-tuple-element.20), channel_id=1, source_target_pairs={{0,2},{2,0},{4,6},{6,4},{8,10},{10,8},{12,14},{14,12},{16,18},{18,... | collective-permute-start | bytes 688136 | tf_op jit(solution)/shard_map/ppermute | solution.py:388
  35.9 1.1 %collective-permute-done.15.refs_2_ = f32[448,128]{1,0:T(8,128)S(1)} collective-permute-done((f32[448,128]{1,0:T(8,128)S(1)}, f32[448,128]{1,0:T(8,128)S(1)}, u32[]{:S(2)}, u32[]{:S(2)}) %collective-permute-start.15) | collective-permute-done | bytes 229408 | tf_op jit(solution)/shard_map/ppermute | solution.py:388
  37.0 0.2 collective-permute-start.16
  37.2 3.9 %collective-permute-start.11 = (bf16[320,512]{1,0:T(8,128)(2,1)S(1)}, bf16[320,512]{1,0:T(8,128)(2,1)S(1)}, u32[]{:S(2)}, u32[]{:S(2)}) collective-permute-start(bf16[320,512]{1,0:T(8,128)(2,1)S(1)} %get-tuple-element.17.refs_3_.refs_4_), channel_id=1, source_target_pairs={{0,30},{2,4},{4,2},{6,8},{8,6},{10,12},{12,10},{14,16},{16,14},{18... | collective-permute-start | bytes 983048 | tf_op jit(solution)/shard_map/ppermute | solution.py:425
  41.1 1.4 %collective-permute-done.16 = f32[224,128]{1,0:T(8,128)S(1)} collective-permute-done((f32[224,128]{1,0:T(8,128)S(1)}, f32[224,128]{1,0:T(8,128)S(1)}, u32[]{:S(2)}, u32[]{:S(2)}) %collective-permute-start.16) | collective-permute-done | bytes 114720 | tf_op jit(solution)/shard_map/ppermute | solution.py:392
  42.5 3.2 %collective-permute-start.17 = (f32[224,128]{1,0:T(8,128)S(1)}, f32[224,128]{1,0:T(8,128)S(1)}, u32[]{:S(2)}, u32[]{:S(2)}) collective-permute-start(f32[224,128]{1,0:T(8,128)S(1)} %add.39), channel_id=1, source_target_pairs={{0,1},{1,0},{2,3},{3,2},{4,5},{5,4},{6,7},{7,6},{8,9},{9,8},{10,11... | collective-permute-start | bytes 344072 | tf_op jit(solution)/shard_map/ppermute | solution.py:395
  45.7 0.1 collective-permute-start.12
  45.8 1.1 %collective-permute-start.10 = (bf16[320,512]{1,0:T(8,128)(2,1)S(1)}, bf16[320,512]{1,0:T(8,128)(2,1)S(1)}, u32[]{:S(2)}, u32[]{:S(2)}) collective-permute-start(bf16[320,512]{1,0:T(8,128)(2,1)S(1)} %get-tuple-element.16.refs_2_.refs_3_), channel_id=1, source_target_pairs={{0,30},{2,4},{4,2},{6,8},{8,6},{10,12},{12,10},{14,16},{16,14},{18... | collective-permute-start | bytes 983048 | tf_op jit(solution)/shard_map/ppermute | solution.py:425
  46.9 1.6 %collective-permute-start.8 = (bf16[320,512]{1,0:T(8,128)(2,1)S(1)}, bf16[320,512]{1,0:T(8,128)(2,1)S(1)}, u32[]{:S(2)}, u32[]{:S(2)}) collective-permute-start(bf16[320,512]{1,0:T(8,128)(2,1)S(1)} %get-tuple-element.16.refs_2_.refs_3_), channel_id=1, source_target_pairs={{0,2},{2,0},{4,6},{6,4},{8,10},{10,8},{12,14},{14,12},{16,18},{18,... | collective-permute-start | bytes 983048 | tf_op jit(solution)/shard_map/ppermute | solution.py:425
  48.5 1.2 %collective-permute-done.17 = f32[224,128]{1,0:T(8,128)S(1)} collective-permute-done((f32[224,128]{1,0:T(8,128)S(1)}, f32[224,128]{1,0:T(8,128)S(1)}, u32[]{:S(2)}, u32[]{:S(2)}) %collective-permute-start.17) | collective-permute-done | bytes 114720 | tf_op jit(solution)/shard_map/ppermute | solution.py:395
  49.8 1.0 %collective-permute-start.18 = (f32[224,128]{1,0:T(8,128)S(1)}, f32[224,128]{1,0:T(8,128)S(1)}, u32[]{:S(2)}, u32[]{:S(2)}) collective-permute-start(f32[224,128]{1,0:T(8,128)S(1)} %add.40), channel_id=1, source_target_pairs={{0,8},{2,10},{4,12},{6,14},{8,0},{10,2},{12,4},{14,6},{16,24},{18,... | collective-permute-start | bytes 344072 | tf_op jit(solution)/shard_map/ppermute | solution.py:395
  50.8 3.6 %collective-permute-done.12.refs_8_ = bf16[320,512]{1,0:T(8,128)(2,1)} collective-permute-done((bf16[320,512]{1,0:T(8,128)(2,1)S(1)}, bf16[320,512]{1,0:T(8,128)(2,1)}, u32[]{:S(2)}, u32[]{:S(2)}) %collective-permute-start.12) | collective-permute-done | bytes 327712 | tf_op jit(solution)/shard_map/ppermute | solution.py:443
  54.3 0.9 %collective-permute-start.13 = (bf16[320,512]{1,0:T(8,128)(2,1)S(1)}, bf16[320,512]{1,0:T(8,128)(2,1)S(1)}, u32[]{:S(2)}, u32[]{:S(2)}) collective-permute-start(bf16[320,512]{1,0:T(8,128)(2,1)S(1)} %collective-permute-done.11.refs_7_), channel_id=1, source_target_pairs={{0,1},{1,0},{2,3},{3,2},{4,5},{5,4},{6,7},{7,6},{8,9},{9,8},{10,11... | collective-permute-start | bytes 983048 | tf_op jit(solution)/shard_map/ppermute | solution.py:445
  55.3 0.2 collective-permute-done.18
  55.5 3.1 %collective-permute-start.19 = (f32[224,128]{1,0:T(8,128)S(1)}, f32[224,128]{1,0:T(8,128)S(1)}, u32[]{:S(2)}, u32[]{:S(2)}) collective-permute-start(f32[224,128]{1,0:T(8,128)S(1)} %add.41.refs_0_), channel_id=1, source_target_pairs={{0,16},{2,18},{4,20},{6,22},{8,24},{10,26},{12,28},{14,30},{16,0},... | collective-permute-start | bytes 344072 | tf_op jit(solution)/shard_map/ppermute | solution.py:401
  58.6 3.6 %conv_back.1.refs_2_.refs_1_ = f32[2,320,512]{2,1,0:T(8,128)S(1)} custom-call(s32[2]{0:T(128)S(1)} %pad_add_fusion.refs_0_, bf16[27,64,64]{2,1,0:T(8,128)(2,1)S(1)} %copy-done.5, bf16[320,512]{1,0:T(8,128)(2,1)S(1)} %get-tuple-element.16.refs_2_.refs_3_, bf16[320,512]{1,0:T(8,128)(2,1)S(1)} %get-tuple-element.17.refs_3_.refs_4_, ...), custom_call_target="tpu_custom_call" | custom-call | flops 1761607680 | bytes 5000000 | tf_op jit(solution)/shard_map/conv_back/pallas_call | solution.py:34
  62.2 2.6 %collective-permute-done.19.refs_1_ = f32[224,128]{1,0:T(8,128)S(1)} collective-permute-done((f32[224,128]{1,0:T(8,128)S(1)}, f32[224,128]{1,0:T(8,128)S(1)}, u32[]{:S(2)}, u32[]{:S(2)}) %collective-permute-start.19) | collective-permute-done | bytes 114720 | tf_op jit(solution)/shard_map/ppermute | solution.py:401
  64.8 2.5 %collective-permute-start.20 = (bf16[224,128]{1,0:T(8,128)(2,1)S(1)}, bf16[224,128]{1,0:T(8,128)(2,1)S(1)}, u32[]{:S(2)}, u32[]{:S(2)}) collective-permute-start(bf16[224,128]{1,0:T(8,128)(2,1)S(1)} %finish.1.refs_6_), channel_id=1, source_target_pairs={{0,4},{2,6},{4,0},{6,2},{8,12},{10,14},{12,8},{14,10},{16,20},{18,... | collective-permute-start | bytes 172040 | tf_op jit(solution)/shard_map/ppermute | solution.py:406
  67.3 2.2 %collective-permute-done.20.refs_7_ = bf16[224,128]{1,0:T(8,128)(2,1)S(1)} collective-permute-done((bf16[224,128]{1,0:T(8,128)(2,1)S(1)}, bf16[224,128]{1,0:T(8,128)(2,1)S(1)}, u32[]{:S(2)}, u32[]{:S(2)}) %collective-permute-start.20) | collective-permute-done | bytes 57376 | tf_op jit(solution)/shard_map/ppermute | solution.py:406
  69.5 0.1 pad_add_fusion.1.refs_5_
  69.6 1.1 %collective-permute-done.22.refs_9_ = bf16[224,128]{1,0:T(8,128)(2,1)S(1)} collective-permute-done((bf16[224,128]{1,0:T(8,128)(2,1)S(1)}, bf16[224,128]{1,0:T(8,128)(2,1)S(1)}, u32[]{:S(2)}, u32[]{:S(2)}) %collective-permute-start.22) | collective-permute-done | bytes 57376 | tf_op jit(solution)/shard_map/ppermute | solution.py:407
  70.7 2.3 %finish_both.1 = (bf16[2,320,512]{2,1,0:T(8,128)(2,1)}, f32[27,64,64]{2,1,0:T(8,128)}) custom-call(s32[2]{0:T(128)S(1)} %pad_add_fusion.refs_0_, f32[2,320,512]{2,1,0:T(8,128)S(1)} %conv_back.1.refs_2_.refs_1_, bf16[27,64,64]{2,1,0:T(8,128)(2,1)S(1)} %copy-done.5, bf16[320,512]{1,0:T(8,128)(2,1)S(1)} %collective-permute-done.13.refs_3_, ...), custom_call_target="tpu_custom_call" | custom-call | flops 251658240 | bytes 4000000 | tf_op jit(solution)/shard_map/finish_both/pallas_call | solution.py:34
  (36 shorter events, 0.2 us)
Async XLA Ops:
  0.6 8.9 %copy-start.8 = (bf16[2,64]{1,0:T(2,128)(2,1)S(1)}, bf16[2,64]{1,0:T(2,128)(2,1)}, u32[]{:S(2)}) copy-start(bf16[2,64]{1,0:T(2,128)(2,1)} %param.10) | copy-start | bytes 772
  0.6 9.1 %copy-start.6 = (f32[1,2,2,8,320]{4,3,2,1,0:T(8,128)S(1)}, f32[1,2,2,8,320]{4,3,2,1,0:T(8,128)}, u32[]{:S(2)}) copy-start(f32[1,2,2,8,320]{4,3,2,1,0:T(8,128)} %param.11) | copy-start | bytes 122884
  1.8 11.4 %collective-permute-start.4 = (bf16[320,512]{1,0:T(8,128)(2,1)S(1)}, bf16[320,512]{1,0:T(8,128)(2,1)S(1)}, u32[]{:S(2)}, u32[]{:S(2)}) collective-permute-start(bf16[320,512]{1,0:T(8,128)(2,1)S(1)} %get-tuple-element.25.refs_3_.refs_1_), channel_id=1, source_target_pairs={{0,30},{2,4},{4,2},{6,8},{8,6},{10,12},{12,10},{14,16},{16,14},{18... | collective-permute-start | bytes 983048 | tf_op jit(solution)/shard_map/ppermute | solution.py:425
  7.3 7.3 %collective-permute-start.5 = (bf16[320,512]{1,0:T(8,128)(2,1)S(1)}, bf16[320,512]{1,0:T(8,128)(2,1)S(1)}, u32[]{:S(2)}, u32[]{:S(2)}) collective-permute-start(bf16[320,512]{1,0:T(8,128)(2,1)S(1)} %get-tuple-element.25.refs_3_.refs_1_), channel_id=1, source_target_pairs={{0,1},{1,0},{2,3},{3,2},{4,5},{5,4},{6,7},{7,6},{8,9},{9,8},{10,11... | collective-permute-start | bytes 983048 | tf_op jit(solution)/shard_map/ppermute | solution.py:443
  8.8 7.3 %collective-permute-start.2 = (bf16[320,512]{1,0:T(8,128)(2,1)S(1)}, bf16[320,512]{1,0:T(8,128)(2,1)S(1)}, u32[]{:S(2)}, u32[]{:S(2)}) collective-permute-start(bf16[320,512]{1,0:T(8,128)(2,1)S(1)} %get-tuple-element.25.refs_3_.refs_1_), channel_id=1, source_target_pairs={{0,2},{2,0},{4,6},{6,4},{8,10},{10,8},{12,14},{14,12},{16,18},{18,... | collective-permute-start | bytes 983048 | tf_op jit(solution)/shard_map/ppermute | solution.py:425
  8.8 8.8 %collective-permute-start.1 = (bf16[320,512]{1,0:T(8,128)(2,1)S(1)}, bf16[320,512]{1,0:T(8,128)(2,1)S(1)}, u32[]{:S(2)}, u32[]{:S(2)}) collective-permute-start(bf16[320,512]{1,0:T(8,128)(2,1)S(1)} %get-tuple-element.26.refs_2_.refs_0_), channel_id=1, source_target_pairs={{0,2},{2,0},{4,6},{6,4},{8,10},{10,8},{12,14},{14,12},{16,18},{18,... | collective-permute-start | bytes 983048 | tf_op jit(solution)/shard_map/ppermute | solution.py:425
  9.3 9.4 %collective-permute-start.3 = (bf16[320,512]{1,0:T(8,128)(2,1)S(1)}, bf16[320,512]{1,0:T(8,128)(2,1)}, u32[]{:S(2)}, u32[]{:S(2)}) collective-permute-start(bf16[320,512]{1,0:T(8,128)(2,1)S(1)} %get-tuple-element.26.refs_2_.refs_0_), channel_id=1, source_target_pairs={{0,30},{2,4},{4,2},{6,8},{8,6},{10,12},{12,10},{14,16},{16,14},{18... | collective-permute-start | bytes 983048 | tf_op jit(solution)/shard_map/ppermute | solution.py:425
  13.2 11.8 %collective-permute-start = (bf16[256,640]{1,0:T(8,128)(2,1)}, bf16[256,640]{1,0:T(8,128)(2,1)S(1)}, u32[]{:S(2)}, u32[]{:S(2)}) collective-permute-start(bf16[256,640]{1,0:T(8,128)(2,1)} %get-tuple-element.15), channel_id=1, source_target_pairs={{0,1},{1,0},{2,3},{3,2},{4,5},{5,4},{6,7},{7,6},{8,9},{9,8},{10,11... | collective-permute-start | bytes 983048 | tf_op jit(solution)/shard_map/ppermute | solution.py:487
  14.5 14.6 %collective-permute-start.6 = (bf16[320,512]{1,0:T(8,128)(2,1)S(1)}, bf16[320,512]{1,0:T(8,128)(2,1)S(1)}, u32[]{:S(2)}, u32[]{:S(2)}) collective-permute-start(bf16[320,512]{1,0:T(8,128)(2,1)S(1)} %collective-permute-done.4.refs_7_.refs_5_), channel_id=1, source_target_pairs={{0,1},{1,0},{2,3},{3,2},{4,5},{5,4},{6,7},{7,6},{8,9},{9,8},{10,11... | collective-permute-start | bytes 983048 | tf_op jit(solution)/shard_map/ppermute | solution.py:445
  16.0 13.1 %collective-permute-start.7 = (bf16[320,512]{1,0:T(8,128)(2,1)S(1)}, bf16[320,512]{1,0:T(8,128)(2,1)S(1)}, u32[]{:S(2)}, u32[]{:S(2)}) collective-permute-start(bf16[320,512]{1,0:T(8,128)(2,1)S(1)} %collective-permute-done.5.refs_8_.refs_5_), channel_id=1, source_target_pairs={{0,2},{2,0},{4,6},{6,4},{8,10},{10,8},{12,14},{14,12},{16,18},{18,... | collective-permute-start | bytes 983048 | tf_op jit(solution)/shard_map/ppermute | solution.py:425
  17.6 4.0 %copy-start.5 = (bf16[27,64,64]{2,1,0:T(8,128)(2,1)S(1)}, bf16[27,64,64]{2,1,0:T(8,128)(2,1)}, u32[]{:S(2)}) copy-start(bf16[27,64,64]{2,1,0:T(8,128)(2,1)} %refs_2_.2) | copy-start | bytes 663556
  20.3 1.3 %copy-start = (bf16[768,1280]{1,0:T(8,128)(2,1)}, bf16[768,1280]{1,0:T(8,128)(2,1)S(1)}, u32[]{:S(2)}) copy-start(bf16[768,1280]{1,0:T(8,128)(2,1)S(1)} %stack_full.1.refs_8_.refs_1_) | copy-start | bytes 5898244
  21.6 3.5 %copy-start.2 = (bf16[640,640]{1,0:T(8,128)(2,1)S(1)}, bf16[640,640]{1,0:T(8,128)(2,1)}, u32[]{:S(2)}) copy-start(bf16[640,640]{1,0:T(8,128)(2,1)} %constant.54.clone.refs_2_.refs_3_) | copy-start | bytes 2457604
  21.6 3.5 %copy-start.3 = (bf16[640,640]{1,0:T(8,128)(2,1)S(1)}, bf16[640,640]{1,0:T(8,128)(2,1)}, u32[]{:S(2)}) copy-start(bf16[640,640]{1,0:T(8,128)(2,1)} %constant.55.clone.refs_3_.refs_4_) | copy-start | bytes 2457604
  21.6 3.5 %copy-start.4 = (f32[2,16,2,8,320]{4,3,2,1,0:T(8,128)S(1)}, f32[2,16,2,8,320]{4,3,2,1,0:T(8,128)}, u32[]{:S(2)}) copy-start(f32[2,16,2,8,320]{4,3,2,1,0:T(8,128)} %refs_1_.6) | copy-start | bytes 1966084
  21.6 3.5 %copy-start.7 = (s32[1,4,320]{2,1,0:T(4,128)S(1)}, s32[1,4,320]{2,1,0:T(4,128)}, u32[]{:S(2)}) copy-start(s32[1,4,320]{2,1,0:T(4,128)} %param.13) | copy-start | bytes 15364
  27.2 3.9 %copy-start.1 = (bf16[768,1280]{1,0:T(8,128)(2,1)S(1)}, bf16[768,1280]{1,0:T(8,128)(2,1)}, u32[]{:S(2)}) copy-start(bf16[768,1280]{1,0:T(8,128)(2,1)} %copy-done) | copy-start | bytes 5898244
  34.1 2.9 %collective-permute-start.15 = (f32[448,128]{1,0:T(8,128)S(1)}, f32[448,128]{1,0:T(8,128)S(1)}, u32[]{:S(2)}, u32[]{:S(2)}) collective-permute-start(f32[448,128]{1,0:T(8,128)S(1)} %get-tuple-element.20), channel_id=1, source_target_pairs={{0,2},{2,0},{4,6},{6,4},{8,10},{10,8},{12,14},{14,12},{16,18},{18,... | collective-permute-start | bytes 688136 | tf_op jit(solution)/shard_map/ppermute | solution.py:388
  37.0 5.5 %collective-permute-start.16 = (f32[224,128]{1,0:T(8,128)S(1)}, f32[224,128]{1,0:T(8,128)S(1)}, u32[]{:S(2)}, u32[]{:S(2)}) collective-permute-start(f32[224,128]{1,0:T(8,128)S(1)} %get-tuple-element.22), channel_id=1, source_target_pairs={{0,4},{2,6},{4,0},{6,2},{8,12},{10,14},{12,8},{14,10},{16,20},{18,... | collective-permute-start | bytes 344072 | tf_op jit(solution)/shard_map/ppermute | solution.py:392
  37.2 12.6 %collective-permute-start.11 = (bf16[320,512]{1,0:T(8,128)(2,1)S(1)}, bf16[320,512]{1,0:T(8,128)(2,1)S(1)}, u32[]{:S(2)}, u32[]{:S(2)}) collective-permute-start(bf16[320,512]{1,0:T(8,128)(2,1)S(1)} %get-tuple-element.17.refs_3_.refs_4_), channel_id=1, source_target_pairs={{0,30},{2,4},{4,2},{6,8},{8,6},{10,12},{12,10},{14,16},{16,14},{18... | collective-permute-start | bytes 983048 | tf_op jit(solution)/shard_map/ppermute | solution.py:425
  42.5 7.2 %collective-permute-start.17 = (f32[224,128]{1,0:T(8,128)S(1)}, f32[224,128]{1,0:T(8,128)S(1)}, u32[]{:S(2)}, u32[]{:S(2)}) collective-permute-start(f32[224,128]{1,0:T(8,128)S(1)} %add.39), channel_id=1, source_target_pairs={{0,1},{1,0},{2,3},{3,2},{4,5},{5,4},{6,7},{7,6},{8,9},{9,8},{10,11... | collective-permute-start | bytes 344072 | tf_op jit(solution)/shard_map/ppermute | solution.py:395
  45.7 8.6 %collective-permute-start.12 = (bf16[320,512]{1,0:T(8,128)(2,1)S(1)}, bf16[320,512]{1,0:T(8,128)(2,1)}, u32[]{:S(2)}, u32[]{:S(2)}) collective-permute-start(bf16[320,512]{1,0:T(8,128)(2,1)S(1)} %get-tuple-element.17.refs_3_.refs_4_), channel_id=1, source_target_pairs={{0,1},{1,0},{2,3},{3,2},{4,5},{5,4},{6,7},{7,6},{8,9},{9,8},{10,11... | collective-permute-start | bytes 983048 | tf_op jit(solution)/shard_map/ppermute | solution.py:443
  45.8 9.7 %collective-permute-start.10 = (bf16[320,512]{1,0:T(8,128)(2,1)S(1)}, bf16[320,512]{1,0:T(8,128)(2,1)S(1)}, u32[]{:S(2)}, u32[]{:S(2)}) collective-permute-start(bf16[320,512]{1,0:T(8,128)(2,1)S(1)} %get-tuple-element.16.refs_2_.refs_3_), channel_id=1, source_target_pairs={{0,30},{2,4},{4,2},{6,8},{8,6},{10,12},{12,10},{14,16},{16,14},{18... | collective-permute-start | bytes 983048 | tf_op jit(solution)/shard_map/ppermute | solution.py:425
  46.9 11.7 %collective-permute-start.8 = (bf16[320,512]{1,0:T(8,128)(2,1)S(1)}, bf16[320,512]{1,0:T(8,128)(2,1)S(1)}, u32[]{:S(2)}, u32[]{:S(2)}) collective-permute-start(bf16[320,512]{1,0:T(8,128)(2,1)S(1)} %get-tuple-element.16.refs_2_.refs_3_), channel_id=1, source_target_pairs={{0,2},{2,0},{4,6},{6,4},{8,10},{10,8},{12,14},{14,12},{16,18},{18,... | collective-permute-start | bytes 983048 | tf_op jit(solution)/shard_map/ppermute | solution.py:425
  49.8 8.8 %collective-permute-start.9 = (bf16[320,512]{1,0:T(8,128)(2,1)S(1)}, bf16[320,512]{1,0:T(8,128)(2,1)S(1)}, u32[]{:S(2)}, u32[]{:S(2)}) collective-permute-start(bf16[320,512]{1,0:T(8,128)(2,1)S(1)} %get-tuple-element.17.refs_3_.refs_4_), channel_id=1, source_target_pairs={{0,2},{2,0},{4,6},{6,4},{8,10},{10,8},{12,14},{14,12},{16,18},{18,... | collective-permute-start | bytes 983048 | tf_op jit(solution)/shard_map/ppermute | solution.py:425
  49.8 5.7 %collective-permute-start.18 = (f32[224,128]{1,0:T(8,128)S(1)}, f32[224,128]{1,0:T(8,128)S(1)}, u32[]{:S(2)}, u32[]{:S(2)}) collective-permute-start(f32[224,128]{1,0:T(8,128)S(1)} %add.40), channel_id=1, source_target_pairs={{0,8},{2,10},{4,12},{6,14},{8,0},{10,2},{12,4},{14,6},{16,24},{18,... | collective-permute-start | bytes 344072 | tf_op jit(solution)/shard_map/ppermute | solution.py:395
  54.3 15.2 %collective-permute-start.13 = (bf16[320,512]{1,0:T(8,128)(2,1)S(1)}, bf16[320,512]{1,0:T(8,128)(2,1)S(1)}, u32[]{:S(2)}, u32[]{:S(2)}) collective-permute-start(bf16[320,512]{1,0:T(8,128)(2,1)S(1)} %collective-permute-done.11.refs_7_), channel_id=1, source_target_pairs={{0,1},{1,0},{2,3},{3,2},{4,5},{5,4},{6,7},{7,6},{8,9},{9,8},{10,11... | collective-permute-start | bytes 983048 | tf_op jit(solution)/shard_map/ppermute | solution.py:445
  55.5 14.1 %collective-permute-start.14 = (bf16[320,512]{1,0:T(8,128)(2,1)}, bf16[320,512]{1,0:T(8,128)(2,1)S(1)}, u32[]{:S(2)}, u32[]{:S(2)}) collective-permute-start(bf16[320,512]{1,0:T(8,128)(2,1)} %collective-permute-done.12.refs_8_), channel_id=1, source_target_pairs={{0,2},{2,0},{4,6},{6,4},{8,10},{10,8},{12,14},{14,12},{16,18},{18,... | collective-permute-start | bytes 983048 | tf_op jit(solution)/shard_map/ppermute | solution.py:425
  55.5 9.3 %collective-permute-start.19 = (f32[224,128]{1,0:T(8,128)S(1)}, f32[224,128]{1,0:T(8,128)S(1)}, u32[]{:S(2)}, u32[]{:S(2)}) collective-permute-start(f32[224,128]{1,0:T(8,128)S(1)} %add.41.refs_0_), channel_id=1, source_target_pairs={{0,16},{2,18},{4,20},{6,22},{8,24},{10,26},{12,28},{14,30},{16,0},... | collective-permute-start | bytes 344072 | tf_op jit(solution)/shard_map/ppermute | solution.py:401
  64.8 4.7 %collective-permute-start.20 = (bf16[224,128]{1,0:T(8,128)(2,1)S(1)}, bf16[224,128]{1,0:T(8,128)(2,1)S(1)}, u32[]{:S(2)}, u32[]{:S(2)}) collective-permute-start(bf16[224,128]{1,0:T(8,128)(2,1)S(1)} %finish.1.refs_6_), channel_id=1, source_target_pairs={{0,4},{2,6},{4,0},{6,2},{8,12},{10,14},{12,8},{14,10},{16,20},{18,... | collective-permute-start | bytes 172040 | tf_op jit(solution)/shard_map/ppermute | solution.py:406
  67.3 2.2 %collective-permute-start.21 = (bf16[224,128]{1,0:T(8,128)(2,1)S(1)}, bf16[224,128]{1,0:T(8,128)(2,1)S(1)}, u32[]{:S(2)}, u32[]{:S(2)}) collective-permute-start(bf16[224,128]{1,0:T(8,128)(2,1)S(1)} %finish.1.refs_6_), channel_id=1, source_target_pairs={{0,2},{2,0},{4,6},{6,4},{8,10},{10,8},{12,14},{14,12},{16,18},{18,... | collective-permute-start | bytes 172040 | tf_op jit(solution)/shard_map/ppermute | solution.py:407
  69.5 1.2 %collective-permute-start.22 = (bf16[224,128]{1,0:T(8,128)(2,1)S(1)}, bf16[224,128]{1,0:T(8,128)(2,1)S(1)}, u32[]{:S(2)}, u32[]{:S(2)}) collective-permute-start(bf16[224,128]{1,0:T(8,128)(2,1)S(1)} %collective-permute-done.20.refs_7_), channel_id=1, source_target_pairs={{0,2},{2,0},{4,6},{6,4},{8,10},{10,8},{12,14},{14,12},{16,18},{18,... | collective-permute-start | bytes 172040 | tf_op jit(solution)/shard_map/ppermute | solution.py:407

commit v3 on v2

--- a/solution.py
+++ b/solution.py
@@ -208,26 +208,6 @@
     )
 
 
-def conv_main_body(entries, flip, back, scal_ref, weight_ref, *refs):
-    inputs, out_ref, band = refs[:-2], refs[-2], refs[-1]
-    depth_len = out_ref.shape[0]
-    fill_band(scal_ref, weight_ref, band, entries, tuple(range(depth_len)), flip, back)
-    for start in range(0, out_ref.shape[2], LANES):
-        lanes = slice(start, start + LANES)
-        result = conv_columns(inputs, band, lanes)
-        for j in range(depth_len):
-            out_ref[j, :, lanes] = result[:, j * LANES : (j + 1) * LANES]
-
-
-def corner_plans(groups, flip, back, scal_ref, weight_ref, inputs, bands):
-    plans = {}
-    for (entries, out_place), band in zip(groups, bands):
-        fill_band(scal_ref, weight_ref, band, entries, (out_place,), flip, back)
-        plans[out_place] = (inputs[: len(entries)], band)
-        inputs = inputs[len(entries) :]
-    return plans
-
-
 def stack_body(*refs):
     inputs, out_ref = refs[:-1], refs[-1]
     rows, packed_len = inputs[0].shape
@@ -236,6 +216,28 @@
             pair = jnp.concatenate([ref[:, start : start + LANES], ref[:, start + LANES : start + 2 * LANES]], axis=0)
             value = pair.astype(F32).T
             out_ref[k * LANES : (k + 1) * LANES, 2 * rows * i : 2 * rows * (i + 1)] = value.astype(BF16)
+
+
+def conv_main_body(entries, flip, back, stacked, scal_ref, weight_ref, *refs):
+    inputs, out_ref, band = refs[: len(entries)], refs[len(entries)], refs[-1]
+    if stacked:
+        stack_body(*[inputs[k] for k in stacked], refs[len(entries) + 1])
+    depth_len = out_ref.shape[0]
+    fill_band(scal_ref, weight_ref, band, entries, tuple(range(depth_len)), flip, back)
+    for start in range(0, out_ref.shape[2], LANES):
+        lanes = slice(start, start + LANES)
+        result = conv_columns(inputs, band, lanes)
+        for j in range(depth_len):
+            out_ref[j, :, lanes] = result[:, j * LANES : (j + 1) * LANES]
+
+
+def corner_plans(groups, flip, back, scal_ref, weight_ref, inputs, bands):
+    plans = {}
+    for (entries, out_place), band in zip(groups, bands):
+        fill_band(scal_ref, weight_ref, band, entries, (out_place,), flip, back)
+        plans[out_place] = (inputs[: len(entries)], band)
+        inputs = inputs[len(entries) :]
+    return plans
 
 
 def grad_act_body(groups, flip, scal_ref, acc_ref, image_ref, spread_ref, weight_ref, *refs):
@@ -483,6 +485,7 @@
     )
     own_slices = [lax.dynamic_index_in_dim(features[0], pick(j), 0, keepdims=False) for j in order]
     full_in, main_in, corner_in, ends_in = halo(own_slices)
+    sent_lines, _ = lax.optimization_barrier((sent_lines, full_in[depth_len : 2 * depth_len]))
     other_lines = [
         lax.ppermute(sent_lines, "slab", [(i, (i + k) % slabs) for i in range(slabs)]) for k in range(1, slabs)
     ]
@@ -495,11 +498,12 @@
     conv_flops = 2 * row_len * len(main_entries) * packed_len * 3 * depth_len * LANES
     small_flops = 2 * row_len * 2 * packed_len * 3 * LANES
 
-    def conv_main(name, back, inputs, after=()):
+    def conv_main(name, back, inputs, after=(), stacked=()):
         return call(
             name,
-            functools.partial(conv_main_body, main_entries, flip, back),
-            jax.ShapeDtypeStruct(slab_shape, F32),
+            functools.partial(conv_main_body, main_entries, flip, back, stacked),
+            [jax.ShapeDtypeStruct(slab_shape, F32)]
+            + [jax.ShapeDtypeStruct((len(stacked) * LANES, packed_len // LANES * row_len), BF16)] * bool(stacked),
             (scal, conv_weight, *inputs),
             "SV" + "V" * len(inputs),
             scratch=[pltpu.VMEM((len(main_entries) * LANES, 3 * depth_len * LANES), BF16)],
@@ -508,17 +512,8 @@
             after=after,
         )
 
-    def stack(name, inputs):
-        return call(
-            name,
-            stack_body,
-            jax.ShapeDtypeStruct((len(inputs) * LANES, packed_len // LANES * row_len), BF16),
-            tuple(inputs),
-            "V" * len(inputs),
-            nbytes=5000000,
-        )
-
-    acc = conv_main("conv_act", False, main_in)
+    whole = tuple(range(3 * depth_len))
+    acc, stack_full = conv_main("conv_act", False, main_in, (), whole)
     grad_image = call(
         "coil_back",
         functools.partial(coil_backward_body, slabs),
@@ -531,7 +526,6 @@
         nbytes=5000000,
     )
 
-    stack_full = stack("stack_full", full_in)
     grad_outs = call(
         "grad_act",
         functools.partial(grad_act_body, corner_groups, flip),
@@ -542,7 +536,7 @@
         flops=small_flops,
         nbytes=4000000,
         scratch=bands,
-        after=[stack_full],
+        after=[],
     )
 
     grad_act, stack_ends = grad_outs[:depth_len], grad_outs[depth_len:]
@@ -567,7 +561,7 @@
         nbytes=5000000,
     )
 
-    acc_back = conv_main("conv_back", True, main_grad)
+    (acc_back,) = conv_main("conv_back", True, main_grad)
     pieces, spots = sum_over_mesh(keep, send, phases, slabs, [acc_back])
     grad_features, grad_weight = call(
         "finish_both",

time: 73.4 us -> 72.2 us (0.984)
  waiting for transfers between devices: 17 us -> 27.3 us
  starting transfers between devices: 31 us -> 22.4 us
  Pallas kernels: 21.4 us -> 19.8 us
  local copies, waits for them, and re-layouts: 2.55 us -> 1.25 us
    ppermute x10, starting transfers between devices: 14.3 us -> 8.49 us  [pass_phase(): return lax.ppermute(value, 'phase', perm)]
    ppermute x2, starting transfers between devices: 1.6 us -> 4.55 us  [halo(): slab_in = [lax.ppermute(own[edge[0]], 'slab', edge[2]) for edge in edges]]
    ppermute x1, waiting for transfers between devices: 0.01 us -> 2.4 us  [local(): lax.ppermute(sent_lines, 'slab', [(i, (i + k) % slabs) for i in range(sla...]
    ppermute x2, waiting for transfers between devices: 1.44 us -> 3.64 us  [sum_over_mesh(): part = part + lax.ppermute(part, axis, perm)]
    ppermute x2, starting transfers between devices: 4.14 us -> 2.2 us  [sum_over_mesh(): part = part + lax.ppermute(part, axis, perm)]
    ppermute x2, waiting for transfers between devices: 1.96 us -> 3.77 us  [halo(): lax.ppermute(off_in[edge[0]], 'slab', edge[2])]
    ppermute x1, starting transfers between devices: 1.74 us -> 0.07 us  [sum_over_mesh(): lax.ppermute(send, 'phase', pair_on(phases))]
    ppermute x10, waiting for transfers between devices: 1.16 us -> 2.83 us  [pass_phase(): return lax.ppermute(value, 'phase', perm)]
  transfers between devices with their start and end apart: 23 -> 23, of which waited for: 11 -> 11; matrix products, arithmetic and copies ran while one was open for 1% -> 1% of each run, Pallas kernels for 19% -> 17%
where the time goes in v3:
time: 72.2 us; the launch traced here: 71.9 us
  waiting for transfers between devices  27.3 us (38%)
  starting transfers between devices  22.4 us (31%)
  Pallas kernels  19.8 us (27%)
  local copies, waits for them, and re-layouts  1.25 us (2%)
  between operations  0.85 us (1%)
    pallas_call x9, Pallas kernels, call(): pl.pallas_call(run, out_shape=outs, in_specs=[SPECS[kind] for kind in kin...  19.8 us
    ppermute x10, starting transfers between devices, pass_phase(): return lax.ppermute(value, 'phase', perm)  8.49 us
    ppermute x2, starting transfers between devices, halo(): slab_in = [lax.ppermute(own[edge[0]], 'slab', edge[2]) for edge in edges]  4.55 us
    ppermute x2, waiting for transfers between devices, halo(): lax.ppermute(off_in[edge[0]], 'slab', edge[2])  3.77 us
    ppermute x2, waiting for transfers between devices, halo(): slab_in = [lax.ppermute(own[edge[0]], 'slab', edge[2]) for edge in edges]  3.75 us
    ppermute x2, waiting for transfers between devices, sum_over_mesh(): part = part + lax.ppermute(part, axis, perm)  3.64 us
    ppermute x1, waiting for transfers between devices, sum_over_mesh(): lax.ppermute(part, axis, perm)  3.27 us
    ppermute x1, waiting for transfers between devices, sum_over_mesh(): part = part + lax.ppermute(other, 'phase', across)  2.88 us
  transfers between devices with their start and end apart: 23, of which 11 were waited for; matrix products, arithmetic and copies ran while one was open for 1% of the time, Pallas kernels for 17%

profile of v3, /device:TPU:0, one launch (start us, length us, event | category | flops | bytes accessed | tf_op | source)
XLA Modules:
  0.0 71.9 jit_solution(10645896162316972624)
XLA Ops:
  0.7 1.1 %dynamic-slice_bitcast_fusion = (bf16[320,512]{1,0:T(8,128)(2,1)S(1)}, bf16[320,512]{1,0:T(8,128)(2,1)S(1)}) fusion(bf16[1,2,320,512]{3,2,1,0:T(8,128)(2,1)} %param.8, s32[]{:T(128)S(6)} %select_n.28, s32[]{:T(128)S(6)} %select_n.27), kind=kLoop, calls=%fused_computation | loop fusion | bytes 1310728 | tf_op jit(solution)/shard_map/jit(dynamic_index_in_dim)/squeeze | solution.py:486
  1.8 3.0 %collective-permute-start.5 = (bf16[320,512]{1,0:T(8,128)(2,1)S(1)}, bf16[320,512]{1,0:T(8,128)(2,1)S(1)}, u32[]{:S(2)}, u32[]{:S(2)}) collective-permute-start(bf16[320,512]{1,0:T(8,128)(2,1)S(1)} %get-tuple-element.31.refs_3_), channel_id=1, source_target_pairs={{0,1},{1,0},{2,3},{3,2},{4,5},{5,4},{6,7},{7,6},{8,9},{9,8},{10,11... | collective-permute-start | bytes 983048 | tf_op jit(solution)/shard_map/ppermute | solution.py:445
  4.8 4.6 %collective-permute-start.4 = (bf16[320,512]{1,0:T(8,128)(2,1)S(1)}, bf16[320,512]{1,0:T(8,128)(2,1)S(1)}, u32[]{:S(2)}, u32[]{:S(2)}) collective-permute-start(bf16[320,512]{1,0:T(8,128)(2,1)S(1)} %get-tuple-element.31.refs_3_), channel_id=1, source_target_pairs={{0,30},{2,4},{4,2},{6,8},{8,6},{10,12},{12,10},{14,16},{16,14},{18... | collective-permute-start | bytes 983048 | tf_op jit(solution)/shard_map/ppermute | solution.py:427
  9.5 0.6 collective-permute-start.3
  10.1 0.1 multiply_negate_fusion
  10.2 0.0 copy-start.3
  10.2 0.1 neg.8
  10.3 3.5 %coil_forward.1 = (f32[256,640]{1,0:T(8,128)S(1)}, bf16[256,640]{1,0:T(8,128)(2,1)}) custom-call(f32[2,2,8,320]{3,2,1,0:T(8,128)S(1)} %bitcast.17, f32[2,16,2,8,320]{4,3,2,1,0:T(8,128)} %refs_1_.6, bf16[640,640]{1,0:T(8,128)(2,1)} %constant.54.clone.refs_2_.refs_3_, bf16[640,640]{1,0:T(8,128)(2,1)} %constant.55.clone.refs_3_.refs_4_), custom_call_target="tpu_custom_call" | custom-call | flops 629145600 | bytes 4000000 | tf_op jit(solution)/shard_map/coil_forward/pallas_call | solution.py:34
  13.8 0.0 collective-permute-done.refs_4_
  13.8 0.5 collective-permute-start.2
  14.3 0.0 collective-permute-done.5.refs_8_.refs_5_
  14.3 0.1 collective-permute-start.7
  14.4 1.6 %collective-permute-start.6 = (bf16[320,512]{1,0:T(8,128)(2,1)S(1)}, bf16[320,512]{1,0:T(8,128)(2,1)S(1)}, u32[]{:S(2)}, u32[]{:S(2)}) collective-permute-start(bf16[320,512]{1,0:T(8,128)(2,1)S(1)} %collective-permute-done.4.refs_7_), channel_id=1, source_target_pairs={{0,1},{1,0},{2,3},{3,2},{4,5},{5,4},{6,7},{7,6},{8,9},{9,8},{10,11... | collective-permute-start | bytes 983048 | tf_op jit(solution)/shard_map/ppermute | solution.py:447
  16.0 0.1 pad_add_fusion.refs_0_
  16.1 2.8 %collective-permute-done.3.refs_6_ = bf16[320,512]{1,0:T(8,128)(2,1)} collective-permute-done((bf16[320,512]{1,0:T(8,128)(2,1)S(1)}, bf16[320,512]{1,0:T(8,128)(2,1)}, u32[]{:S(2)}, u32[]{:S(2)}) %collective-permute-start.3) | collective-permute-done | bytes 327712 | tf_op jit(solution)/shard_map/ppermute | solution.py:427
  18.9 3.3 %conv_act.1 = (f32[2,320,512]{2,1,0:T(8,128)S(1)}, bf16[768,1280]{1,0:T(8,128)(2,1)S(1)}) custom-call(s32[2]{0:T(128)S(1)} %pad_add_fusion.refs_0_, bf16[27,64,64]{2,1,0:T(8,128)(2,1)S(1)} %copy-done.3, bf16[320,512]{1,0:T(8,128)(2,1)S(1)} %get-tuple-element.32.refs_2_, bf16[320,512]{1,0:T(8,128)(2,1)S(1)} %get-tuple-element.31.refs_3_, ...), custom_call_target="tpu_custom_call" | custom-call | flops 1761607680 | bytes 5000000 | tf_op jit(solution)/shard_map/conv_act/pallas_call | solution.py:34
  22.2 2.4 %collective-permute-done.2.refs_6_ = bf16[256,640]{1,0:T(8,128)(2,1)S(1)} collective-permute-done((bf16[256,640]{1,0:T(8,128)(2,1)}, bf16[256,640]{1,0:T(8,128)(2,1)S(1)}, u32[]{:S(2)}, u32[]{:S(2)}) %collective-permute-start.2) | collective-permute-done | bytes 327712 | tf_op jit(solution)/shard_map/ppermute | solution.py:490
  24.6 2.1 %coil_back.1.refs_2_ = f32[2,2,8,320]{3,2,1,0:T(8,128)} custom-call(f32[2,2,8,320]{3,2,1,0:T(8,128)S(1)} %bitcast.18, f32[2,16,2,8,320]{4,3,2,1,0:T(8,128)S(1)} %copy-done.2, s32[4,320]{1,0:T(4,128)S(1)} %bitcast.19, bf16[640,640]{1,0:T(8,128)(2,1)S(1)} %copy-done, bf16[640,640]{1,0:T(8,128)(2,1)S(1)} %copy-done.1, ...), custom_call_target="tpu_custom_call" | custom-call | flops 629145600 | bytes 5000000 | tf_op jit(solution)/shard_map/coil_back/pallas_call | solution.py:34
  26.8 3.8 %collective-permute-done.6.refs_6_ = bf16[320,512]{1,0:T(8,128)(2,1)S(1)} collective-permute-done((bf16[320,512]{1,0:T(8,128)(2,1)S(1)}, bf16[320,512]{1,0:T(8,128)(2,1)S(1)}, u32[]{:S(2)}, u32[]{:S(2)}) %collective-permute-start.6) | collective-permute-done | bytes 327712 | tf_op jit(solution)/shard_map/ppermute | solution.py:447
  30.5 1.9 %grad_act.1 = (bf16[320,512]{1,0:T(8,128)(2,1)S(1)}, bf16[320,512]{1,0:T(8,128)(2,1)S(1)}, bf16[384,1280]{1,0:T(8,128)(2,1)S(1)}) custom-call(s32[2]{0:T(128)S(1)} %pad_add_fusion.refs_0_, f32[2,320,512]{2,1,0:T(8,128)S(1)} %get-tuple-element.20.refs_7_.refs_1_, f32[2,2,8,320]{3,2,1,0:T(8,128)} %coil_back.1.refs_2_, ...), custom_call_target="tpu_custom_call" | custom-call | flops 251658240 | bytes 4000000 | tf_op jit(solution)/shard_map/grad_act/pallas_call | solution.py:34
  32.4 3.1 %grad_weight.1 = (f32[448,128]{1,0:T(8,128)S(1)}, f32[448,128]{1,0:T(8,128)S(1)}) custom-call(s32[2]{0:T(128)S(1)} %pad_add_fusion.refs_0_, bf16[768,1280]{1,0:T(8,128)(2,1)S(1)} %get-tuple-element.23.refs_1_, bf16[384,1280]{1,0:T(8,128)(2,1)S(1)} %get-tuple-element.24.refs_2_, bf16[320,512]{1,0:T(8,128)(2,1)S(1)} %get-tuple-element.21.refs_2_.refs_3_, ...), custom_call_target="tpu_custom_call" | custom-call | flops 1761607680 | bytes 5000000 | tf_op jit(solution)/shard_map/grad_weight/pallas_call | solution.py:34
  35.5 0.1 collective-permute-start.15
  35.6 1.4 %collective-permute-done.15.refs_2_ = f32[448,128]{1,0:T(8,128)S(1)} collective-permute-done((f32[448,128]{1,0:T(8,128)S(1)}, f32[448,128]{1,0:T(8,128)S(1)}, u32[]{:S(2)}, u32[]{:S(2)}) %collective-permute-start.15) | collective-permute-done | bytes 229408 | tf_op jit(solution)/shard_map/ppermute | solution.py:390
  37.1 0.1 collective-permute-start.16
  37.1 2.3 %collective-permute-start.11 = (bf16[320,512]{1,0:T(8,128)(2,1)S(1)}, bf16[320,512]{1,0:T(8,128)(2,1)S(1)}, u32[]{:S(2)}, u32[]{:S(2)}) collective-permute-start(bf16[320,512]{1,0:T(8,128)(2,1)S(1)} %get-tuple-element.22.refs_3_.refs_4_), channel_id=1, source_target_pairs={{0,30},{2,4},{4,2},{6,8},{8,6},{10,12},{12,10},{14,16},{16,14},{18... | collective-permute-start | bytes 983048 | tf_op jit(solution)/shard_map/ppermute | solution.py:427
  39.4 2.9 %collective-permute-done.16 = f32[224,128]{1,0:T(8,128)S(1)} collective-permute-done((f32[224,128]{1,0:T(8,128)S(1)}, f32[224,128]{1,0:T(8,128)S(1)}, u32[]{:S(2)}, u32[]{:S(2)}) %collective-permute-start.16) | collective-permute-done | bytes 114720 | tf_op jit(solution)/shard_map/ppermute | solution.py:394
  42.3 0.6 collective-permute-start.17
  42.9 1.5 %collective-permute-start.12 = (bf16[320,512]{1,0:T(8,128)(2,1)S(1)}, bf16[320,512]{1,0:T(8,128)(2,1)}, u32[]{:S(2)}, u32[]{:S(2)}) collective-permute-start(bf16[320,512]{1,0:T(8,128)(2,1)S(1)} %get-tuple-element.22.refs_3_.refs_4_), channel_id=1, source_target_pairs={{0,1},{1,0},{2,3},{3,2},{4,5},{5,4},{6,7},{7,6},{8,9},{9,8},{10,11... | collective-permute-start | bytes 983048 | tf_op jit(solution)/shard_map/ppermute | solution.py:445
  44.4 0.8 %collective-permute-start.10 = (bf16[320,512]{1,0:T(8,128)(2,1)S(1)}, bf16[320,512]{1,0:T(8,128)(2,1)S(1)}, u32[]{:S(2)}, u32[]{:S(2)}) collective-permute-start(bf16[320,512]{1,0:T(8,128)(2,1)S(1)} %get-tuple-element.21.refs_2_.refs_3_), channel_id=1, source_target_pairs={{0,30},{2,4},{4,2},{6,8},{8,6},{10,12},{12,10},{14,16},{16,14},{18... | collective-permute-start | bytes 983048 | tf_op jit(solution)/shard_map/ppermute | solution.py:427
  45.3 0.0 collective-permute-start.8
  45.3 3.2 %collective-permute-done.17 = f32[224,128]{1,0:T(8,128)S(1)} collective-permute-done((f32[224,128]{1,0:T(8,128)S(1)}, f32[224,128]{1,0:T(8,128)S(1)}, u32[]{:S(2)}, u32[]{:S(2)}) %collective-permute-start.17) | collective-permute-done | bytes 114720 | tf_op jit(solution)/shard_map/ppermute | solution.py:397
  48.5 0.0 collective-permute-done.11.refs_7_
  48.5 1.6 %collective-permute-start.18 = (f32[224,128]{1,0:T(8,128)S(1)}, f32[224,128]{1,0:T(8,128)S(1)}, u32[]{:S(2)}, u32[]{:S(2)}) collective-permute-start(f32[224,128]{1,0:T(8,128)S(1)} %add.40), channel_id=1, source_target_pairs={{0,8},{2,10},{4,12},{6,14},{8,0},{10,2},{12,4},{14,6},{16,24},{18,... | collective-permute-start | bytes 344072 | tf_op jit(solution)/shard_map/ppermute | solution.py:397
  50.1 3.7 %collective-permute-done.12.refs_8_ = bf16[320,512]{1,0:T(8,128)(2,1)} collective-permute-done((bf16[320,512]{1,0:T(8,128)(2,1)S(1)}, bf16[320,512]{1,0:T(8,128)(2,1)}, u32[]{:S(2)}, u32[]{:S(2)}) %collective-permute-start.12) | collective-permute-done | bytes 327712 | tf_op jit(solution)/shard_map/ppermute | solution.py:445
  53.9 0.5 collective-permute-start.13
  54.4 0.4 collective-permute-done.18
  54.9 0.0 collective-permute-done.10.refs_6_
  54.9 2.2 %collective-permute-start.19 = (f32[224,128]{1,0:T(8,128)S(1)}, f32[224,128]{1,0:T(8,128)S(1)}, u32[]{:S(2)}, u32[]{:S(2)}) collective-permute-start(f32[224,128]{1,0:T(8,128)S(1)} %add.41.refs_0_), channel_id=1, source_target_pairs={{0,16},{2,18},{4,20},{6,22},{8,24},{10,26},{12,28},{14,30},{16,0},... | collective-permute-start | bytes 344072 | tf_op jit(solution)/shard_map/ppermute | solution.py:403
  57.1 0.0 collective-permute-done.8.refs_4_
  57.1 3.6 %conv_back.1.refs_2_.refs_1_ = f32[2,320,512]{2,1,0:T(8,128)S(1)} custom-call(s32[2]{0:T(128)S(1)} %pad_add_fusion.refs_0_, bf16[27,64,64]{2,1,0:T(8,128)(2,1)S(1)} %copy-done.3, bf16[320,512]{1,0:T(8,128)(2,1)S(1)} %get-tuple-element.21.refs_2_.refs_3_, bf16[320,512]{1,0:T(8,128)(2,1)S(1)} %get-tuple-element.22.refs_3_.refs_4_, ...), custom_call_target="tpu_custom_call" | custom-call | flops 1761607680 | bytes 5000000 | tf_op jit(solution)/shard_map/conv_back/pallas_call | solution.py:34
  60.7 3.3 %collective-permute-done.19.refs_1_ = f32[224,128]{1,0:T(8,128)S(1)} collective-permute-done((f32[224,128]{1,0:T(8,128)S(1)}, f32[224,128]{1,0:T(8,128)S(1)}, u32[]{:S(2)}, u32[]{:S(2)}) %collective-permute-start.19) | collective-permute-done | bytes 114720 | tf_op jit(solution)/shard_map/ppermute | solution.py:403
  64.0 2.2 %collective-permute-start.20 = (bf16[224,128]{1,0:T(8,128)(2,1)S(1)}, bf16[224,128]{1,0:T(8,128)(2,1)S(1)}, u32[]{:S(2)}, u32[]{:S(2)}) collective-permute-start(bf16[224,128]{1,0:T(8,128)(2,1)S(1)} %finish.1.refs_6_), channel_id=1, source_target_pairs={{0,4},{2,6},{4,0},{6,2},{8,12},{10,14},{12,8},{14,10},{16,20},{18,... | collective-permute-start | bytes 172040 | tf_op jit(solution)/shard_map/ppermute | solution.py:408
  66.1 2.2 %collective-permute-done.20.refs_7_ = bf16[224,128]{1,0:T(8,128)(2,1)S(1)} collective-permute-done((bf16[224,128]{1,0:T(8,128)(2,1)S(1)}, bf16[224,128]{1,0:T(8,128)(2,1)S(1)}, u32[]{:S(2)}, u32[]{:S(2)}) %collective-permute-start.20) | collective-permute-done | bytes 57376 | tf_op jit(solution)/shard_map/ppermute | solution.py:408
  68.3 0.0 collective-permute-start.22
  68.3 0.1 pad_add_fusion.1.refs_5_
  68.4 0.0 collective-permute-done.13.refs_3_
  68.4 1.1 %collective-permute-done.22.refs_9_ = bf16[224,128]{1,0:T(8,128)(2,1)S(1)} collective-permute-done((bf16[224,128]{1,0:T(8,128)(2,1)S(1)}, bf16[224,128]{1,0:T(8,128)(2,1)S(1)}, u32[]{:S(2)}, u32[]{:S(2)}) %collective-permute-start.22) | collective-permute-done | bytes 57376 | tf_op jit(solution)/shard_map/ppermute | solution.py:409
  69.5 2.3 %finish_both.1 = (bf16[2,320,512]{2,1,0:T(8,128)(2,1)}, f32[27,64,64]{2,1,0:T(8,128)}) custom-call(s32[2]{0:T(128)S(1)} %pad_add_fusion.refs_0_, f32[2,320,512]{2,1,0:T(8,128)S(1)} %conv_back.1.refs_2_.refs_1_, bf16[27,64,64]{2,1,0:T(8,128)(2,1)S(1)} %copy-done.3, bf16[320,512]{1,0:T(8,128)(2,1)S(1)} %collective-permute-done.13.refs_3_, ...), custom_call_target="tpu_custom_call" | custom-call | flops 251658240 | bytes 4000000 | tf_op jit(solution)/shard_map/finish_both/pallas_call | solution.py:34
  (31 shorter events, 0.1 us)
Async XLA Ops:
  0.6 9.5 %copy-start.6 = (bf16[2,64]{1,0:T(2,128)(2,1)S(1)}, bf16[2,64]{1,0:T(2,128)(2,1)}, u32[]{:S(2)}) copy-start(bf16[2,64]{1,0:T(2,128)(2,1)} %param.10) | copy-start | bytes 772
  0.6 9.7 %copy-start.4 = (f32[1,2,2,8,320]{4,3,2,1,0:T(8,128)S(1)}, f32[1,2,2,8,320]{4,3,2,1,0:T(8,128)}, u32[]{:S(2)}) copy-start(f32[1,2,2,8,320]{4,3,2,1,0:T(8,128)} %param.11) | copy-start | bytes 122884
  1.8 12.5 %collective-permute-start.5 = (bf16[320,512]{1,0:T(8,128)(2,1)S(1)}, bf16[320,512]{1,0:T(8,128)(2,1)S(1)}, u32[]{:S(2)}, u32[]{:S(2)}) collective-permute-start(bf16[320,512]{1,0:T(8,128)(2,1)S(1)} %get-tuple-element.31.refs_3_), channel_id=1, source_target_pairs={{0,1},{1,0},{2,3},{3,2},{4,5},{5,4},{6,7},{7,6},{8,9},{9,8},{10,11... | collective-permute-start | bytes 983048 | tf_op jit(solution)/shard_map/ppermute | solution.py:445
  4.8 9.0 %collective-permute-start.1 = (bf16[320,512]{1,0:T(8,128)(2,1)S(1)}, bf16[320,512]{1,0:T(8,128)(2,1)S(1)}, u32[]{:S(2)}, u32[]{:S(2)}) collective-permute-start(bf16[320,512]{1,0:T(8,128)(2,1)S(1)} %get-tuple-element.31.refs_3_), channel_id=1, source_target_pairs={{0,2},{2,0},{4,6},{6,4},{8,10},{10,8},{12,14},{14,12},{16,18},{18,... | collective-permute-start | bytes 983048 | tf_op jit(solution)/shard_map/ppermute | solution.py:427
  4.8 9.6 %collective-permute-start.4 = (bf16[320,512]{1,0:T(8,128)(2,1)S(1)}, bf16[320,512]{1,0:T(8,128)(2,1)S(1)}, u32[]{:S(2)}, u32[]{:S(2)}) collective-permute-start(bf16[320,512]{1,0:T(8,128)(2,1)S(1)} %get-tuple-element.31.refs_3_), channel_id=1, source_target_pairs={{0,30},{2,4},{4,2},{6,8},{8,6},{10,12},{12,10},{14,16},{16,14},{18... | collective-permute-start | bytes 983048 | tf_op jit(solution)/shard_map/ppermute | solution.py:427
  9.5 4.3 %collective-permute-start = (bf16[320,512]{1,0:T(8,128)(2,1)S(1)}, bf16[320,512]{1,0:T(8,128)(2,1)S(1)}, u32[]{:S(2)}, u32[]{:S(2)}) collective-permute-start(bf16[320,512]{1,0:T(8,128)(2,1)S(1)} %get-tuple-element.32.refs_2_), channel_id=1, source_target_pairs={{0,2},{2,0},{4,6},{6,4},{8,10},{10,8},{12,14},{14,12},{16,18},{18,... | collective-permute-start | bytes 983048 | tf_op jit(solution)/shard_map/ppermute | solution.py:427
  9.5 9.4 %collective-permute-start.3 = (bf16[320,512]{1,0:T(8,128)(2,1)S(1)}, bf16[320,512]{1,0:T(8,128)(2,1)}, u32[]{:S(2)}, u32[]{:S(2)}) collective-permute-start(bf16[320,512]{1,0:T(8,128)(2,1)S(1)} %get-tuple-element.32.refs_2_), channel_id=1, source_target_pairs={{0,30},{2,4},{4,2},{6,8},{8,6},{10,12},{12,10},{14,16},{16,14},{18... | collective-permute-start | bytes 983048 | tf_op jit(solution)/shard_map/ppermute | solution.py:427
  10.2 8.7 %copy-start.3 = (bf16[27,64,64]{2,1,0:T(8,128)(2,1)S(1)}, bf16[27,64,64]{2,1,0:T(8,128)(2,1)}, u32[]{:S(2)}) copy-start(bf16[27,64,64]{2,1,0:T(8,128)(2,1)} %refs_2_.2) | copy-start | bytes 663556
  13.8 10.8 %collective-permute-start.2 = (bf16[256,640]{1,0:T(8,128)(2,1)}, bf16[256,640]{1,0:T(8,128)(2,1)S(1)}, u32[]{:S(2)}, u32[]{:S(2)}) collective-permute-start(bf16[256,640]{1,0:T(8,128)(2,1)} %get-tuple-element.19), channel_id=1, source_target_pairs={{0,1},{1,0},{2,3},{3,2},{4,5},{5,4},{6,7},{7,6},{8,9},{9,8},{10,11... | collective-permute-start | bytes 983048 | tf_op jit(solution)/shard_map/ppermute | solution.py:490
  14.3 12.4 %collective-permute-start.7 = (bf16[320,512]{1,0:T(8,128)(2,1)S(1)}, bf16[320,512]{1,0:T(8,128)(2,1)S(1)}, u32[]{:S(2)}, u32[]{:S(2)}) collective-permute-start(bf16[320,512]{1,0:T(8,128)(2,1)S(1)} %collective-permute-done.5.refs_8_.refs_5_), channel_id=1, source_target_pairs={{0,2},{2,0},{4,6},{6,4},{8,10},{10,8},{12,14},{14,12},{16,18},{18,... | collective-permute-start | bytes 983048 | tf_op jit(solution)/shard_map/ppermute | solution.py:427
  14.4 16.1 %collective-permute-start.6 = (bf16[320,512]{1,0:T(8,128)(2,1)S(1)}, bf16[320,512]{1,0:T(8,128)(2,1)S(1)}, u32[]{:S(2)}, u32[]{:S(2)}) collective-permute-start(bf16[320,512]{1,0:T(8,128)(2,1)S(1)} %collective-permute-done.4.refs_7_), channel_id=1, source_target_pairs={{0,1},{1,0},{2,3},{3,2},{4,5},{5,4},{6,7},{7,6},{8,9},{9,8},{10,11... | collective-permute-start | bytes 983048 | tf_op jit(solution)/shard_map/ppermute | solution.py:447
  16.1 8.5 %copy-start = (bf16[640,640]{1,0:T(8,128)(2,1)S(1)}, bf16[640,640]{1,0:T(8,128)(2,1)}, u32[]{:S(2)}) copy-start(bf16[640,640]{1,0:T(8,128)(2,1)} %constant.54.clone.refs_2_.refs_3_) | copy-start | bytes 2457604
  16.1 8.5 %copy-start.1 = (bf16[640,640]{1,0:T(8,128)(2,1)S(1)}, bf16[640,640]{1,0:T(8,128)(2,1)}, u32[]{:S(2)}) copy-start(bf16[640,640]{1,0:T(8,128)(2,1)} %constant.55.clone.refs_3_.refs_4_) | copy-start | bytes 2457604
  16.1 8.5 %copy-start.2 = (f32[2,16,2,8,320]{4,3,2,1,0:T(8,128)S(1)}, f32[2,16,2,8,320]{4,3,2,1,0:T(8,128)}, u32[]{:S(2)}) copy-start(f32[2,16,2,8,320]{4,3,2,1,0:T(8,128)} %refs_1_.6) | copy-start | bytes 1966084
  16.1 8.6 %copy-start.5 = (s32[1,4,320]{2,1,0:T(4,128)S(1)}, s32[1,4,320]{2,1,0:T(4,128)}, u32[]{:S(2)}) copy-start(s32[1,4,320]{2,1,0:T(4,128)} %param.13) | copy-start | bytes 15364
  35.5 1.6 %collective-permute-start.15 = (f32[448,128]{1,0:T(8,128)S(1)}, f32[448,128]{1,0:T(8,128)S(1)}, u32[]{:S(2)}, u32[]{:S(2)}) collective-permute-start(f32[448,128]{1,0:T(8,128)S(1)} %get-tuple-element.26), channel_id=1, source_target_pairs={{0,2},{2,0},{4,6},{6,4},{8,10},{10,8},{12,14},{14,12},{16,18},{18,... | collective-permute-start | bytes 688136 | tf_op jit(solution)/shard_map/ppermute | solution.py:390
  37.1 5.3 %collective-permute-start.16 = (f32[224,128]{1,0:T(8,128)S(1)}, f32[224,128]{1,0:T(8,128)S(1)}, u32[]{:S(2)}, u32[]{:S(2)}) collective-permute-start(f32[224,128]{1,0:T(8,128)S(1)} %get-tuple-element.28), channel_id=1, source_target_pairs={{0,4},{2,6},{4,0},{6,2},{8,12},{10,14},{12,8},{14,10},{16,20},{18,... | collective-permute-start | bytes 344072 | tf_op jit(solution)/shard_map/ppermute | solution.py:394
  37.1 11.4 %collective-permute-start.11 = (bf16[320,512]{1,0:T(8,128)(2,1)S(1)}, bf16[320,512]{1,0:T(8,128)(2,1)S(1)}, u32[]{:S(2)}, u32[]{:S(2)}) collective-permute-start(bf16[320,512]{1,0:T(8,128)(2,1)S(1)} %get-tuple-element.22.refs_3_.refs_4_), channel_id=1, source_target_pairs={{0,30},{2,4},{4,2},{6,8},{8,6},{10,12},{12,10},{14,16},{16,14},{18... | collective-permute-start | bytes 983048 | tf_op jit(solution)/shard_map/ppermute | solution.py:427
  42.3 6.1 %collective-permute-start.17 = (f32[224,128]{1,0:T(8,128)S(1)}, f32[224,128]{1,0:T(8,128)S(1)}, u32[]{:S(2)}, u32[]{:S(2)}) collective-permute-start(f32[224,128]{1,0:T(8,128)S(1)} %add.39), channel_id=1, source_target_pairs={{0,1},{1,0},{2,3},{3,2},{4,5},{5,4},{6,7},{7,6},{8,9},{9,8},{10,11... | collective-permute-start | bytes 344072 | tf_op jit(solution)/shard_map/ppermute | solution.py:397
  42.9 11.0 %collective-permute-start.12 = (bf16[320,512]{1,0:T(8,128)(2,1)S(1)}, bf16[320,512]{1,0:T(8,128)(2,1)}, u32[]{:S(2)}, u32[]{:S(2)}) collective-permute-start(bf16[320,512]{1,0:T(8,128)(2,1)S(1)} %get-tuple-element.22.refs_3_.refs_4_), channel_id=1, source_target_pairs={{0,1},{1,0},{2,3},{3,2},{4,5},{5,4},{6,7},{7,6},{8,9},{9,8},{10,11... | collective-permute-start | bytes 983048 | tf_op jit(solution)/shard_map/ppermute | solution.py:445
  44.4 10.4 %collective-permute-start.10 = (bf16[320,512]{1,0:T(8,128)(2,1)S(1)}, bf16[320,512]{1,0:T(8,128)(2,1)S(1)}, u32[]{:S(2)}, u32[]{:S(2)}) collective-permute-start(bf16[320,512]{1,0:T(8,128)(2,1)S(1)} %get-tuple-element.21.refs_2_.refs_3_), channel_id=1, source_target_pairs={{0,30},{2,4},{4,2},{6,8},{8,6},{10,12},{12,10},{14,16},{16,14},{18... | collective-permute-start | bytes 983048 | tf_op jit(solution)/shard_map/ppermute | solution.py:427
  45.3 11.8 %collective-permute-start.8 = (bf16[320,512]{1,0:T(8,128)(2,1)S(1)}, bf16[320,512]{1,0:T(8,128)(2,1)S(1)}, u32[]{:S(2)}, u32[]{:S(2)}) collective-permute-start(bf16[320,512]{1,0:T(8,128)(2,1)S(1)} %get-tuple-element.21.refs_2_.refs_3_), channel_id=1, source_target_pairs={{0,2},{2,0},{4,6},{6,4},{8,10},{10,8},{12,14},{14,12},{16,18},{18,... | collective-permute-start | bytes 983048 | tf_op jit(solution)/shard_map/ppermute | solution.py:427
  48.5 8.6 %collective-permute-start.9 = (bf16[320,512]{1,0:T(8,128)(2,1)S(1)}, bf16[320,512]{1,0:T(8,128)(2,1)S(1)}, u32[]{:S(2)}, u32[]{:S(2)}) collective-permute-start(bf16[320,512]{1,0:T(8,128)(2,1)S(1)} %get-tuple-element.22.refs_3_.refs_4_), channel_id=1, source_target_pairs={{0,2},{2,0},{4,6},{6,4},{8,10},{10,8},{12,14},{14,12},{16,18},{18,... | collective-permute-start | bytes 983048 | tf_op jit(solution)/shard_map/ppermute | solution.py:427
  48.5 6.3 %collective-permute-start.18 = (f32[224,128]{1,0:T(8,128)S(1)}, f32[224,128]{1,0:T(8,128)S(1)}, u32[]{:S(2)}, u32[]{:S(2)}) collective-permute-start(f32[224,128]{1,0:T(8,128)S(1)} %add.40), channel_id=1, source_target_pairs={{0,8},{2,10},{4,12},{6,14},{8,0},{10,2},{12,4},{14,6},{16,24},{18,... | collective-permute-start | bytes 344072 | tf_op jit(solution)/shard_map/ppermute | solution.py:397
  53.9 14.5 %collective-permute-start.13 = (bf16[320,512]{1,0:T(8,128)(2,1)S(1)}, bf16[320,512]{1,0:T(8,128)(2,1)S(1)}, u32[]{:S(2)}, u32[]{:S(2)}) collective-permute-start(bf16[320,512]{1,0:T(8,128)(2,1)S(1)} %collective-permute-done.11.refs_7_), channel_id=1, source_target_pairs={{0,1},{1,0},{2,3},{3,2},{4,5},{5,4},{6,7},{7,6},{8,9},{9,8},{10,11... | collective-permute-start | bytes 983048 | tf_op jit(solution)/shard_map/ppermute | solution.py:447
  54.8 13.5 %collective-permute-start.14 = (bf16[320,512]{1,0:T(8,128)(2,1)}, bf16[320,512]{1,0:T(8,128)(2,1)S(1)}, u32[]{:S(2)}, u32[]{:S(2)}) collective-permute-start(bf16[320,512]{1,0:T(8,128)(2,1)} %collective-permute-done.12.refs_8_), channel_id=1, source_target_pairs={{0,2},{2,0},{4,6},{6,4},{8,10},{10,8},{12,14},{14,12},{16,18},{18,... | collective-permute-start | bytes 983048 | tf_op jit(solution)/shard_map/ppermute | solution.py:427
  54.9 9.1 %collective-permute-start.19 = (f32[224,128]{1,0:T(8,128)S(1)}, f32[224,128]{1,0:T(8,128)S(1)}, u32[]{:S(2)}, u32[]{:S(2)}) collective-permute-start(f32[224,128]{1,0:T(8,128)S(1)} %add.41.refs_0_), channel_id=1, source_target_pairs={{0,16},{2,18},{4,20},{6,22},{8,24},{10,26},{12,28},{14,30},{16,0},... | collective-permute-start | bytes 344072 | tf_op jit(solution)/shard_map/ppermute | solution.py:403
  64.0 4.3 %collective-permute-start.20 = (bf16[224,128]{1,0:T(8,128)(2,1)S(1)}, bf16[224,128]{1,0:T(8,128)(2,1)S(1)}, u32[]{:S(2)}, u32[]{:S(2)}) collective-permute-start(bf16[224,128]{1,0:T(8,128)(2,1)S(1)} %finish.1.refs_6_), channel_id=1, source_target_pairs={{0,4},{2,6},{4,0},{6,2},{8,12},{10,14},{12,8},{14,10},{16,20},{18,... | collective-permute-start | bytes 172040 | tf_op jit(solution)/shard_map/ppermute | solution.py:408
  66.1 2.2 %collective-permute-start.21 = (bf16[224,128]{1,0:T(8,128)(2,1)S(1)}, bf16[224,128]{1,0:T(8,128)(2,1)S(1)}, u32[]{:S(2)}, u32[]{:S(2)}) collective-permute-start(bf16[224,128]{1,0:T(8,128)(2,1)S(1)} %finish.1.refs_6_), channel_id=1, source_target_pairs={{0,2},{2,0},{4,6},{6,4},{8,10},{10,8},{12,14},{14,12},{16,18},{18,... | collective-permute-start | bytes 172040 | tf_op jit(solution)/shard_map/ppermute | solution.py:409
  68.3 1.2 %collective-permute-start.22 = (bf16[224,128]{1,0:T(8,128)(2,1)S(1)}, bf16[224,128]{1,0:T(8,128)(2,1)S(1)}, u32[]{:S(2)}, u32[]{:S(2)}) collective-permute-start(bf16[224,128]{1,0:T(8,128)(2,1)S(1)} %collective-permute-done.20.refs_7_), channel_id=1, source_target_pairs={{0,2},{2,0},{4,6},{6,4},{8,10},{10,8},{12,14},{14,12},{16,18},{18,... | collective-permute-start | bytes 172040 | tf_op jit(solution)/shard_map/ppermute | solution.py:409

commit v4 on v3

--- a/solution.py
+++ b/solution.py
@@ -395,6 +395,7 @@
     steps = exchanges("slab", 1, slabs, slabs) + exchanges("phase", 4, phases // 4, phases)
     for axis, perm in steps[:-1]:
         part = part + lax.ppermute(part, axis, perm)
+    late = part
     axis, perm = steps[-1]
     part = call(
         "finish",
@@ -409,7 +410,7 @@
     pieces += [lax.ppermute(piece, "phase", pair_on(phases)) for piece in pieces]
     spots = [2 * core + column, 2 * core + 1 - column]
     spots += [2 * (1 - core) + column, 2 * (1 - core) + 1 - column]
-    return pieces, jnp.stack(spots).astype(jnp.int32)
+    return pieces, jnp.stack(spots).astype(jnp.int32), late
 
 
 def local(phases, slabs, features, conv_weight, projection, grad_out, sens, mask):
@@ -562,7 +563,10 @@
     )
 
     (acc_back,) = conv_main("conv_back", True, main_grad)
-    pieces, spots = sum_over_mesh(keep, send, phases, slabs, [acc_back])
+    pieces, spots, late = sum_over_mesh(keep, send, phases, slabs, [acc_back])
+    for k in range(len(edges)):
+        value, _ = lax.optimization_barrier((main_grad[3 * depth_len + k], late))
+        corner_grad[2 * k + 1] = pass_phase(value, on)
     grad_features, grad_weight = call(
         "finish_both",
         functools.partial(final_body, corner_groups, flip),

time: 72.2 us -> 71.7 us (level)
    ppermute x2, waiting for transfers between devices: 3.64 us -> 7.91 us  [sum_over_mesh(): part = part + lax.ppermute(part, axis, perm)]
    ppermute x2, waiting for transfers between devices: 3.75 us -> 0.01 us  [halo(): slab_in = [lax.ppermute(own[edge[0]], 'slab', edge[2]) for edge in edges]]
    ppermute x1, starting transfers between devices: 2.22 us -> 1.31 us  [sum_over_mesh(): lax.ppermute(part, axis, perm)]
  transfers between devices with their start and end apart: 23 -> 23, of which waited for: 11 -> 10; matrix products, arithmetic and copies ran while one was open for 1% -> 1% of each run, Pallas kernels for 17% -> 18%
where the time goes in v4:
time: 71.7 us; the launch traced here: 71.4 us
  waiting for transfers between devices  27.5 us (38%)
  starting transfers between devices  21.7 us (30%)
  Pallas kernels  19.8 us (28%)
  local copies, waits for them, and re-layouts  1.25 us (2%)
  between operations  0.84 us (1%)
    pallas_call x9, Pallas kernels, call(): pl.pallas_call(run, out_shape=outs, in_specs=[SPECS[kind] for kind in kin...  19.8 us
    ppermute x10, starting transfers between devices, pass_phase(): return lax.ppermute(value, 'phase', perm)  8.84 us
    ppermute x2, waiting for transfers between devices, sum_over_mesh(): part = part + lax.ppermute(part, axis, perm)  7.91 us
    ppermute x2, starting transfers between devices, halo(): slab_in = [lax.ppermute(own[edge[0]], 'slab', edge[2]) for edge in edges]  4.55 us
    ppermute x2, waiting for transfers between devices, halo(): lax.ppermute(off_in[edge[0]], 'slab', edge[2])  3.77 us
    ppermute x1, waiting for transfers between devices, sum_over_mesh(): lax.ppermute(part, axis, perm)  2.89 us
    ppermute x1, waiting for transfers between devices, sum_over_mesh(): part = part + lax.ppermute(other, 'phase', across)  2.88 us
    ppermute x10, waiting for transfers between devices, pass_phase(): return lax.ppermute(value, 'phase', perm)  2.83 us
  transfers between devices with their start and end apart: 23, of which 10 were waited for; matrix products, arithmetic and copies ran while one was open for 1% of the time, Pallas kernels for 18%

profile of v4, /device:TPU:0, one launch (start us, length us, event | category | flops | bytes accessed | tf_op | source)
XLA Modules:
  0.0 71.4 jit_solution(8386173633485283417)
XLA Ops:
  0.7 1.1 %dynamic-slice_bitcast_fusion = (bf16[320,512]{1,0:T(8,128)(2,1)S(1)}, bf16[320,512]{1,0:T(8,128)(2,1)S(1)}) fusion(bf16[1,2,320,512]{3,2,1,0:T(8,128)(2,1)} %param.8, s32[]{:T(128)S(6)} %select_n.28, s32[]{:T(128)S(6)} %select_n.27), kind=kLoop, calls=%fused_computation | loop fusion | bytes 1310728 | tf_op jit(solution)/shard_map/jit(dynamic_index_in_dim)/squeeze | solution.py:487
  1.8 3.0 %collective-permute-start.5 = (bf16[320,512]{1,0:T(8,128)(2,1)S(1)}, bf16[320,512]{1,0:T(8,128)(2,1)S(1)}, u32[]{:S(2)}, u32[]{:S(2)}) collective-permute-start(bf16[320,512]{1,0:T(8,128)(2,1)S(1)} %get-tuple-element.33.refs_3_), channel_id=1, source_target_pairs={{0,1},{1,0},{2,3},{3,2},{4,5},{5,4},{6,7},{7,6},{8,9},{9,8},{10,11... | collective-permute-start | bytes 983048 | tf_op jit(solution)/shard_map/ppermute | solution.py:446
  4.8 4.6 %collective-permute-start.4 = (bf16[320,512]{1,0:T(8,128)(2,1)S(1)}, bf16[320,512]{1,0:T(8,128)(2,1)S(1)}, u32[]{:S(2)}, u32[]{:S(2)}) collective-permute-start(bf16[320,512]{1,0:T(8,128)(2,1)S(1)} %get-tuple-element.33.refs_3_), channel_id=1, source_target_pairs={{0,30},{2,4},{4,2},{6,8},{8,6},{10,12},{12,10},{14,16},{16,14},{18... | collective-permute-start | bytes 983048 | tf_op jit(solution)/shard_map/ppermute | solution.py:428
  9.5 0.0 collective-permute-start
  9.5 0.6 collective-permute-start.3
  10.1 0.1 multiply_negate_fusion
  10.2 0.0 copy-start.3
  10.2 0.1 neg.8
  10.3 3.5 %coil_forward.1 = (f32[256,640]{1,0:T(8,128)S(1)}, bf16[256,640]{1,0:T(8,128)(2,1)}) custom-call(f32[2,2,8,320]{3,2,1,0:T(8,128)S(1)} %bitcast.17, f32[2,16,2,8,320]{4,3,2,1,0:T(8,128)} %refs_1_.6, bf16[640,640]{1,0:T(8,128)(2,1)} %constant.54.clone.refs_2_.refs_3_, bf16[640,640]{1,0:T(8,128)(2,1)} %constant.55.clone.refs_3_.refs_4_), custom_call_target="tpu_custom_call" | custom-call | flops 629145600 | bytes 4000000 | tf_op jit(solution)/shard_map/coil_forward/pallas_call | solution.py:34
  13.8 0.0 collective-permute-done.1.refs_5_
  13.8 0.0 collective-permute-done.refs_4_
  13.8 0.5 collective-permute-start.2
  14.3 0.0 collective-permute-done.5.refs_8_.refs_5_
  14.3 0.1 collective-permute-start.7
  14.4 0.0 collective-permute-done.4.refs_7_
  14.4 1.6 %collective-permute-start.6 = (bf16[320,512]{1,0:T(8,128)(2,1)S(1)}, bf16[320,512]{1,0:T(8,128)(2,1)S(1)}, u32[]{:S(2)}, u32[]{:S(2)}) collective-permute-start(bf16[320,512]{1,0:T(8,128)(2,1)S(1)} %collective-permute-done.4.refs_7_), channel_id=1, source_target_pairs={{0,1},{1,0},{2,3},{3,2},{4,5},{5,4},{6,7},{7,6},{8,9},{9,8},{10,11... | collective-permute-start | bytes 983048 | tf_op jit(solution)/shard_map/ppermute | solution.py:448
  16.0 0.1 pad_add_fusion.refs_0_
  16.1 2.8 %collective-permute-done.3.refs_6_ = bf16[320,512]{1,0:T(8,128)(2,1)} collective-permute-done((bf16[320,512]{1,0:T(8,128)(2,1)S(1)}, bf16[320,512]{1,0:T(8,128)(2,1)}, u32[]{:S(2)}, u32[]{:S(2)}) %collective-permute-start.3) | collective-permute-done | bytes 327712 | tf_op jit(solution)/shard_map/ppermute | solution.py:428
  18.9 3.3 %conv_act.1 = (f32[2,320,512]{2,1,0:T(8,128)S(1)}, bf16[768,1280]{1,0:T(8,128)(2,1)S(1)}) custom-call(s32[2]{0:T(128)S(1)} %pad_add_fusion.refs_0_, bf16[27,64,64]{2,1,0:T(8,128)(2,1)S(1)} %copy-done.3, bf16[320,512]{1,0:T(8,128)(2,1)S(1)} %get-tuple-element.34.refs_2_, bf16[320,512]{1,0:T(8,128)(2,1)S(1)} %get-tuple-element.33.refs_3_, ...), custom_call_target="tpu_custom_call" | custom-call | flops 1761607680 | bytes 5000000 | tf_op jit(solution)/shard_map/conv_act/pallas_call | solution.py:34
  22.2 2.4 %collective-permute-done.2.refs_6_ = bf16[256,640]{1,0:T(8,128)(2,1)S(1)} collective-permute-done((bf16[256,640]{1,0:T(8,128)(2,1)}, bf16[256,640]{1,0:T(8,128)(2,1)S(1)}, u32[]{:S(2)}, u32[]{:S(2)}) %collective-permute-start.2) | collective-permute-done | bytes 327712 | tf_op jit(solution)/shard_map/ppermute | solution.py:491
  24.6 2.1 %coil_back.1.refs_2_ = f32[2,2,8,320]{3,2,1,0:T(8,128)} custom-call(f32[2,2,8,320]{3,2,1,0:T(8,128)S(1)} %bitcast.18, f32[2,16,2,8,320]{4,3,2,1,0:T(8,128)S(1)} %copy-done.2, s32[4,320]{1,0:T(4,128)S(1)} %bitcast.19, bf16[640,640]{1,0:T(8,128)(2,1)S(1)} %copy-done, bf16[640,640]{1,0:T(8,128)(2,1)S(1)} %copy-done.1, ...), custom_call_target="tpu_custom_call" | custom-call | flops 629145600 | bytes 5000000 | tf_op jit(solution)/shard_map/coil_back/pallas_call | solution.py:34
  26.8 3.8 %collective-permute-done.6.refs_6_ = bf16[320,512]{1,0:T(8,128)(2,1)S(1)} collective-permute-done((bf16[320,512]{1,0:T(8,128)(2,1)S(1)}, bf16[320,512]{1,0:T(8,128)(2,1)S(1)}, u32[]{:S(2)}, u32[]{:S(2)}) %collective-permute-start.6) | collective-permute-done | bytes 327712 | tf_op jit(solution)/shard_map/ppermute | solution.py:448
  30.5 1.9 %grad_act.1 = (bf16[320,512]{1,0:T(8,128)(2,1)S(1)}, bf16[320,512]{1,0:T(8,128)(2,1)S(1)}, bf16[384,1280]{1,0:T(8,128)(2,1)S(1)}) custom-call(s32[2]{0:T(128)S(1)} %pad_add_fusion.refs_0_, f32[2,320,512]{2,1,0:T(8,128)S(1)} %get-tuple-element.21.refs_7_.refs_1_, f32[2,2,8,320]{3,2,1,0:T(8,128)} %coil_back.1.refs_2_, ...), custom_call_target="tpu_custom_call" | custom-call | flops 251658240 | bytes 4000000 | tf_op jit(solution)/shard_map/grad_act/pallas_call | solution.py:34
  32.4 3.1 %grad_weight.1 = (f32[448,128]{1,0:T(8,128)S(1)}, f32[448,128]{1,0:T(8,128)S(1)}) custom-call(s32[2]{0:T(128)S(1)} %pad_add_fusion.refs_0_, bf16[768,1280]{1,0:T(8,128)(2,1)S(1)} %get-tuple-element.24.refs_1_, bf16[384,1280]{1,0:T(8,128)(2,1)S(1)} %get-tuple-element.25.refs_2_, bf16[320,512]{1,0:T(8,128)(2,1)S(1)} %get-tuple-element.22.refs_2_.refs_3_, ...), custom_call_target="tpu_custom_call" | custom-call | flops 1761607680 | bytes 5000000 | tf_op jit(solution)/shard_map/grad_weight/pallas_call | solution.py:34
  35.5 0.1 collective-permute-start.14
  35.6 1.4 %collective-permute-done.14.refs_2_ = f32[448,128]{1,0:T(8,128)S(1)} collective-permute-done((f32[448,128]{1,0:T(8,128)S(1)}, f32[448,128]{1,0:T(8,128)S(1)}, u32[]{:S(2)}, u32[]{:S(2)}) %collective-permute-start.14) | collective-permute-done | bytes 229408 | tf_op jit(solution)/shard_map/ppermute | solution.py:390
  37.1 0.1 collective-permute-start.15
  37.1 2.3 %collective-permute-start.11 = (bf16[320,512]{1,0:T(8,128)(2,1)S(1)}, bf16[320,512]{1,0:T(8,128)(2,1)S(1)}, u32[]{:S(2)}, u32[]{:S(2)}) collective-permute-start(bf16[320,512]{1,0:T(8,128)(2,1)S(1)} %get-tuple-element.23.refs_3_.refs_4_), channel_id=1, source_target_pairs={{0,30},{2,4},{4,2},{6,8},{8,6},{10,12},{12,10},{14,16},{16,14},{18... | collective-permute-start | bytes 983048 | tf_op jit(solution)/shard_map/ppermute | solution.py:428
  39.4 2.9 %collective-permute-done.15 = f32[224,128]{1,0:T(8,128)S(1)} collective-permute-done((f32[224,128]{1,0:T(8,128)S(1)}, f32[224,128]{1,0:T(8,128)S(1)}, u32[]{:S(2)}, u32[]{:S(2)}) %collective-permute-start.15) | collective-permute-done | bytes 114720 | tf_op jit(solution)/shard_map/ppermute | solution.py:394
  42.3 0.6 collective-permute-start.16
  42.9 1.5 %collective-permute-start.12 = (bf16[320,512]{1,0:T(8,128)(2,1)S(1)}, bf16[320,512]{1,0:T(8,128)(2,1)}, u32[]{:S(2)}, u32[]{:S(2)}) collective-permute-start(bf16[320,512]{1,0:T(8,128)(2,1)S(1)} %get-tuple-element.23.refs_3_.refs_4_), channel_id=1, source_target_pairs={{0,1},{1,0},{2,3},{3,2},{4,5},{5,4},{6,7},{7,6},{8,9},{9,8},{10,11... | collective-permute-start | bytes 983048 | tf_op jit(solution)/shard_map/ppermute | solution.py:446
  44.4 0.8 %collective-permute-start.10 = (bf16[320,512]{1,0:T(8,128)(2,1)S(1)}, bf16[320,512]{1,0:T(8,128)(2,1)S(1)}, u32[]{:S(2)}, u32[]{:S(2)}) collective-permute-start(bf16[320,512]{1,0:T(8,128)(2,1)S(1)} %get-tuple-element.22.refs_2_.refs_3_), channel_id=1, source_target_pairs={{0,30},{2,4},{4,2},{6,8},{8,6},{10,12},{12,10},{14,16},{16,14},{18... | collective-permute-start | bytes 983048 | tf_op jit(solution)/shard_map/ppermute | solution.py:428
  45.3 0.0 collective-permute-start.8
  45.3 3.2 %collective-permute-done.16 = f32[224,128]{1,0:T(8,128)S(1)} collective-permute-done((f32[224,128]{1,0:T(8,128)S(1)}, f32[224,128]{1,0:T(8,128)S(1)}, u32[]{:S(2)}, u32[]{:S(2)}) %collective-permute-start.16) | collective-permute-done | bytes 114720 | tf_op jit(solution)/shard_map/ppermute | solution.py:397
  48.5 0.0 collective-permute-start.9
  48.5 0.0 collective-permute-done.11.refs_7_
  48.5 1.6 %collective-permute-start.17 = (f32[224,128]{1,0:T(8,128)S(1)}, f32[224,128]{1,0:T(8,128)S(1)}, u32[]{:S(2)}, u32[]{:S(2)}) collective-permute-start(f32[224,128]{1,0:T(8,128)S(1)} %add.36), channel_id=1, source_target_pairs={{0,8},{2,10},{4,12},{6,14},{8,0},{10,2},{12,4},{14,6},{16,24},{18,... | collective-permute-start | bytes 344072 | tf_op jit(solution)/shard_map/ppermute | solution.py:397
  50.1 4.7 %collective-permute-done.17 = f32[224,128]{1,0:T(8,128)S(1)} collective-permute-done((f32[224,128]{1,0:T(8,128)S(1)}, f32[224,128]{1,0:T(8,128)S(1)}, u32[]{:S(2)}, u32[]{:S(2)}) %collective-permute-start.17) | collective-permute-done | bytes 114720 | tf_op jit(solution)/shard_map/ppermute | solution.py:397
  54.8 0.5 collective-permute-start.13
  55.4 1.3 %collective-permute-start.19 = (f32[224,128]{1,0:T(8,128)S(1)}, f32[224,128]{1,0:T(8,128)S(1)}, u32[]{:S(2)}, u32[]{:S(2)}) collective-permute-start(f32[224,128]{1,0:T(8,128)S(1)} %add.37.refs_0_), channel_id=1, source_target_pairs={{0,16},{2,18},{4,20},{6,22},{8,24},{10,26},{12,28},{14,30},{16,0},... | collective-permute-start | bytes 344072 | tf_op jit(solution)/shard_map/ppermute | solution.py:404
  56.7 0.4 collective-permute-start.18
  57.1 3.6 %conv_back.1.refs_2_.refs_1_ = f32[2,320,512]{2,1,0:T(8,128)S(1)} custom-call(s32[2]{0:T(128)S(1)} %pad_add_fusion.refs_0_, bf16[27,64,64]{2,1,0:T(8,128)(2,1)S(1)} %copy-done.3, bf16[320,512]{1,0:T(8,128)(2,1)S(1)} %get-tuple-element.22.refs_2_.refs_3_, bf16[320,512]{1,0:T(8,128)(2,1)S(1)} %get-tuple-element.23.refs_3_.refs_4_, ...), custom_call_target="tpu_custom_call" | custom-call | flops 1761607680 | bytes 5000000 | tf_op jit(solution)/shard_map/conv_back/pallas_call | solution.py:34
  60.6 2.9 %collective-permute-done.19.refs_1_ = f32[224,128]{1,0:T(8,128)S(1)} collective-permute-done((f32[224,128]{1,0:T(8,128)S(1)}, f32[224,128]{1,0:T(8,128)S(1)}, u32[]{:S(2)}, u32[]{:S(2)}) %collective-permute-start.19) | collective-permute-done | bytes 114720 | tf_op jit(solution)/shard_map/ppermute | solution.py:404
  63.5 2.1 %collective-permute-start.20 = (bf16[224,128]{1,0:T(8,128)(2,1)S(1)}, bf16[224,128]{1,0:T(8,128)(2,1)S(1)}, u32[]{:S(2)}, u32[]{:S(2)}) collective-permute-start(bf16[224,128]{1,0:T(8,128)(2,1)S(1)} %finish.1.refs_6_), channel_id=1, source_target_pairs={{0,4},{2,6},{4,0},{6,2},{8,12},{10,14},{12,8},{14,10},{16,20},{18,... | collective-permute-start | bytes 172040 | tf_op jit(solution)/shard_map/ppermute | solution.py:409
  65.6 2.2 %collective-permute-done.20.refs_7_ = bf16[224,128]{1,0:T(8,128)(2,1)S(1)} collective-permute-done((bf16[224,128]{1,0:T(8,128)(2,1)S(1)}, bf16[224,128]{1,0:T(8,128)(2,1)S(1)}, u32[]{:S(2)}, u32[]{:S(2)}) %collective-permute-start.20) | collective-permute-done | bytes 57376 | tf_op jit(solution)/shard_map/ppermute | solution.py:409
  67.8 0.1 pad_add_fusion.1.refs_5_
  67.9 1.2 %collective-permute-done.22.refs_9_ = bf16[224,128]{1,0:T(8,128)(2,1)S(1)} collective-permute-done((bf16[224,128]{1,0:T(8,128)(2,1)S(1)}, bf16[224,128]{1,0:T(8,128)(2,1)S(1)}, u32[]{:S(2)}, u32[]{:S(2)}) %collective-permute-start.22) | collective-permute-done | bytes 57376 | tf_op jit(solution)/shard_map/ppermute | solution.py:410
  69.0 2.3 %finish_both.1 = (bf16[2,320,512]{2,1,0:T(8,128)(2,1)}, f32[27,64,64]{2,1,0:T(8,128)}) custom-call(s32[2]{0:T(128)S(1)} %pad_add_fusion.refs_0_, f32[2,320,512]{2,1,0:T(8,128)S(1)} %conv_back.1.refs_2_.refs_1_, bf16[27,64,64]{2,1,0:T(8,128)(2,1)S(1)} %copy-done.3, bf16[320,512]{1,0:T(8,128)(2,1)S(1)} %collective-permute-done.13.refs_3_, ...), custom_call_target="tpu_custom_call" | custom-call | flops 251658240 | bytes 4000000 | tf_op jit(solution)/shard_map/finish_both/pallas_call | solution.py:34
  (31 shorter events, 0.1 us)
Async XLA Ops:
  0.6 9.5 %copy-start.6 = (bf16[2,64]{1,0:T(2,128)(2,1)S(1)}, bf16[2,64]{1,0:T(2,128)(2,1)}, u32[]{:S(2)}) copy-start(bf16[2,64]{1,0:T(2,128)(2,1)} %param.10) | copy-start | bytes 772
  0.6 9.7 %copy-start.4 = (f32[1,2,2,8,320]{4,3,2,1,0:T(8,128)S(1)}, f32[1,2,2,8,320]{4,3,2,1,0:T(8,128)}, u32[]{:S(2)}) copy-start(f32[1,2,2,8,320]{4,3,2,1,0:T(8,128)} %param.11) | copy-start | bytes 122884
  1.8 12.5 %collective-permute-start.5 = (bf16[320,512]{1,0:T(8,128)(2,1)S(1)}, bf16[320,512]{1,0:T(8,128)(2,1)S(1)}, u32[]{:S(2)}, u32[]{:S(2)}) collective-permute-start(bf16[320,512]{1,0:T(8,128)(2,1)S(1)} %get-tuple-element.33.refs_3_), channel_id=1, source_target_pairs={{0,1},{1,0},{2,3},{3,2},{4,5},{5,4},{6,7},{7,6},{8,9},{9,8},{10,11... | collective-permute-start | bytes 983048 | tf_op jit(solution)/shard_map/ppermute | solution.py:446
  4.8 9.0 %collective-permute-start.1 = (bf16[320,512]{1,0:T(8,128)(2,1)S(1)}, bf16[320,512]{1,0:T(8,128)(2,1)S(1)}, u32[]{:S(2)}, u32[]{:S(2)}) collective-permute-start(bf16[320,512]{1,0:T(8,128)(2,1)S(1)} %get-tuple-element.33.refs_3_), channel_id=1, source_target_pairs={{0,2},{2,0},{4,6},{6,4},{8,10},{10,8},{12,14},{14,12},{16,18},{18,... | collective-permute-start | bytes 983048 | tf_op jit(solution)/shard_map/ppermute | solution.py:428
  4.8 9.6 %collective-permute-start.4 = (bf16[320,512]{1,0:T(8,128)(2,1)S(1)}, bf16[320,512]{1,0:T(8,128)(2,1)S(1)}, u32[]{:S(2)}, u32[]{:S(2)}) collective-permute-start(bf16[320,512]{1,0:T(8,128)(2,1)S(1)} %get-tuple-element.33.refs_3_), channel_id=1, source_target_pairs={{0,30},{2,4},{4,2},{6,8},{8,6},{10,12},{12,10},{14,16},{16,14},{18... | collective-permute-start | bytes 983048 | tf_op jit(solution)/shard_map/ppermute | solution.py:428
  9.5 4.3 %collective-permute-start = (bf16[320,512]{1,0:T(8,128)(2,1)S(1)}, bf16[320,512]{1,0:T(8,128)(2,1)S(1)}, u32[]{:S(2)}, u32[]{:S(2)}) collective-permute-start(bf16[320,512]{1,0:T(8,128)(2,1)S(1)} %get-tuple-element.34.refs_2_), channel_id=1, source_target_pairs={{0,2},{2,0},{4,6},{6,4},{8,10},{10,8},{12,14},{14,12},{16,18},{18,... | collective-permute-start | bytes 983048 | tf_op jit(solution)/shard_map/ppermute | solution.py:428
  9.5 9.4 %collective-permute-start.3 = (bf16[320,512]{1,0:T(8,128)(2,1)S(1)}, bf16[320,512]{1,0:T(8,128)(2,1)}, u32[]{:S(2)}, u32[]{:S(2)}) collective-permute-start(bf16[320,512]{1,0:T(8,128)(2,1)S(1)} %get-tuple-element.34.refs_2_), channel_id=1, source_target_pairs={{0,30},{2,4},{4,2},{6,8},{8,6},{10,12},{12,10},{14,16},{16,14},{18... | collective-permute-start | bytes 983048 | tf_op jit(solution)/shard_map/ppermute | solution.py:428
  10.2 8.7 %copy-start.3 = (bf16[27,64,64]{2,1,0:T(8,128)(2,1)S(1)}, bf16[27,64,64]{2,1,0:T(8,128)(2,1)}, u32[]{:S(2)}) copy-start(bf16[27,64,64]{2,1,0:T(8,128)(2,1)} %refs_2_.2) | copy-start | bytes 663556
  13.8 10.8 %collective-permute-start.2 = (bf16[256,640]{1,0:T(8,128)(2,1)}, bf16[256,640]{1,0:T(8,128)(2,1)S(1)}, u32[]{:S(2)}, u32[]{:S(2)}) collective-permute-start(bf16[256,640]{1,0:T(8,128)(2,1)} %get-tuple-element.20), channel_id=1, source_target_pairs={{0,1},{1,0},{2,3},{3,2},{4,5},{5,4},{6,7},{7,6},{8,9},{9,8},{10,11... | collective-permute-start | bytes 983048 | tf_op jit(solution)/shard_map/ppermute | solution.py:491
  14.3 12.4 %collective-permute-start.7 = (bf16[320,512]{1,0:T(8,128)(2,1)S(1)}, bf16[320,512]{1,0:T(8,128)(2,1)S(1)}, u32[]{:S(2)}, u32[]{:S(2)}) collective-permute-start(bf16[320,512]{1,0:T(8,128)(2,1)S(1)} %collective-permute-done.5.refs_8_.refs_5_), channel_id=1, source_target_pairs={{0,2},{2,0},{4,6},{6,4},{8,10},{10,8},{12,14},{14,12},{16,18},{18,... | collective-permute-start | bytes 983048 | tf_op jit(solution)/shard_map/ppermute | solution.py:428
  14.4 16.1 %collective-permute-start.6 = (bf16[320,512]{1,0:T(8,128)(2,1)S(1)}, bf16[320,512]{1,0:T(8,128)(2,1)S(1)}, u32[]{:S(2)}, u32[]{:S(2)}) collective-permute-start(bf16[320,512]{1,0:T(8,128)(2,1)S(1)} %collective-permute-done.4.refs_7_), channel_id=1, source_target_pairs={{0,1},{1,0},{2,3},{3,2},{4,5},{5,4},{6,7},{7,6},{8,9},{9,8},{10,11... | collective-permute-start | bytes 983048 | tf_op jit(solution)/shard_map/ppermute | solution.py:448
  16.1 8.5 %copy-start = (bf16[640,640]{1,0:T(8,128)(2,1)S(1)}, bf16[640,640]{1,0:T(8,128)(2,1)}, u32[]{:S(2)}) copy-start(bf16[640,640]{1,0:T(8,128)(2,1)} %constant.54.clone.refs_2_.refs_3_) | copy-start | bytes 2457604
  16.1 8.5 %copy-start.1 = (bf16[640,640]{1,0:T(8,128)(2,1)S(1)}, bf16[640,640]{1,0:T(8,128)(2,1)}, u32[]{:S(2)}) copy-start(bf16[640,640]{1,0:T(8,128)(2,1)} %constant.55.clone.refs_3_.refs_4_) | copy-start | bytes 2457604
  16.1 8.5 %copy-start.2 = (f32[2,16,2,8,320]{4,3,2,1,0:T(8,128)S(1)}, f32[2,16,2,8,320]{4,3,2,1,0:T(8,128)}, u32[]{:S(2)}) copy-start(f32[2,16,2,8,320]{4,3,2,1,0:T(8,128)} %refs_1_.6) | copy-start | bytes 1966084
  16.1 8.6 %copy-start.5 = (s32[1,4,320]{2,1,0:T(4,128)S(1)}, s32[1,4,320]{2,1,0:T(4,128)}, u32[]{:S(2)}) copy-start(s32[1,4,320]{2,1,0:T(4,128)} %param.13) | copy-start | bytes 15364
  35.5 1.6 %collective-permute-start.14 = (f32[448,128]{1,0:T(8,128)S(1)}, f32[448,128]{1,0:T(8,128)S(1)}, u32[]{:S(2)}, u32[]{:S(2)}) collective-permute-start(f32[448,128]{1,0:T(8,128)S(1)} %get-tuple-element.27), channel_id=1, source_target_pairs={{0,2},{2,0},{4,6},{6,4},{8,10},{10,8},{12,14},{14,12},{16,18},{18,... | collective-permute-start | bytes 688136 | tf_op jit(solution)/shard_map/ppermute | solution.py:390
  37.1 5.3 %collective-permute-start.15 = (f32[224,128]{1,0:T(8,128)S(1)}, f32[224,128]{1,0:T(8,128)S(1)}, u32[]{:S(2)}, u32[]{:S(2)}) collective-permute-start(f32[224,128]{1,0:T(8,128)S(1)} %get-tuple-element.29), channel_id=1, source_target_pairs={{0,4},{2,6},{4,0},{6,2},{8,12},{10,14},{12,8},{14,10},{16,20},{18,... | collective-permute-start | bytes 344072 | tf_op jit(solution)/shard_map/ppermute | solution.py:394
  37.1 11.4 %collective-permute-start.11 = (bf16[320,512]{1,0:T(8,128)(2,1)S(1)}, bf16[320,512]{1,0:T(8,128)(2,1)S(1)}, u32[]{:S(2)}, u32[]{:S(2)}) collective-permute-start(bf16[320,512]{1,0:T(8,128)(2,1)S(1)} %get-tuple-element.23.refs_3_.refs_4_), channel_id=1, source_target_pairs={{0,30},{2,4},{4,2},{6,8},{8,6},{10,12},{12,10},{14,16},{16,14},{18... | collective-permute-start | bytes 983048 | tf_op jit(solution)/shard_map/ppermute | solution.py:428
  42.3 6.1 %collective-permute-start.16 = (f32[224,128]{1,0:T(8,128)S(1)}, f32[224,128]{1,0:T(8,128)S(1)}, u32[]{:S(2)}, u32[]{:S(2)}) collective-permute-start(f32[224,128]{1,0:T(8,128)S(1)} %add.35), channel_id=1, source_target_pairs={{0,1},{1,0},{2,3},{3,2},{4,5},{5,4},{6,7},{7,6},{8,9},{9,8},{10,11... | collective-permute-start | bytes 344072 | tf_op jit(solution)/shard_map/ppermute | solution.py:397
  42.9 12.5 %collective-permute-start.12 = (bf16[320,512]{1,0:T(8,128)(2,1)S(1)}, bf16[320,512]{1,0:T(8,128)(2,1)}, u32[]{:S(2)}, u32[]{:S(2)}) collective-permute-start(bf16[320,512]{1,0:T(8,128)(2,1)S(1)} %get-tuple-element.23.refs_3_.refs_4_), channel_id=1, source_target_pairs={{0,1},{1,0},{2,3},{3,2},{4,5},{5,4},{6,7},{7,6},{8,9},{9,8},{10,11... | collective-permute-start | bytes 983048 | tf_op jit(solution)/shard_map/ppermute | solution.py:446
  44.4 12.3 %collective-permute-start.10 = (bf16[320,512]{1,0:T(8,128)(2,1)S(1)}, bf16[320,512]{1,0:T(8,128)(2,1)S(1)}, u32[]{:S(2)}, u32[]{:S(2)}) collective-permute-start(bf16[320,512]{1,0:T(8,128)(2,1)S(1)} %get-tuple-element.22.refs_2_.refs_3_), channel_id=1, source_target_pairs={{0,30},{2,4},{4,2},{6,8},{8,6},{10,12},{12,10},{14,16},{16,14},{18... | collective-permute-start | bytes 983048 | tf_op jit(solution)/shard_map/ppermute | solution.py:428
  45.3 11.8 %collective-permute-start.8 = (bf16[320,512]{1,0:T(8,128)(2,1)S(1)}, bf16[320,512]{1,0:T(8,128)(2,1)S(1)}, u32[]{:S(2)}, u32[]{:S(2)}) collective-permute-start(bf16[320,512]{1,0:T(8,128)(2,1)S(1)} %get-tuple-element.22.refs_2_.refs_3_), channel_id=1, source_target_pairs={{0,2},{2,0},{4,6},{6,4},{8,10},{10,8},{12,14},{14,12},{16,18},{18,... | collective-permute-start | bytes 983048 | tf_op jit(solution)/shard_map/ppermute | solution.py:428
  48.5 8.6 %collective-permute-start.9 = (bf16[320,512]{1,0:T(8,128)(2,1)S(1)}, bf16[320,512]{1,0:T(8,128)(2,1)S(1)}, u32[]{:S(2)}, u32[]{:S(2)}) collective-permute-start(bf16[320,512]{1,0:T(8,128)(2,1)S(1)} %get-tuple-element.23.refs_3_.refs_4_), channel_id=1, source_target_pairs={{0,2},{2,0},{4,6},{6,4},{8,10},{10,8},{12,14},{14,12},{16,18},{18,... | collective-permute-start | bytes 983048 | tf_op jit(solution)/shard_map/ppermute | solution.py:428
  48.5 6.3 %collective-permute-start.17 = (f32[224,128]{1,0:T(8,128)S(1)}, f32[224,128]{1,0:T(8,128)S(1)}, u32[]{:S(2)}, u32[]{:S(2)}) collective-permute-start(f32[224,128]{1,0:T(8,128)S(1)} %add.36), channel_id=1, source_target_pairs={{0,8},{2,10},{4,12},{6,14},{8,0},{10,2},{12,4},{14,6},{16,24},{18,... | collective-permute-start | bytes 344072 | tf_op jit(solution)/shard_map/ppermute | solution.py:397
  54.8 13.0 %collective-permute-start.13 = (bf16[320,512]{1,0:T(8,128)(2,1)S(1)}, bf16[320,512]{1,0:T(8,128)(2,1)S(1)}, u32[]{:S(2)}, u32[]{:S(2)}) collective-permute-start(bf16[320,512]{1,0:T(8,128)(2,1)S(1)} %collective-permute-done.11.refs_7_), channel_id=1, source_target_pairs={{0,1},{1,0},{2,3},{3,2},{4,5},{5,4},{6,7},{7,6},{8,9},{9,8},{10,11... | collective-permute-start | bytes 983048 | tf_op jit(solution)/shard_map/ppermute | solution.py:448
  55.4 8.1 %collective-permute-start.19 = (f32[224,128]{1,0:T(8,128)S(1)}, f32[224,128]{1,0:T(8,128)S(1)}, u32[]{:S(2)}, u32[]{:S(2)}) collective-permute-start(f32[224,128]{1,0:T(8,128)S(1)} %add.37.refs_0_), channel_id=1, source_target_pairs={{0,16},{2,18},{4,20},{6,22},{8,24},{10,26},{12,28},{14,30},{16,0},... | collective-permute-start | bytes 344072 | tf_op jit(solution)/shard_map/ppermute | solution.py:404
  56.7 12.3 %collective-permute-start.18 = (bf16[320,512]{1,0:T(8,128)(2,1)}, bf16[320,512]{1,0:T(8,128)(2,1)S(1)}, u32[]{:S(2)}, u32[]{:S(2)}) collective-permute-start(bf16[320,512]{1,0:T(8,128)(2,1)} %collective-permute-done.12.refs_8_), channel_id=1, source_target_pairs={{0,2},{2,0},{4,6},{6,4},{8,10},{10,8},{12,14},{14,12},{16,18},{18,... | collective-permute-start | bytes 983048 | tf_op jit(solution)/shard_map/ppermute | solution.py:428
  63.5 4.2 %collective-permute-start.20 = (bf16[224,128]{1,0:T(8,128)(2,1)S(1)}, bf16[224,128]{1,0:T(8,128)(2,1)S(1)}, u32[]{:S(2)}, u32[]{:S(2)}) collective-permute-start(bf16[224,128]{1,0:T(8,128)(2,1)S(1)} %finish.1.refs_6_), channel_id=1, source_target_pairs={{0,4},{2,6},{4,0},{6,2},{8,12},{10,14},{12,8},{14,10},{16,20},{18,... | collective-permute-start | bytes 172040 | tf_op jit(solution)/shard_map/ppermute | solution.py:409
  65.6 2.3 %collective-permute-start.21 = (bf16[224,128]{1,0:T(8,128)(2,1)S(1)}, bf16[224,128]{1,0:T(8,128)(2,1)S(1)}, u32[]{:S(2)}, u32[]{:S(2)}) collective-permute-start(bf16[224,128]{1,0:T(8,128)(2,1)S(1)} %finish.1.refs_6_), channel_id=1, source_target_pairs={{0,2},{2,0},{4,6},{6,4},{8,10},{10,8},{12,14},{14,12},{16,18},{18,... | collective-permute-start | bytes 172040 | tf_op jit(solution)/shard_map/ppermute | solution.py:410
  67.8 1.2 %collective-permute-start.22 = (bf16[224,128]{1,0:T(8,128)(2,1)S(1)}, bf16[224,128]{1,0:T(8,128)(2,1)S(1)}, u32[]{:S(2)}, u32[]{:S(2)}) collective-permute-start(bf16[224,128]{1,0:T(8,128)(2,1)S(1)} %collective-permute-done.20.refs_7_), channel_id=1, source_target_pairs={{0,2},{2,0},{4,6},{6,4},{8,10},{10,8},{12,14},{14,12},{16,18},{18,... | collective-permute-start | bytes 172040 | tf_op jit(solution)/shard_map/ppermute | solution.py:410

commit v5 on v4

--- a/solution.py
+++ b/solution.py
@@ -13,7 +13,7 @@
 F32, BF16 = jnp.float32, jnp.bfloat16
 VMEM = pl.BlockSpec(memory_space=pltpu.VMEM)
 SMEM = pl.BlockSpec(memory_space=pltpu.SMEM)
-LIMIT = 48 * 1024 * 1024
+LIMIT = 32 * 1024 * 1024
 LANES = 128
 
 

time: 71.7 us -> 71.7 us (level)
  no operation moved by 1% of the time
where the time goes in v5:
time: 71.7 us; the launch traced here: 71.4 us
  waiting for transfers between devices  27.5 us (38%)
  starting transfers between devices  21.7 us (30%)
  Pallas kernels  19.8 us (28%)
  local copies, waits for them, and re-layouts  1.25 us (2%)
  between operations  0.84 us (1%)
    pallas_call x9, Pallas kernels, call(): pl.pallas_call(run, out_shape=outs, in_specs=[SPECS[kind] for kind in kin...  19.8 us
    ppermute x10, starting transfers between devices, pass_phase(): return lax.ppermute(value, 'phase', perm)  8.84 us
    ppermute x2, waiting for transfers between devices, sum_over_mesh(): part = part + lax.ppermute(part, axis, perm)  7.91 us
    ppermute x2, starting transfers between devices, halo(): slab_in = [lax.ppermute(own[edge[0]], 'slab', edge[2]) for edge in edges]  4.55 us
    ppermute x2, waiting for transfers between devices, halo(): lax.ppermute(off_in[edge[0]], 'slab', edge[2])  3.77 us
    ppermute x1, waiting for transfers between devices, sum_over_mesh(): lax.ppermute(part, axis, perm)  2.89 us
    ppermute x1, waiting for transfers between devices, sum_over_mesh(): part = part + lax.ppermute(other, 'phase', across)  2.88 us
    ppermute x10, waiting for transfers between devices, pass_phase(): return lax.ppermute(value, 'phase', perm)  2.83 us
  transfers between devices with their start and end apart: 23, of which 10 were waited for; matrix products, arithmetic and copies ran while one was open for 1% of the time, Pallas kernels for 18%

profile of v5, /device:TPU:0, one launch (start us, length us, event | category | flops | bytes accessed | tf_op | source)
XLA Modules:
  0.0 71.4 jit_solution(6652562620175984532)
XLA Ops:
  0.7 1.1 %dynamic-slice_bitcast_fusion = (bf16[320,512]{1,0:T(8,128)(2,1)S(1)}, bf16[320,512]{1,0:T(8,128)(2,1)S(1)}) fusion(bf16[1,2,320,512]{3,2,1,0:T(8,128)(2,1)} %param.8, s32[]{:T(128)S(6)} %select_n.28, s32[]{:T(128)S(6)} %select_n.27), kind=kLoop, calls=%fused_computation | loop fusion | bytes 1310728 | tf_op jit(solution)/shard_map/jit(dynamic_index_in_dim)/squeeze | solution.py:487
  1.8 3.0 %collective-permute-start.5 = (bf16[320,512]{1,0:T(8,128)(2,1)S(1)}, bf16[320,512]{1,0:T(8,128)(2,1)S(1)}, u32[]{:S(2)}, u32[]{:S(2)}) collective-permute-start(bf16[320,512]{1,0:T(8,128)(2,1)S(1)} %get-tuple-element.33.refs_3_), channel_id=1, source_target_pairs={{0,1},{1,0},{2,3},{3,2},{4,5},{5,4},{6,7},{7,6},{8,9},{9,8},{10,11... | collective-permute-start | bytes 983048 | tf_op jit(solution)/shard_map/ppermute | solution.py:446
  4.8 4.6 %collective-permute-start.4 = (bf16[320,512]{1,0:T(8,128)(2,1)S(1)}, bf16[320,512]{1,0:T(8,128)(2,1)S(1)}, u32[]{:S(2)}, u32[]{:S(2)}) collective-permute-start(bf16[320,512]{1,0:T(8,128)(2,1)S(1)} %get-tuple-element.33.refs_3_), channel_id=1, source_target_pairs={{0,30},{2,4},{4,2},{6,8},{8,6},{10,12},{12,10},{14,16},{16,14},{18... | collective-permute-start | bytes 983048 | tf_op jit(solution)/shard_map/ppermute | solution.py:428
  9.5 0.0 collective-permute-start
  9.5 0.6 collective-permute-start.3
  10.1 0.1 multiply_negate_fusion
  10.2 0.0 copy-start.3
  10.2 0.1 neg.8
  10.3 3.5 %coil_forward.1 = (f32[256,640]{1,0:T(8,128)S(1)}, bf16[256,640]{1,0:T(8,128)(2,1)}) custom-call(f32[2,2,8,320]{3,2,1,0:T(8,128)S(1)} %bitcast.17, f32[2,16,2,8,320]{4,3,2,1,0:T(8,128)} %refs_1_.6, bf16[640,640]{1,0:T(8,128)(2,1)} %constant.54.clone.refs_2_.refs_3_, bf16[640,640]{1,0:T(8,128)(2,1)} %constant.55.clone.refs_3_.refs_4_), custom_call_target="tpu_custom_call" | custom-call | flops 629145600 | bytes 4000000 | tf_op jit(solution)/shard_map/coil_forward/pallas_call | solution.py:34
  13.8 0.0 collective-permute-done.1.refs_5_
  13.8 0.0 collective-permute-done.refs_4_
  13.8 0.5 collective-permute-start.2
  14.3 0.0 collective-permute-done.5.refs_8_.refs_5_
  14.3 0.1 collective-permute-start.7
  14.4 0.0 collective-permute-done.4.refs_7_
  14.4 1.6 %collective-permute-start.6 = (bf16[320,512]{1,0:T(8,128)(2,1)S(1)}, bf16[320,512]{1,0:T(8,128)(2,1)S(1)}, u32[]{:S(2)}, u32[]{:S(2)}) collective-permute-start(bf16[320,512]{1,0:T(8,128)(2,1)S(1)} %collective-permute-done.4.refs_7_), channel_id=1, source_target_pairs={{0,1},{1,0},{2,3},{3,2},{4,5},{5,4},{6,7},{7,6},{8,9},{9,8},{10,11... | collective-permute-start | bytes 983048 | tf_op jit(solution)/shard_map/ppermute | solution.py:448
  16.0 0.1 pad_add_fusion.refs_0_
  16.1 2.8 %collective-permute-done.3.refs_6_ = bf16[320,512]{1,0:T(8,128)(2,1)} collective-permute-done((bf16[320,512]{1,0:T(8,128)(2,1)S(1)}, bf16[320,512]{1,0:T(8,128)(2,1)}, u32[]{:S(2)}, u32[]{:S(2)}) %collective-permute-start.3) | collective-permute-done | bytes 327712 | tf_op jit(solution)/shard_map/ppermute | solution.py:428
  18.9 3.3 %conv_act.1 = (f32[2,320,512]{2,1,0:T(8,128)S(1)}, bf16[768,1280]{1,0:T(8,128)(2,1)S(1)}) custom-call(s32[2]{0:T(128)S(1)} %pad_add_fusion.refs_0_, bf16[27,64,64]{2,1,0:T(8,128)(2,1)S(1)} %copy-done.3, bf16[320,512]{1,0:T(8,128)(2,1)S(1)} %get-tuple-element.34.refs_2_, bf16[320,512]{1,0:T(8,128)(2,1)S(1)} %get-tuple-element.33.refs_3_, ...), custom_call_target="tpu_custom_call" | custom-call | flops 1761607680 | bytes 5000000 | tf_op jit(solution)/shard_map/conv_act/pallas_call | solution.py:34
  22.2 2.4 %collective-permute-done.2.refs_6_ = bf16[256,640]{1,0:T(8,128)(2,1)S(1)} collective-permute-done((bf16[256,640]{1,0:T(8,128)(2,1)}, bf16[256,640]{1,0:T(8,128)(2,1)S(1)}, u32[]{:S(2)}, u32[]{:S(2)}) %collective-permute-start.2) | collective-permute-done | bytes 327712 | tf_op jit(solution)/shard_map/ppermute | solution.py:491
  24.6 2.1 %coil_back.1.refs_2_ = f32[2,2,8,320]{3,2,1,0:T(8,128)} custom-call(f32[2,2,8,320]{3,2,1,0:T(8,128)S(1)} %bitcast.18, f32[2,16,2,8,320]{4,3,2,1,0:T(8,128)S(1)} %copy-done.2, s32[4,320]{1,0:T(4,128)S(1)} %bitcast.19, bf16[640,640]{1,0:T(8,128)(2,1)S(1)} %copy-done, bf16[640,640]{1,0:T(8,128)(2,1)S(1)} %copy-done.1, ...), custom_call_target="tpu_custom_call" | custom-call | flops 629145600 | bytes 5000000 | tf_op jit(solution)/shard_map/coil_back/pallas_call | solution.py:34
  26.8 3.8 %collective-permute-done.6.refs_6_ = bf16[320,512]{1,0:T(8,128)(2,1)S(1)} collective-permute-done((bf16[320,512]{1,0:T(8,128)(2,1)S(1)}, bf16[320,512]{1,0:T(8,128)(2,1)S(1)}, u32[]{:S(2)}, u32[]{:S(2)}) %collective-permute-start.6) | collective-permute-done | bytes 327712 | tf_op jit(solution)/shard_map/ppermute | solution.py:448
  30.5 1.9 %grad_act.1 = (bf16[320,512]{1,0:T(8,128)(2,1)S(1)}, bf16[320,512]{1,0:T(8,128)(2,1)S(1)}, bf16[384,1280]{1,0:T(8,128)(2,1)S(1)}) custom-call(s32[2]{0:T(128)S(1)} %pad_add_fusion.refs_0_, f32[2,320,512]{2,1,0:T(8,128)S(1)} %get-tuple-element.21.refs_7_.refs_1_, f32[2,2,8,320]{3,2,1,0:T(8,128)} %coil_back.1.refs_2_, ...), custom_call_target="tpu_custom_call" | custom-call | flops 251658240 | bytes 4000000 | tf_op jit(solution)/shard_map/grad_act/pallas_call | solution.py:34
  32.4 3.1 %grad_weight.1 = (f32[448,128]{1,0:T(8,128)S(1)}, f32[448,128]{1,0:T(8,128)S(1)}) custom-call(s32[2]{0:T(128)S(1)} %pad_add_fusion.refs_0_, bf16[768,1280]{1,0:T(8,128)(2,1)S(1)} %get-tuple-element.24.refs_1_, bf16[384,1280]{1,0:T(8,128)(2,1)S(1)} %get-tuple-element.25.refs_2_, bf16[320,512]{1,0:T(8,128)(2,1)S(1)} %get-tuple-element.22.refs_2_.refs_3_, ...), custom_call_target="tpu_custom_call" | custom-call | flops 1761607680 | bytes 5000000 | tf_op jit(solution)/shard_map/grad_weight/pallas_call | solution.py:34
  35.5 0.1 collective-permute-start.14
  35.6 1.4 %collective-permute-done.14.refs_2_ = f32[448,128]{1,0:T(8,128)S(1)} collective-permute-done((f32[448,128]{1,0:T(8,128)S(1)}, f32[448,128]{1,0:T(8,128)S(1)}, u32[]{:S(2)}, u32[]{:S(2)}) %collective-permute-start.14) | collective-permute-done | bytes 229408 | tf_op jit(solution)/shard_map/ppermute | solution.py:390
  37.1 0.1 collective-permute-start.15
  37.1 2.3 %collective-permute-start.11 = (bf16[320,512]{1,0:T(8,128)(2,1)S(1)}, bf16[320,512]{1,0:T(8,128)(2,1)S(1)}, u32[]{:S(2)}, u32[]{:S(2)}) collective-permute-start(bf16[320,512]{1,0:T(8,128)(2,1)S(1)} %get-tuple-element.23.refs_3_.refs_4_), channel_id=1, source_target_pairs={{0,30},{2,4},{4,2},{6,8},{8,6},{10,12},{12,10},{14,16},{16,14},{18... | collective-permute-start | bytes 983048 | tf_op jit(solution)/shard_map/ppermute | solution.py:428
  39.4 2.9 %collective-permute-done.15 = f32[224,128]{1,0:T(8,128)S(1)} collective-permute-done((f32[224,128]{1,0:T(8,128)S(1)}, f32[224,128]{1,0:T(8,128)S(1)}, u32[]{:S(2)}, u32[]{:S(2)}) %collective-permute-start.15) | collective-permute-done | bytes 114720 | tf_op jit(solution)/shard_map/ppermute | solution.py:394
  42.3 0.6 collective-permute-start.16
  42.9 1.5 %collective-permute-start.12 = (bf16[320,512]{1,0:T(8,128)(2,1)S(1)}, bf16[320,512]{1,0:T(8,128)(2,1)}, u32[]{:S(2)}, u32[]{:S(2)}) collective-permute-start(bf16[320,512]{1,0:T(8,128)(2,1)S(1)} %get-tuple-element.23.refs_3_.refs_4_), channel_id=1, source_target_pairs={{0,1},{1,0},{2,3},{3,2},{4,5},{5,4},{6,7},{7,6},{8,9},{9,8},{10,11... | collective-permute-start | bytes 983048 | tf_op jit(solution)/shard_map/ppermute | solution.py:446
  44.4 0.8 %collective-permute-start.10 = (bf16[320,512]{1,0:T(8,128)(2,1)S(1)}, bf16[320,512]{1,0:T(8,128)(2,1)S(1)}, u32[]{:S(2)}, u32[]{:S(2)}) collective-permute-start(bf16[320,512]{1,0:T(8,128)(2,1)S(1)} %get-tuple-element.22.refs_2_.refs_3_), channel_id=1, source_target_pairs={{0,30},{2,4},{4,2},{6,8},{8,6},{10,12},{12,10},{14,16},{16,14},{18... | collective-permute-start | bytes 983048 | tf_op jit(solution)/shard_map/ppermute | solution.py:428
  45.3 0.0 collective-permute-start.8
  45.3 3.2 %collective-permute-done.16 = f32[224,128]{1,0:T(8,128)S(1)} collective-permute-done((f32[224,128]{1,0:T(8,128)S(1)}, f32[224,128]{1,0:T(8,128)S(1)}, u32[]{:S(2)}, u32[]{:S(2)}) %collective-permute-start.16) | collective-permute-done | bytes 114720 | tf_op jit(solution)/shard_map/ppermute | solution.py:397
  48.5 0.0 collective-permute-start.9
  48.5 0.0 collective-permute-done.11.refs_7_
  48.5 1.6 %collective-permute-start.17 = (f32[224,128]{1,0:T(8,128)S(1)}, f32[224,128]{1,0:T(8,128)S(1)}, u32[]{:S(2)}, u32[]{:S(2)}) collective-permute-start(f32[224,128]{1,0:T(8,128)S(1)} %add.36), channel_id=1, source_target_pairs={{0,8},{2,10},{4,12},{6,14},{8,0},{10,2},{12,4},{14,6},{16,24},{18,... | collective-permute-start | bytes 344072 | tf_op jit(solution)/shard_map/ppermute | solution.py:397
  50.1 4.7 %collective-permute-done.17 = f32[224,128]{1,0:T(8,128)S(1)} collective-permute-done((f32[224,128]{1,0:T(8,128)S(1)}, f32[224,128]{1,0:T(8,128)S(1)}, u32[]{:S(2)}, u32[]{:S(2)}) %collective-permute-start.17) | collective-permute-done | bytes 114720 | tf_op jit(solution)/shard_map/ppermute | solution.py:397
  54.8 0.5 collective-permute-start.13
  55.4 1.3 %collective-permute-start.19 = (f32[224,128]{1,0:T(8,128)S(1)}, f32[224,128]{1,0:T(8,128)S(1)}, u32[]{:S(2)}, u32[]{:S(2)}) collective-permute-start(f32[224,128]{1,0:T(8,128)S(1)} %add.37.refs_0_), channel_id=1, source_target_pairs={{0,16},{2,18},{4,20},{6,22},{8,24},{10,26},{12,28},{14,30},{16,0},... | collective-permute-start | bytes 344072 | tf_op jit(solution)/shard_map/ppermute | solution.py:404
  56.7 0.4 collective-permute-start.18
  57.1 3.6 %conv_back.1.refs_2_.refs_1_ = f32[2,320,512]{2,1,0:T(8,128)S(1)} custom-call(s32[2]{0:T(128)S(1)} %pad_add_fusion.refs_0_, bf16[27,64,64]{2,1,0:T(8,128)(2,1)S(1)} %copy-done.3, bf16[320,512]{1,0:T(8,128)(2,1)S(1)} %get-tuple-element.22.refs_2_.refs_3_, bf16[320,512]{1,0:T(8,128)(2,1)S(1)} %get-tuple-element.23.refs_3_.refs_4_, ...), custom_call_target="tpu_custom_call" | custom-call | flops 1761607680 | bytes 5000000 | tf_op jit(solution)/shard_map/conv_back/pallas_call | solution.py:34
  60.6 2.9 %collective-permute-done.19.refs_1_ = f32[224,128]{1,0:T(8,128)S(1)} collective-permute-done((f32[224,128]{1,0:T(8,128)S(1)}, f32[224,128]{1,0:T(8,128)S(1)}, u32[]{:S(2)}, u32[]{:S(2)}) %collective-permute-start.19) | collective-permute-done | bytes 114720 | tf_op jit(solution)/shard_map/ppermute | solution.py:404
  63.5 2.1 %collective-permute-start.20 = (bf16[224,128]{1,0:T(8,128)(2,1)S(1)}, bf16[224,128]{1,0:T(8,128)(2,1)S(1)}, u32[]{:S(2)}, u32[]{:S(2)}) collective-permute-start(bf16[224,128]{1,0:T(8,128)(2,1)S(1)} %finish.1.refs_6_), channel_id=1, source_target_pairs={{0,4},{2,6},{4,0},{6,2},{8,12},{10,14},{12,8},{14,10},{16,20},{18,... | collective-permute-start | bytes 172040 | tf_op jit(solution)/shard_map/ppermute | solution.py:409
  65.6 2.2 %collective-permute-done.20.refs_7_ = bf16[224,128]{1,0:T(8,128)(2,1)S(1)} collective-permute-done((bf16[224,128]{1,0:T(8,128)(2,1)S(1)}, bf16[224,128]{1,0:T(8,128)(2,1)S(1)}, u32[]{:S(2)}, u32[]{:S(2)}) %collective-permute-start.20) | collective-permute-done | bytes 57376 | tf_op jit(solution)/shard_map/ppermute | solution.py:409
  67.8 0.1 pad_add_fusion.1.refs_5_
  67.9 1.2 %collective-permute-done.22.refs_9_ = bf16[224,128]{1,0:T(8,128)(2,1)S(1)} collective-permute-done((bf16[224,128]{1,0:T(8,128)(2,1)S(1)}, bf16[224,128]{1,0:T(8,128)(2,1)S(1)}, u32[]{:S(2)}, u32[]{:S(2)}) %collective-permute-start.22) | collective-permute-done | bytes 57376 | tf_op jit(solution)/shard_map/ppermute | solution.py:410
  69.0 2.3 %finish_both.1 = (bf16[2,320,512]{2,1,0:T(8,128)(2,1)}, f32[27,64,64]{2,1,0:T(8,128)}) custom-call(s32[2]{0:T(128)S(1)} %pad_add_fusion.refs_0_, f32[2,320,512]{2,1,0:T(8,128)S(1)} %conv_back.1.refs_2_.refs_1_, bf16[27,64,64]{2,1,0:T(8,128)(2,1)S(1)} %copy-done.3, bf16[320,512]{1,0:T(8,128)(2,1)S(1)} %collective-permute-done.13.refs_3_, ...), custom_call_target="tpu_custom_call" | custom-call | flops 251658240 | bytes 4000000 | tf_op jit(solution)/shard_map/finish_both/pallas_call | solution.py:34
  (31 shorter events, 0.1 us)
Async XLA Ops:
  0.6 9.5 %copy-start.6 = (bf16[2,64]{1,0:T(2,128)(2,1)S(1)}, bf16[2,64]{1,0:T(2,128)(2,1)}, u32[]{:S(2)}) copy-start(bf16[2,64]{1,0:T(2,128)(2,1)} %param.10) | copy-start | bytes 772
  0.6 9.7 %copy-start.4 = (f32[1,2,2,8,320]{4,3,2,1,0:T(8,128)S(1)}, f32[1,2,2,8,320]{4,3,2,1,0:T(8,128)}, u32[]{:S(2)}) copy-start(f32[1,2,2,8,320]{4,3,2,1,0:T(8,128)} %param.11) | copy-start | bytes 122884
  1.8 12.5 %collective-permute-start.5 = (bf16[320,512]{1,0:T(8,128)(2,1)S(1)}, bf16[320,512]{1,0:T(8,128)(2,1)S(1)}, u32[]{:S(2)}, u32[]{:S(2)}) collective-permute-start(bf16[320,512]{1,0:T(8,128)(2,1)S(1)} %get-tuple-element.33.refs_3_), channel_id=1, source_target_pairs={{0,1},{1,0},{2,3},{3,2},{4,5},{5,4},{6,7},{7,6},{8,9},{9,8},{10,11... | collective-permute-start | bytes 983048 | tf_op jit(solution)/shard_map/ppermute | solution.py:446
  4.8 9.0 %collective-permute-start.1 = (bf16[320,512]{1,0:T(8,128)(2,1)S(1)}, bf16[320,512]{1,0:T(8,128)(2,1)S(1)}, u32[]{:S(2)}, u32[]{:S(2)}) collective-permute-start(bf16[320,512]{1,0:T(8,128)(2,1)S(1)} %get-tuple-element.33.refs_3_), channel_id=1, source_target_pairs={{0,2},{2,0},{4,6},{6,4},{8,10},{10,8},{12,14},{14,12},{16,18},{18,... | collective-permute-start | bytes 983048 | tf_op jit(solution)/shard_map/ppermute | solution.py:428
  4.8 9.6 %collective-permute-start.4 = (bf16[320,512]{1,0:T(8,128)(2,1)S(1)}, bf16[320,512]{1,0:T(8,128)(2,1)S(1)}, u32[]{:S(2)}, u32[]{:S(2)}) collective-permute-start(bf16[320,512]{1,0:T(8,128)(2,1)S(1)} %get-tuple-element.33.refs_3_), channel_id=1, source_target_pairs={{0,30},{2,4},{4,2},{6,8},{8,6},{10,12},{12,10},{14,16},{16,14},{18... | collective-permute-start | bytes 983048 | tf_op jit(solution)/shard_map/ppermute | solution.py:428
  9.5 4.3 %collective-permute-start = (bf16[320,512]{1,0:T(8,128)(2,1)S(1)}, bf16[320,512]{1,0:T(8,128)(2,1)S(1)}, u32[]{:S(2)}, u32[]{:S(2)}) collective-permute-start(bf16[320,512]{1,0:T(8,128)(2,1)S(1)} %get-tuple-element.34.refs_2_), channel_id=1, source_target_pairs={{0,2},{2,0},{4,6},{6,4},{8,10},{10,8},{12,14},{14,12},{16,18},{18,... | collective-permute-start | bytes 983048 | tf_op jit(solution)/shard_map/ppermute | solution.py:428
  9.5 9.4 %collective-permute-start.3 = (bf16[320,512]{1,0:T(8,128)(2,1)S(1)}, bf16[320,512]{1,0:T(8,128)(2,1)}, u32[]{:S(2)}, u32[]{:S(2)}) collective-permute-start(bf16[320,512]{1,0:T(8,128)(2,1)S(1)} %get-tuple-element.34.refs_2_), channel_id=1, source_target_pairs={{0,30},{2,4},{4,2},{6,8},{8,6},{10,12},{12,10},{14,16},{16,14},{18... | collective-permute-start | bytes 983048 | tf_op jit(solution)/shard_map/ppermute | solution.py:428
  10.2 8.7 %copy-start.3 = (bf16[27,64,64]{2,1,0:T(8,128)(2,1)S(1)}, bf16[27,64,64]{2,1,0:T(8,128)(2,1)}, u32[]{:S(2)}) copy-start(bf16[27,64,64]{2,1,0:T(8,128)(2,1)} %refs_2_.2) | copy-start | bytes 663556
  13.8 10.8 %collective-permute-start.2 = (bf16[256,640]{1,0:T(8,128)(2,1)}, bf16[256,640]{1,0:T(8,128)(2,1)S(1)}, u32[]{:S(2)}, u32[]{:S(2)}) collective-permute-start(bf16[256,640]{1,0:T(8,128)(2,1)} %get-tuple-element.20), channel_id=1, source_target_pairs={{0,1},{1,0},{2,3},{3,2},{4,5},{5,4},{6,7},{7,6},{8,9},{9,8},{10,11... | collective-permute-start | bytes 983048 | tf_op jit(solution)/shard_map/ppermute | solution.py:491
  14.3 12.4 %collective-permute-start.7 = (bf16[320,512]{1,0:T(8,128)(2,1)S(1)}, bf16[320,512]{1,0:T(8,128)(2,1)S(1)}, u32[]{:S(2)}, u32[]{:S(2)}) collective-permute-start(bf16[320,512]{1,0:T(8,128)(2,1)S(1)} %collective-permute-done.5.refs_8_.refs_5_), channel_id=1, source_target_pairs={{0,2},{2,0},{4,6},{6,4},{8,10},{10,8},{12,14},{14,12},{16,18},{18,... | collective-permute-start | bytes 983048 | tf_op jit(solution)/shard_map/ppermute | solution.py:428
  14.4 16.1 %collective-permute-start.6 = (bf16[320,512]{1,0:T(8,128)(2,1)S(1)}, bf16[320,512]{1,0:T(8,128)(2,1)S(1)}, u32[]{:S(2)}, u32[]{:S(2)}) collective-permute-start(bf16[320,512]{1,0:T(8,128)(2,1)S(1)} %collective-permute-done.4.refs_7_), channel_id=1, source_target_pairs={{0,1},{1,0},{2,3},{3,2},{4,5},{5,4},{6,7},{7,6},{8,9},{9,8},{10,11... | collective-permute-start | bytes 983048 | tf_op jit(solution)/shard_map/ppermute | solution.py:448
  16.1 8.5 %copy-start = (bf16[640,640]{1,0:T(8,128)(2,1)S(1)}, bf16[640,640]{1,0:T(8,128)(2,1)}, u32[]{:S(2)}) copy-start(bf16[640,640]{1,0:T(8,128)(2,1)} %constant.54.clone.refs_2_.refs_3_) | copy-start | bytes 2457604
  16.1 8.5 %copy-start.1 = (bf16[640,640]{1,0:T(8,128)(2,1)S(1)}, bf16[640,640]{1,0:T(8,128)(2,1)}, u32[]{:S(2)}) copy-start(bf16[640,640]{1,0:T(8,128)(2,1)} %constant.55.clone.refs_3_.refs_4_) | copy-start | bytes 2457604
  16.1 8.5 %copy-start.2 = (f32[2,16,2,8,320]{4,3,2,1,0:T(8,128)S(1)}, f32[2,16,2,8,320]{4,3,2,1,0:T(8,128)}, u32[]{:S(2)}) copy-start(f32[2,16,2,8,320]{4,3,2,1,0:T(8,128)} %refs_1_.6) | copy-start | bytes 1966084
  16.1 8.6 %copy-start.5 = (s32[1,4,320]{2,1,0:T(4,128)S(1)}, s32[1,4,320]{2,1,0:T(4,128)}, u32[]{:S(2)}) copy-start(s32[1,4,320]{2,1,0:T(4,128)} %param.13) | copy-start | bytes 15364
  35.5 1.6 %collective-permute-start.14 = (f32[448,128]{1,0:T(8,128)S(1)}, f32[448,128]{1,0:T(8,128)S(1)}, u32[]{:S(2)}, u32[]{:S(2)}) collective-permute-start(f32[448,128]{1,0:T(8,128)S(1)} %get-tuple-element.27), channel_id=1, source_target_pairs={{0,2},{2,0},{4,6},{6,4},{8,10},{10,8},{12,14},{14,12},{16,18},{18,... | collective-permute-start | bytes 688136 | tf_op jit(solution)/shard_map/ppermute | solution.py:390
  37.1 5.3 %collective-permute-start.15 = (f32[224,128]{1,0:T(8,128)S(1)}, f32[224,128]{1,0:T(8,128)S(1)}, u32[]{:S(2)}, u32[]{:S(2)}) collective-permute-start(f32[224,128]{1,0:T(8,128)S(1)} %get-tuple-element.29), channel_id=1, source_target_pairs={{0,4},{2,6},{4,0},{6,2},{8,12},{10,14},{12,8},{14,10},{16,20},{18,... | collective-permute-start | bytes 344072 | tf_op jit(solution)/shard_map/ppermute | solution.py:394
  37.1 11.4 %collective-permute-start.11 = (bf16[320,512]{1,0:T(8,128)(2,1)S(1)}, bf16[320,512]{1,0:T(8,128)(2,1)S(1)}, u32[]{:S(2)}, u32[]{:S(2)}) collective-permute-start(bf16[320,512]{1,0:T(8,128)(2,1)S(1)} %get-tuple-element.23.refs_3_.refs_4_), channel_id=1, source_target_pairs={{0,30},{2,4},{4,2},{6,8},{8,6},{10,12},{12,10},{14,16},{16,14},{18... | collective-permute-start | bytes 983048 | tf_op jit(solution)/shard_map/ppermute | solution.py:428
  42.3 6.1 %collective-permute-start.16 = (f32[224,128]{1,0:T(8,128)S(1)}, f32[224,128]{1,0:T(8,128)S(1)}, u32[]{:S(2)}, u32[]{:S(2)}) collective-permute-start(f32[224,128]{1,0:T(8,128)S(1)} %add.35), channel_id=1, source_target_pairs={{0,1},{1,0},{2,3},{3,2},{4,5},{5,4},{6,7},{7,6},{8,9},{9,8},{10,11... | collective-permute-start | bytes 344072 | tf_op jit(solution)/shard_map/ppermute | solution.py:397
  42.9 12.5 %collective-permute-start.12 = (bf16[320,512]{1,0:T(8,128)(2,1)S(1)}, bf16[320,512]{1,0:T(8,128)(2,1)}, u32[]{:S(2)}, u32[]{:S(2)}) collective-permute-start(bf16[320,512]{1,0:T(8,128)(2,1)S(1)} %get-tuple-element.23.refs_3_.refs_4_), channel_id=1, source_target_pairs={{0,1},{1,0},{2,3},{3,2},{4,5},{5,4},{6,7},{7,6},{8,9},{9,8},{10,11... | collective-permute-start | bytes 983048 | tf_op jit(solution)/shard_map/ppermute | solution.py:446
  44.4 12.3 %collective-permute-start.10 = (bf16[320,512]{1,0:T(8,128)(2,1)S(1)}, bf16[320,512]{1,0:T(8,128)(2,1)S(1)}, u32[]{:S(2)}, u32[]{:S(2)}) collective-permute-start(bf16[320,512]{1,0:T(8,128)(2,1)S(1)} %get-tuple-element.22.refs_2_.refs_3_), channel_id=1, source_target_pairs={{0,30},{2,4},{4,2},{6,8},{8,6},{10,12},{12,10},{14,16},{16,14},{18... | collective-permute-start | bytes 983048 | tf_op jit(solution)/shard_map/ppermute | solution.py:428
  45.3 11.8 %collective-permute-start.8 = (bf16[320,512]{1,0:T(8,128)(2,1)S(1)}, bf16[320,512]{1,0:T(8,128)(2,1)S(1)}, u32[]{:S(2)}, u32[]{:S(2)}) collective-permute-start(bf16[320,512]{1,0:T(8,128)(2,1)S(1)} %get-tuple-element.22.refs_2_.refs_3_), channel_id=1, source_target_pairs={{0,2},{2,0},{4,6},{6,4},{8,10},{10,8},{12,14},{14,12},{16,18},{18,... | collective-permute-start | bytes 983048 | tf_op jit(solution)/shard_map/ppermute | solution.py:428
  48.5 8.6 %collective-permute-start.9 = (bf16[320,512]{1,0:T(8,128)(2,1)S(1)}, bf16[320,512]{1,0:T(8,128)(2,1)S(1)}, u32[]{:S(2)}, u32[]{:S(2)}) collective-permute-start(bf16[320,512]{1,0:T(8,128)(2,1)S(1)} %get-tuple-element.23.refs_3_.refs_4_), channel_id=1, source_target_pairs={{0,2},{2,0},{4,6},{6,4},{8,10},{10,8},{12,14},{14,12},{16,18},{18,... | collective-permute-start | bytes 983048 | tf_op jit(solution)/shard_map/ppermute | solution.py:428
  48.5 6.3 %collective-permute-start.17 = (f32[224,128]{1,0:T(8,128)S(1)}, f32[224,128]{1,0:T(8,128)S(1)}, u32[]{:S(2)}, u32[]{:S(2)}) collective-permute-start(f32[224,128]{1,0:T(8,128)S(1)} %add.36), channel_id=1, source_target_pairs={{0,8},{2,10},{4,12},{6,14},{8,0},{10,2},{12,4},{14,6},{16,24},{18,... | collective-permute-start | bytes 344072 | tf_op jit(solution)/shard_map/ppermute | solution.py:397
  54.8 13.0 %collective-permute-start.13 = (bf16[320,512]{1,0:T(8,128)(2,1)S(1)}, bf16[320,512]{1,0:T(8,128)(2,1)S(1)}, u32[]{:S(2)}, u32[]{:S(2)}) collective-permute-start(bf16[320,512]{1,0:T(8,128)(2,1)S(1)} %collective-permute-done.11.refs_7_), channel_id=1, source_target_pairs={{0,1},{1,0},{2,3},{3,2},{4,5},{5,4},{6,7},{7,6},{8,9},{9,8},{10,11... | collective-permute-start | bytes 983048 | tf_op jit(solution)/shard_map/ppermute | solution.py:448
  55.4 8.1 %collective-permute-start.19 = (f32[224,128]{1,0:T(8,128)S(1)}, f32[224,128]{1,0:T(8,128)S(1)}, u32[]{:S(2)}, u32[]{:S(2)}) collective-permute-start(f32[224,128]{1,0:T(8,128)S(1)} %add.37.refs_0_), channel_id=1, source_target_pairs={{0,16},{2,18},{4,20},{6,22},{8,24},{10,26},{12,28},{14,30},{16,0},... | collective-permute-start | bytes 344072 | tf_op jit(solution)/shard_map/ppermute | solution.py:404
  56.7 12.3 %collective-permute-start.18 = (bf16[320,512]{1,0:T(8,128)(2,1)}, bf16[320,512]{1,0:T(8,128)(2,1)S(1)}, u32[]{:S(2)}, u32[]{:S(2)}) collective-permute-start(bf16[320,512]{1,0:T(8,128)(2,1)} %collective-permute-done.12.refs_8_), channel_id=1, source_target_pairs={{0,2},{2,0},{4,6},{6,4},{8,10},{10,8},{12,14},{14,12},{16,18},{18,... | collective-permute-start | bytes 983048 | tf_op jit(solution)/shard_map/ppermute | solution.py:428
  63.5 4.2 %collective-permute-start.20 = (bf16[224,128]{1,0:T(8,128)(2,1)S(1)}, bf16[224,128]{1,0:T(8,128)(2,1)S(1)}, u32[]{:S(2)}, u32[]{:S(2)}) collective-permute-start(bf16[224,128]{1,0:T(8,128)(2,1)S(1)} %finish.1.refs_6_), channel_id=1, source_target_pairs={{0,4},{2,6},{4,0},{6,2},{8,12},{10,14},{12,8},{14,10},{16,20},{18,... | collective-permute-start | bytes 172040 | tf_op jit(solution)/shard_map/ppermute | solution.py:409
  65.6 2.3 %collective-permute-start.21 = (bf16[224,128]{1,0:T(8,128)(2,1)S(1)}, bf16[224,128]{1,0:T(8,128)(2,1)S(1)}, u32[]{:S(2)}, u32[]{:S(2)}) collective-permute-start(bf16[224,128]{1,0:T(8,128)(2,1)S(1)} %finish.1.refs_6_), channel_id=1, source_target_pairs={{0,2},{2,0},{4,6},{6,4},{8,10},{10,8},{12,14},{14,12},{16,18},{18,... | collective-permute-start | bytes 172040 | tf_op jit(solution)/shard_map/ppermute | solution.py:410
  67.8 1.2 %collective-permute-start.22 = (bf16[224,128]{1,0:T(8,128)(2,1)S(1)}, bf16[224,128]{1,0:T(8,128)(2,1)S(1)}, u32[]{:S(2)}, u32[]{:S(2)}) collective-permute-start(bf16[224,128]{1,0:T(8,128)(2,1)S(1)} %collective-permute-done.20.refs_7_), channel_id=1, source_target_pairs={{0,2},{2,0},{4,6},{6,4},{8,10},{10,8},{12,14},{14,12},{16,18},{18,... | collective-permute-start | bytes 172040 | tf_op jit(solution)/shard_map/ppermute | solution.py:410
